TPU v7x, 32 devices: a whole 2x2x4 slice. The times are simulated.
32 devices in a mesh: dp: 8 (over y, x, core), tensor: 4 (over z).
Axes of the slice: x: 2, y: 2, z: 4, core: 2. Of those that a mesh axis runs over, the one named last changes fastest.
Arguments:
- tokens: bfloat16 [8192, 2048], P('dp', 'tensor'), may hold values from -6 to 6
- cotangent: bfloat16 [8192, 2048], P('dp', 'tensor'), may hold values from -6 to 6
- norm_gain: bfloat16 [2048], replicated, may hold values from 0.099609375 to 1.8984375
- gate_proj: bfloat16 [2048, 4096], P(None, 'tensor'), may hold values from -0.125 to 0.125
- value_proj: bfloat16 [2048, 4096], P(None, 'tensor'), may hold values from -0.125 to 0.125
- state_proj: bfloat16 [2048, 256], replicated, may hold values from -0.125 to 0.125
- step_proj: bfloat16 [2048, 64], P(None, 'tensor'), may hold values from -0.125 to 0.125
- conv_value: bfloat16 [4, 4096], P(None, 'tensor'), may hold values from -3 to 3
- conv_value_bias: bfloat16 [4096], P('tensor'), may hold values from -3 to 3
- conv_state: bfloat16 [4, 256], replicated, may hold values from -3 to 3
- conv_state_bias: bfloat16 [256], replicated, may hold values from -3 to 3
- step_bias: float32 [64], P('tensor'), may hold values from -4 to -1
- decay_log: float32 [64], P('tensor'), may hold values from -7 to 1
- skip_gain: float32 [64], P('tensor'), may hold values from 0.5 to 2
- gate_gain: bfloat16 [4096], P('tensor'), may hold values from 0.099609375 to 1.8984375
- out_proj: bfloat16 [2048, 4096], P(None, 'tensor'), may hold values from -0.09375 to 0.09375
- token_order: int32 [8192], replicated, may hold values from 0 to 8191, as said below
- lengths: int32 [8, 3], P('dp'), may hold values from 1 to 768, 1024 in all within a row
Outputs:
- layer_output: bfloat16 [8192, 2048], P('dp', 'tensor')
- tokens_grad: bfloat16 [8192, 2048], P('dp', 'tensor')
- norm_gain_grad: float32 [2048], P('tensor')
- gate_proj_grad: float32 [2048, 4096], P('dp', 'tensor')
- value_proj_grad: float32 [2048, 4096], P('dp', 'tensor')
- state_proj_grad: float32 [2048, 256], P(('dp', 'tensor'))
- step_proj_grad: float32 [2048, 64], P('dp', 'tensor')
- conv_value_grad: float32 [4, 4096], P(None, 'tensor')
- conv_value_bias_grad: float32 [4096], P('tensor')
- conv_state_grad: float32 [4, 256], replicated
- conv_state_bias_grad: float32 [256], replicated
- step_bias_grad: float32 [64], P('tensor')
- decay_log_grad: float32 [64], P('tensor')
- skip_gain_grad: float32 [64], P('tensor')
- gate_gain_grad: float32 [4096], P('tensor')
- out_proj_grad: float32 [2048, 4096], P('dp', 'tensor')
Inputs may be any that keep to these rules, and one draw needn't show every extreme that they name: `token_order`: A permutation. Each group's 1024 packed positions hold runs of 256 consecutive given-order tokens, each run from another group of given-order rows, so that a group receives exactly 256 tokens from each of 4 groups and none from the others. Each group's 3 lengths sum to 1024; its longest is exactly 768.
All inputs are finite; a program needn't handle non-finite values.
Results may differ from a plain program's by a relative error of at most 0.0092.
Values may be sent and summed in bfloat16 or wider, within the bound.
A program may use at most 192 MiB of HBM per device.

v0:
```python
import jax
import jax.numpy as jnp
from jax import lax
from jax.sharding import PartitionSpec as P

SPAN = 256


epsilon = 1e-05
highest = lax.Precision.HIGHEST


def contract_rows(left, right):
    return lax.dot_general(
        left, right, (((0,), (0,)), ((), ())), preferred_element_type=jnp.float32
    )


def contract_cols(left, right):
    return lax.dot_general(
        left, right, (((1,), (1,)), ((), ())), preferred_element_type=jnp.float32
    )


def segment_ids(length_row, row_total):
    length_ends = jnp.cumsum(length_row)
    position = jnp.arange(row_total, dtype=jnp.int32)
    return jnp.sum((position[:, None] >= length_ends[None, :]).astype(jnp.int32), axis=1)


def causal_conv(values, tap_weights, seg_ids):
    row_count = values.shape[0]
    summed = jnp.zeros_like(values)
    for tap_index in range(tap_weights.shape[0]):
        offset = tap_weights.shape[0] - 1 - tap_index
        shifted = jnp.pad(values, ((offset, 0), (0, 0)))[:row_count]
        earlier = jnp.pad(seg_ids, (offset, 0), constant_values=-1)[:row_count]
        keep_mask = (earlier == seg_ids).astype(values.dtype)
        summed = summed + tap_weights[tap_index][None, :] * shifted * keep_mask[:, None]
    return summed


def span_step(carry_state, pieces):
    value_block, step_block, decay_block, entry_block, exit_block, segment_block, segment_before = (
        pieces
    )
    cumulative = jnp.cumsum(decay_block, axis=0)
    cum_heads = cumulative.T
    position = jnp.arange(segment_block.shape[0], dtype=jnp.int32)
    allowed = (segment_block[:, None] == segment_block[None, :]) & (
        position[:, None] >= position[None, :]
    )
    spread = cum_heads[:, :, None] - cum_heads[:, None, :]
    decay_mask = jnp.exp(jnp.where(allowed[None], spread, -1e30))
    scores = jnp.dot(exit_block, entry_block.T, precision=highest)
    weighted = value_block * step_block[:, :, None]
    inside = jnp.einsum("ij,hij,jhp->ihp", scores, decay_mask, weighted, precision=highest)
    segment_last = segment_block[-1]
    to_end = (
        jnp.exp(cumulative[-1][None, :] - cumulative)
        * (segment_block == segment_last).astype(cumulative.dtype)[:, None]
    )
    local_state = jnp.einsum("jn,jh,jhp->hnp", entry_block, to_end, weighted, precision=highest)
    from_start = (
        jnp.exp(cumulative) * (segment_block == segment_before).astype(cumulative.dtype)[:, None]
    )
    carried = (
        jnp.einsum("in,hnp->ihp", exit_block, carry_state, precision=highest)
        * from_start[:, :, None]
    )
    carry_factor = jnp.exp(cumulative[-1]) * (segment_last == segment_before).astype(
        cumulative.dtype
    )
    new_state = carry_factor[:, None, None] * carry_state + local_state
    return (new_state, inside + carried)


def scan_ssd(per_head, step_sizes, log_decay, entry_mat, exit_mat, seg_ids):
    blocks = per_head.shape[0] // SPAN
    before_all = jnp.concatenate([jnp.full((1,), -1, dtype=jnp.int32), seg_ids[:-1]])
    before_first = before_all.reshape(blocks, SPAN)[:, 0]

    def split_blocks(values):
        return values.reshape((blocks, SPAN) + values.shape[1:])

    pieces = (
        split_blocks(per_head),
        split_blocks(step_sizes),
        split_blocks(log_decay),
        split_blocks(entry_mat),
        split_blocks(exit_mat),
        split_blocks(seg_ids),
        before_first,
    )
    initial = jnp.zeros((per_head.shape[1], entry_mat.shape[1], per_head.shape[2]), jnp.float32)
    final_state, outputs = lax.scan(jax.checkpoint(span_step), initial, pieces)
    return outputs.reshape(per_head.shape)


def mixer(
    gate_raw,
    value_raw,
    state_raw,
    step_raw,
    conv_value,
    conv_value_bias,
    conv_state,
    conv_state_bias,
    step_bias,
    decay_log,
    skip_gain,
    seg_ids,
):
    value_conv = jax.nn.silu(causal_conv(value_raw, conv_value, seg_ids) + conv_value_bias)
    state_conv = jax.nn.silu(causal_conv(state_raw, conv_state, seg_ids) + conv_state_bias)
    half_state = state_conv.shape[1] // 2
    step_sizes = jax.nn.softplus(step_raw + step_bias)
    log_decay = -step_sizes * jnp.exp(decay_log)
    head_count = step_sizes.shape[1]
    per_head = value_conv.reshape(value_conv.shape[0], head_count, -1)
    ssd_out = scan_ssd(
        per_head,
        step_sizes,
        log_decay,
        state_conv[:, :half_state],
        state_conv[:, half_state:],
        seg_ids,
    )
    ssd_out = ssd_out + skip_gain[None, :, None] * per_head
    return ssd_out.reshape(value_conv.shape) * jax.nn.silu(gate_raw)


def per_device(
    tokens,
    cotangent,
    norm_gain,
    gate_proj,
    value_proj,
    state_proj,
    step_proj,
    conv_value,
    conv_value_bias,
    conv_state,
    conv_state_bias,
    step_bias,
    decay_log,
    skip_gain,
    gate_gain,
    out_proj,
    token_order,
    lengths,
):
    group_count = lax.axis_size("dp")
    my_group = lax.axis_index("dp")
    tensor_count = lax.axis_size("tensor")
    tensor_slot = lax.axis_index("tensor")
    row_count = tokens.shape[0]
    local_width = tokens.shape[1]
    model_width = local_width * tensor_count
    slot_cap = 2 * row_count // group_count
    by_target = token_order.reshape(group_count, row_count)
    source_ids = by_target // row_count
    from_here = source_ids == my_group
    send_slot = jnp.cumsum(from_here.astype(jnp.int32), axis=1) - 1
    local_rows = by_target - my_group * row_count
    flat_slot = jnp.where(
        from_here,
        jnp.arange(group_count, dtype=jnp.int32)[:, None] * slot_cap + send_slot,
        group_count * slot_cap,
    )
    send_rows = (
        jnp.zeros((group_count * slot_cap,), jnp.int32)
        .at[flat_slot.reshape(-1)]
        .set(local_rows.reshape(-1), mode="drop")
    )
    return_slot = (
        jnp.zeros((row_count,), jnp.int32)
        .at[jnp.where(from_here, local_rows, row_count).reshape(-1)]
        .set(flat_slot.reshape(-1), mode="drop")
    )
    target_list = lax.dynamic_index_in_dim(by_target, my_group, 0, keepdims=False)
    list_sources = target_list // row_count
    source_hits = (
        list_sources[:, None] == jnp.arange(group_count, dtype=jnp.int32)[None, :]
    ).astype(jnp.int32)
    arrive_slot = jnp.sum((jnp.cumsum(source_hits, axis=0) - 1) * source_hits, axis=1)
    arrive_pos = list_sources * slot_cap + arrive_slot
    send_shape = (group_count, slot_cap, local_width)
    arrived_tokens, arrived_cotangent = (
        lax.all_to_all(
            tokens[send_rows].reshape(send_shape), "dp", split_axis=0, concat_axis=0, tiled=True
        ),
        lax.all_to_all(
            cotangent[send_rows].reshape(send_shape), "dp", split_axis=0, concat_axis=0, tiled=True
        ),
    )
    packed_tokens = arrived_tokens.reshape(-1, local_width)[arrive_pos]
    packed_cotangent = arrived_cotangent.reshape(-1, local_width)[arrive_pos]
    full_tokens, full_cotangent = (
        lax.all_gather(packed_tokens, "tensor", axis=1, tiled=True),
        lax.all_gather(packed_cotangent, "tensor", axis=1, tiled=True),
    )
    inputs_wide = full_tokens.astype(jnp.float32)
    inv_rms = lax.rsqrt(jnp.mean(inputs_wide * inputs_wide, axis=-1, keepdims=True) + epsilon)
    gain_full = norm_gain.astype(jnp.float32)
    normed = (inputs_wide * inv_rms * gain_full).astype(jnp.bfloat16)
    gate_raw = jnp.dot(normed, gate_proj, preferred_element_type=jnp.float32)
    value_raw = jnp.dot(normed, value_proj, preferred_element_type=jnp.float32)
    state_raw = jnp.dot(normed, state_proj, preferred_element_type=jnp.float32)
    step_raw = jnp.dot(normed, step_proj, preferred_element_type=jnp.float32)
    seg_ids = segment_ids(lengths[0], row_count)

    def local_mixer(
        gate_in,
        value_in,
        state_in,
        step_in,
        taps_value,
        bias_value,
        taps_state,
        bias_state,
        bias_step,
        rate_log,
        skip_heads,
    ):
        return mixer(
            gate_in,
            value_in,
            state_in,
            step_in,
            taps_value,
            bias_value,
            taps_state,
            bias_state,
            bias_step,
            rate_log,
            skip_heads,
            seg_ids,
        )

    gated, mixer_back = jax.vjp(
        local_mixer,
        gate_raw,
        value_raw,
        state_raw,
        step_raw,
        conv_value.astype(jnp.float32),
        conv_value_bias.astype(jnp.float32),
        conv_state.astype(jnp.float32),
        conv_state_bias.astype(jnp.float32),
        step_bias,
        decay_log,
        skip_gain,
    )
    squares = lax.psum(jnp.sum(gated * gated, axis=1), "tensor")
    inner_total = gated.shape[1] * tensor_count
    inner_rms = lax.rsqrt(squares / inner_total + epsilon)
    normalized = gated * inner_rms[:, None]
    gate_gain_wide = gate_gain.astype(jnp.float32)
    scaled = (normalized * gate_gain_wide).astype(jnp.bfloat16)
    out_partial = contract_cols(scaled, out_proj)
    out_share = lax.psum_scatter(out_partial, "tensor", scatter_dimension=1, tiled=True)
    output_packed = (packed_tokens.astype(jnp.float32) + out_share).astype(jnp.bfloat16)
    out_grad = contract_rows(full_cotangent, scaled)
    d_scaled = jnp.dot(full_cotangent, out_proj, preferred_element_type=jnp.float32)
    d_norm_in = d_scaled * gate_gain_wide
    gate_gain_back = jnp.sum(d_scaled * normalized, axis=0)
    inner_dot = lax.psum(jnp.sum(d_norm_in * gated, axis=1), "tensor")
    d_gated = (
        inner_rms[:, None] * d_norm_in - gated * (inner_rms**3 * inner_dot / inner_total)[:, None]
    )
    (
        gate_back,
        value_back,
        state_back,
        step_back,
        conv_value_back,
        conv_value_bias_back,
        conv_state_back,
        conv_state_bias_back,
        step_bias_back,
        decay_log_back,
        skip_gain_back,
    ) = mixer_back(d_gated)
    state_back_sum, conv_state_sum, conv_state_bias_sum = lax.psum(
        (state_back, conv_state_back, conv_state_bias_back), "tensor"
    )
    gate_low = gate_back.astype(jnp.bfloat16)
    value_low = value_back.astype(jnp.bfloat16)
    state_low = state_back_sum.astype(jnp.bfloat16)
    step_low = step_back.astype(jnp.bfloat16)
    gate_grad = contract_rows(normed, gate_low)
    value_grad = contract_rows(normed, value_low)
    step_grad = contract_rows(normed, step_low)
    quarter = row_count // tensor_count
    normed_part = lax.dynamic_slice_in_dim(normed, tensor_slot * quarter, quarter, 0)
    state_part = lax.dynamic_slice_in_dim(state_low, tensor_slot * quarter, quarter, 0)
    state_grad_share = lax.psum_scatter(
        contract_rows(normed_part, state_part), ("dp", "tensor"), scatter_dimension=0, tiled=True
    )
    back_partial = (
        contract_cols(gate_low, gate_proj)
        + contract_cols(value_low, value_proj)
        + contract_cols(step_low, step_proj)
    )
    back_share = lax.psum_scatter(back_partial, "tensor", scatter_dimension=1, tiled=True)
    proj_slice = lax.dynamic_slice_in_dim(state_proj, tensor_slot * local_width, local_width, 0)
    back_share = back_share + contract_cols(state_low, proj_slice)
    unit_share = packed_tokens.astype(jnp.float32) * inv_rms
    gain_share = lax.dynamic_slice_in_dim(gain_full, tensor_slot * local_width, local_width, 0)
    norm_gain_back = jnp.sum(back_share * unit_share, axis=0)
    d_unit = back_share * gain_share
    row_dot = lax.psum(jnp.sum(d_unit * unit_share, axis=1), "tensor")
    input_back = packed_cotangent.astype(jnp.float32) + inv_rms * (
        d_unit - unit_share * (row_dot / model_width)[:, None]
    )
    input_low = input_back.astype(jnp.bfloat16)
    back_rows = (
        jnp.zeros((group_count * slot_cap,), jnp.int32)
        .at[arrive_pos]
        .set(jnp.arange(row_count, dtype=jnp.int32))
    )
    returned_output, returned_grad = (
        lax.all_to_all(
            output_packed[back_rows].reshape(send_shape),
            "dp",
            split_axis=0,
            concat_axis=0,
            tiled=True,
        ),
        lax.all_to_all(
            input_low[back_rows].reshape(send_shape), "dp", split_axis=0, concat_axis=0, tiled=True
        ),
    )
    layer_output = returned_output.reshape(-1, local_width)[return_slot]
    tokens_grad = returned_grad.reshape(-1, local_width)[return_slot]
    gate_share, value_share, step_share, out_grad_share = (
        lax.psum_scatter(gate_grad, "dp", scatter_dimension=0, tiled=True),
        lax.psum_scatter(value_grad, "dp", scatter_dimension=0, tiled=True),
        lax.psum_scatter(step_grad, "dp", scatter_dimension=0, tiled=True),
        lax.psum_scatter(out_grad, "dp", scatter_dimension=0, tiled=True),
    )
    small_sums = lax.psum(
        (
            norm_gain_back,
            conv_value_back,
            conv_value_bias_back,
            conv_state_sum,
            conv_state_bias_sum,
            step_bias_back,
            decay_log_back,
            skip_gain_back,
            gate_gain_back,
        ),
        "dp",
    )
    return (
        layer_output,
        tokens_grad,
        small_sums[0],
        gate_share,
        value_share,
        state_grad_share,
        step_share,
        small_sums[1],
        small_sums[2],
        small_sums[3],
        small_sums[4],
        small_sums[5],
        small_sums[6],
        small_sums[7],
        small_sums[8],
        out_grad_share,
    )


def solution(mesh):
    return jax.shard_map(
        per_device,
        mesh=mesh,
        in_specs=(
            P("dp", "tensor"),
            P("dp", "tensor"),
            P(),
            P(None, "tensor"),
            P(None, "tensor"),
            P(),
            P(None, "tensor"),
            P(None, "tensor"),
            P("tensor"),
            P(),
            P(),
            P("tensor"),
            P("tensor"),
            P("tensor"),
            P("tensor"),
            P(None, "tensor"),
            P(),
            P("dp", None),
        ),
        out_specs=(
            P("dp", "tensor"),
            P("dp", "tensor"),
            P("tensor"),
            P("dp", "tensor"),
            P("dp", "tensor"),
            P(("dp", "tensor"), None),
            P("dp", "tensor"),
            P(None, "tensor"),
            P("tensor"),
            P(),
            P(),
            P("tensor"),
            P("tensor"),
            P("tensor"),
            P("tensor"),
            P("dp", "tensor"),
        ),
        check_vma=False,
    )
```

profile of v0, /device:TPU:0, one launch (start us, length us, event | category | flops | bytes accessed | tf_op | source)
XLA Modules:
  0.0 1378.5 jit_solution(4370650010212430205)
XLA Ops:
  12.3 30.4 %scatter_custom_fusion = s32[2048]{0:T(1024)S(1)} fusion(s32[8192]{0:T(1024)S(1)} %get-tuple-element.798, s32[8192]{0:T(1024)S(1)} %get-tuple-element.753, s32[]{:T(128)} %constant.202.clone.1), kind=kCustom, calls=%fused_computation.323 | custom fusion | bytes 8196 | tf_op jit(solution)/shard_map/scatter | solution.py:174
  42.8 9.2 gather_fusion
  60.3 23.6 %all-to-all-done = bf16[8,256,512]{2,1,0:T(8,128)(2,1)S(1)} async-done(((bf16[8,256,512]{2,1,0:T(8,128)(2,1)}), bf16[8,256,512]{2,1,0:T(8,128)(2,1)S(1)}, u32[]{:S(2)}, u32[]{:S(2)}) %all-to-all-start) | async-done | bytes 2097184 | tf_op jit(solution)/shard_map/all_to_all | solution.py:190
  89.0 9.2 gather_fusion.4
  104.1 24.5 %all-to-all-done.2 = bf16[8,256,512]{2,1,0:T(8,128)(2,1)S(1)} async-done(((bf16[8,256,512]{2,1,0:T(8,128)(2,1)}), bf16[8,256,512]{2,1,0:T(8,128)(2,1)S(1)}, u32[]{:S(2)}, u32[]{:S(2)}) %all-to-all-start.2) | async-done | bytes 2097184 | tf_op jit(solution)/shard_map/all_to_all | solution.py:193
  133.9 35.4 %all-gather.5.cloned.1.call-done = bf16[1024,2048]{1,0:T(8,128)(2,1)} async-done(((bf16[1024,512]{1,0:T(8,128)(2,1)}), bf16[1024,2048]{1,0:T(8,128)(2,1)}) %all-gather.5.cloned.1.call-update) | async-done | bytes 4194320 | tf_op jit(solution)/shard_map/all_gather | solution.py:200
  188.9 7.3 reshape.832
  196.2 7.7 copy.110
  211.1 85.2 %while.41 = (s32[]{:T(128)}, f32[16,128,64]{1,2,0:T(8,128)S(1)}, f32[4,256,16,64]{1,3,2,0:T(8,128)}, f32[4,16,128,64]{2,3,1,0:T(8,128)}, f32[4,256,16]{1,2,0:T(8...) while((s32[]{:T(128)}, f32[16,128,64]{1,2,0:T(8,128)S(1)}, ...), condition=%wide.region_12.13_spmd.clone, body=%wide.region_9.12_spmd.clone.sunk | while | flops 1716864000 | bytes 9876153 | solution.py:96
  225.5 7.2 fusion.275
  246.7 7.3 fusion.275
  267.9 7.2 fusion.275
  289.1 7.2 fusion.275
  296.3 8.1 copy.132
  304.4 7.8 reshape.829
  312.2 14.3 %multiply_reduce_fusion.11 = (f32[1024]{0:T(1024)S(1)}, f32[1024,1024]{1,0:T(8,128)}, f32[1024,1024]{1,0:T(8,128)}) fusion(f32[1024,1024]{1,0:T(8,128)} %reshape.829, f32[1024,1024]{1,0:T(8,128)} %get-tuple-element.759, f32[1024]{0:T(1024)S(1)} %mul.878, bf16[1024,2048]{1,0:T(8,128)(2,1)} %copy-done.3, bf16[2048,1024]{1,0:T(8,128)(2,1)} %param.25), kind=kOutput, calls=%fused_computation.182 | convolution fusion | flops 4308597760 | bytes 25174016 | tf_op jit(solution)/shard_map/dot_general | solution.py:207
  326.5 8.5 psum.105
  335.1 11.9 multiply_reduce_fusion.4
  347.0 10.2 psum.106
  357.2 11.6 multiply_reduce_fusion.5
  368.8 7.2 reshape.830
  376.0 7.7 copy.118
  389.2 202.7 %while.42 = (s32[]{:T(128)}, f32[16,128,64]{1,2,0:T(8,128)S(1)}, f32[4,256,16,64]{1,3,2,0:T(8,128)}, f32[4,256,16]{1,0,2:T(4,128)}, f32[4,256,16]{1,0,2:T(4,128)...) while((s32[]{:T(128)}, f32[16,128,64]{1,2,0:T(8,128)S(1)}, ...), condition=%wide.region_31.32_spmd.clone, body=%wide.region_20.31_spmd.clone.sunk | while | flops 3946451968 | bytes 48006336 | solution.py:96
  418.3 7.7 fusion.295
  468.9 7.7 fusion.295
  519.4 7.7 fusion.295
  569.9 7.7 fusion.295
  593.6 8.1 copy.135
  601.7 7.6 reshape.831
  609.4 13.3 multiply_reduce_fusion.9
  641.3 11.2 fusion.170
  659.9 73.6 %all-reduce.30 = bf16[1024,256]{1,0:T(8,128)(2,1)S(1)} all-reduce(f32[1024,256]{1,0:T(8,128)S(1)} %fusion.120), channel_id=1, replica_groups=mesh['dp'=8,'tensor'=4] {'tensor'}, use_global_device_ids=true, to_apply=%region_33.34 | all-reduce | flops 262144 | bytes 1572864 | tf_op jit(solution)/shard_map/psum | solution.py:285
  736.9 11.7 fusion.169
  750.4 9.0 fusion.186
  761.0 9.1 fusion.187
  775.3 41.7 %reduce-scatter.10.cloned.1.call-done = f32[1024,512]{1,0:T(8,128)} async-done(((f32[1024,2048]{1,0:T(8,128)}), f32[1024,512]{1,0:T(8,128)}) %reduce-scatter.10.cloned.1.call-update) | async-done | bytes 2097168 | tf_op jit(solution)/shard_map/reduce_scatter | solution.py:306
  820.7 12.2 all-reduce.28
  833.0 131.5 %reduce-scatter.8.cloned.1.call-done = f32[1024,512]{1,0:T(8,128)} async-done(((f32[1024,2048]{1,0:T(8,128)}), f32[1024,512]{1,0:T(8,128)}) %reduce-scatter.8.cloned.1.call-update) | async-done | bytes 2097168 | tf_op jit(solution)/shard_map/reduce_scatter | solution.py:262
  967.8 9.2 gather_fusion.6
  980.6 9.2 gather_fusion.2
  989.7 18.0 %all-to-all-done.3 = bf16[8,256,512]{2,1,0:T(8,128)(2,1)S(1)} async-done(((bf16[8,256,512]{2,1,0:T(8,128)(2,1)}), bf16[8,256,512]{2,1,0:T(8,128)(2,1)S(1)}, u32[]{:S(2)}, u32[]{:S(2)}) %all-to-all-start.3) | async-done | bytes 2097184 | tf_op jit(solution)/shard_map/all_to_all | solution.py:331
  1012.1 30.6 %scatter_custom_fusion.2 = s32[1024]{0:T(1024)S(1)} fusion(s32[8192]{0:T(1024)} %get-tuple-element.752, s32[8192]{0:T(1024)} %get-tuple-element.799, s32[]{:T(128)} %constant.202.clone.1), kind=kCustom, calls=%fused_computation.333 | custom fusion | bytes 4608 | tf_op jit(solution)/shard_map/scatter | solution.py:179
  1042.9 26.6 %all-reduce.27 = (f32[512]{0:T(512)}, f32[4,1024]{1,0:T(4,128)}, f32[1024]{0:T(1024)}, f32[4,256]{1,0:T(4,128)}, f32[256]{0:T(256)}, /*index=5*/f32[16]{0:T(128)}, f32[16]{0:T(128)}, f32[16]{0:T(128)}, f32[1024]{0:T(1024)}) all-reduce(f32[512]{0:T(512)S(1)} %get-tuple-element.671, ...), channel_id=1, replica_groups=mesh['dp'=8,'tensor'=4] {'dp'}, use_global_device_ids=true, to_apply=%region_37.38 | all-reduce | flops 7984 | bytes 63872 | tf_op jit(solution)/shard_map/psum | solution.py:343
  1074.7 7.1 gather_fusion.3
  1081.7 65.8 %reduce-scatter.16.cloned.1.call-done = f32[64,256]{1,0:T(8,128)} async-done(((f32[2048,256]{1,0:T(8,128)}), f32[64,256]{1,0:T(8,128)}) %reduce-scatter.16.cloned.1.call-update) | async-done | bytes 65552 | tf_op jit(solution)/shard_map/reduce_scatter | solution.py:298
  1147.5 72.9 %reduce-scatter.20.cloned.1.call-done = f32[256,1024]{1,0:T(8,128)} async-done(((f32[2048,1024]{1,0:T(8,128)}), f32[256,1024]{1,0:T(8,128)}) %reduce-scatter.20.cloned.1.call-update) | async-done | bytes 1048592 | tf_op jit(solution)/shard_map/reduce_scatter | solution.py:341
  1220.4 75.7 %reduce-scatter.12.cloned.1.call-done = f32[256,1024]{1,0:T(8,128)} async-done(((f32[2048,1024]{1,0:T(8,128)}), f32[256,1024]{1,0:T(8,128)}) %reduce-scatter.12.cloned.1.call-update) | async-done | bytes 1048592 | tf_op jit(solution)/shard_map/reduce_scatter | solution.py:338
  1296.2 75.3 %reduce-scatter.14.cloned.1.call-done = f32[256,1024]{1,0:T(8,128)} async-done(((f32[2048,1024]{1,0:T(8,128)}), f32[256,1024]{1,0:T(8,128)}) %reduce-scatter.14.cloned.1.call-update) | async-done | bytes 1048592 | tf_op jit(solution)/shard_map/reduce_scatter | solution.py:339
  (697 shorter events, 336.8 us)
Async XLA Ops:
  7.2 35.6 %copy-start = (bf16[1024,512]{1,0:T(8,128)(2,1)S(1)}, bf16[1024,512]{1,0:T(8,128)(2,1)}, u32[]{:S(2)}) copy-start(bf16[1024,512]{1,0:T(8,128)(2,1)} %param.22) | copy-start | bytes 3145732
  51.9 31.9 %all-to-all-start = ((bf16[8,256,512]{2,1,0:T(8,128)(2,1)}), bf16[8,256,512]{2,1,0:T(8,128)(2,1)S(1)}, u32[]{:S(2)}, u32[]{:S(2)}) async-start(bf16[8,256,512]{2,1,0:T(8,128)(2,1)} %bitcast.520), calls=%async_computation | async-start | bytes 4194304 | tf_op jit(solution)/shard_map/all_to_all | solution.py:190
  57.2 112.1 %all-gather.5.cloned.1.call-start = ((), (), s32[]{:S(2)}) async-start(), calls=%async_computation.18 | async-start | bytes 5242880 | tf_op jit(solution)/shard_map/all_gather | solution.py:200
  60.2 23.6 %copy-start.67 = (s32[1024,1]{0,1:T(1,128)}, s32[1024,1]{0,1:T(1,128)S(1)}, u32[]{:S(2)}) copy-start(s32[1024,1]{0,1:T(1,128)S(1)} %compare_select_fusion.5) | copy-start | bytes 12292
  98.3 30.3 %all-to-all-start.2 = ((bf16[8,256,512]{2,1,0:T(8,128)(2,1)}), bf16[8,256,512]{2,1,0:T(8,128)(2,1)S(1)}, u32[]{:S(2)}, u32[]{:S(2)}) async-start(bf16[8,256,512]{2,1,0:T(8,128)(2,1)} %bitcast.519), calls=%async_computation.3 | async-start | bytes 4194304 | tf_op jit(solution)/shard_map/all_to_all | solution.py:193
  102.0 233.1 %all-gather.7.cloned.1.call-start = ((), (), s32[]{:S(2)}) async-start(), calls=%async_computation.19 | async-start | bytes 5242880 | tf_op jit(solution)/shard_map/all_gather | solution.py:201
  102.1 101.8 %copy-start.80 = (f32[16]{0:T(128)}, f32[16]{0:T(128)S(1)}, u32[]{:S(2)}) copy-start(f32[16]{0:T(128)S(1)} %exp.96) | copy-start | bytes 196
  102.3 254.9 %copy-start.63 = (f32[1024]{0:T(1024)}, f32[1024]{0:T(1024)S(1)}, u32[]{:S(2)}) copy-start(f32[1024]{0:T(1024)S(1)} %convert_element_type.156) | copy-start | bytes 12292
  103.3 253.9 %copy-start.59 = (f32[1024]{0:T(1024)}, f32[1024]{0:T(1024)S(1)}, u32[]{:S(2)}) copy-start(f32[1024]{0:T(1024)S(1)} %mul.878) | copy-start | bytes 12292
  103.9 71.4 %copy-start.69 = (f32[1,256]{1,0:T(1,128)}, f32[1,256]{1,0:T(1,128)S(1)}, u32[]{:S(2)}) copy-start(f32[1,256]{1,0:T(1,128)S(1)} %get-tuple-element.807) | copy-start | bytes 3076
  103.9 71.4 %copy-start.71 = (f32[1,256]{1,0:T(1,128)}, f32[1,256]{1,0:T(1,128)S(1)}, u32[]{:S(2)}) copy-start(f32[1,256]{1,0:T(1,128)S(1)} %get-tuple-element.808) | copy-start | bytes 3076
  103.9 71.4 %copy-start.73 = (f32[1,256]{1,0:T(1,128)}, f32[1,256]{1,0:T(1,128)S(1)}, u32[]{:S(2)}) copy-start(f32[1,256]{1,0:T(1,128)S(1)} %get-tuple-element.809) | copy-start | bytes 3076
  103.9 71.4 %copy-start.77 = (f32[1,256]{1,0:T(1,128)}, f32[1,256]{1,0:T(1,128)S(1)}, u32[]{:S(2)}) copy-start(f32[1,256]{1,0:T(1,128)S(1)} %get-tuple-element.810) | copy-start | bytes 3076
  104.0 79.3 %copy-start.41 = (f32[1024]{0:T(1024)}, f32[1024]{0:T(1024)S(1)}, u32[]{:S(2)}) copy-start(f32[1024]{0:T(1024)S(1)} %get-tuple-element.804) | copy-start | bytes 12292
  104.0 79.3 %copy-start.43 = (f32[1024]{0:T(1024)}, f32[1024]{0:T(1024)S(1)}, u32[]{:S(2)}) copy-start(f32[1024]{0:T(1024)S(1)} %get-tuple-element.805) | copy-start | bytes 12292
  104.0 79.3 %copy-start.45 = (f32[1024]{0:T(1024)}, f32[1024]{0:T(1024)S(1)}, u32[]{:S(2)}) copy-start(f32[1024]{0:T(1024)S(1)} %get-tuple-element.806) | copy-start | bytes 12292
  104.1 79.3 %copy-start.51 = (f32[1,1024]{1,0:T(1,128)}, f32[1,1024]{1,0:T(1,128)S(1)}, u32[]{:S(2)}) copy-start(f32[1,1024]{1,0:T(1,128)S(1)} %get-tuple-element.803) | copy-start | bytes 12292
  104.1 79.3 %copy-start.53 = (f32[1,1024]{1,0:T(1,128)}, f32[1,1024]{1,0:T(1,128)S(1)}, u32[]{:S(2)}) copy-start(f32[1,1024]{1,0:T(1,128)S(1)} %get-tuple-element.800) | copy-start | bytes 12292
  104.1 79.3 %copy-start.55 = (f32[1,1024]{1,0:T(1,128)}, f32[1,1024]{1,0:T(1,128)S(1)}, u32[]{:S(2)}) copy-start(f32[1,1024]{1,0:T(1,128)S(1)} %get-tuple-element.801) | copy-start | bytes 12292
  104.1 79.3 %copy-start.57 = (f32[1,1024]{1,0:T(1,128)}, f32[1,1024]{1,0:T(1,128)S(1)}, u32[]{:S(2)}) copy-start(f32[1,1024]{1,0:T(1,128)S(1)} %get-tuple-element.802) | copy-start | bytes 12292
  133.7 683.3 %reduce-scatter.10.cloned.1.call-start = ((), (), s32[]{:S(2)}) async-start(), calls=%async_computation.12 | async-start | bytes 10485760 | tf_op jit(solution)/shard_map/reduce_scatter | solution.py:306
  335.1 22.1 %copy-start.65 = (f32[1024]{0:T(1024)}, f32[1024]{0:T(1024)S(1)}, u32[]{:S(2)}) copy-start(f32[1024]{0:T(1024)S(1)} %add_rsqrt_fusion) | copy-start | bytes 12292
  403.3 10.8 copy-start.18
  404.0 10.7 copy-start.39
  429.7 10.5 copy-start.12
  453.8 10.8 copy-start.18
  454.6 10.7 copy-start.39
  504.3 10.8 copy-start.18
  505.1 10.7 copy-start.39
  530.7 10.5 copy-start.12
  554.8 10.8 copy-start.18
  555.6 10.7 copy-start.39
  609.4 13.4 copy-start.20
  609.4 13.4 copy-start.87
  640.6 323.9 %reduce-scatter.8.cloned.1.call-start = ((), (), s32[]{:S(2)}) async-start(), calls=%async_computation.11 | async-start | bytes 10485760 | tf_op jit(solution)/shard_map/reduce_scatter | solution.py:262
  652.6 429.2 %reduce-scatter.18.cloned.1.call-start = ((), (), s32[]{:S(2)}) async-start(), calls=%async_computation.16 | async-start | bytes 147456 | tf_op jit(solution)/shard_map/reduce_scatter | solution.py:340
  659.9 487.6 %reduce-scatter.16.cloned.1.call-start = ((), (), s32[]{:S(2)}) async-start(), calls=%async_computation.15 | async-start | bytes 2162688 | tf_op jit(solution)/shard_map/reduce_scatter | solution.py:298
  736.6 483.9 %reduce-scatter.20.cloned.1.call-start = ((), (), s32[]{:S(2)}) async-start(), calls=%async_computation.17 | async-start | bytes 9437184 | tf_op jit(solution)/shard_map/reduce_scatter | solution.py:341
  748.5 547.6 %reduce-scatter.12.cloned.1.call-start = ((), (), s32[]{:S(2)}) async-start(), calls=%async_computation.13 | async-start | bytes 9437184 | tf_op jit(solution)/shard_map/reduce_scatter | solution.py:338
  759.4 612.1 %reduce-scatter.14.cloned.1.call-start = ((), (), s32[]{:S(2)}) async-start(), calls=%async_computation.14 | async-start | bytes 9437184 | tf_op jit(solution)/shard_map/reduce_scatter | solution.py:339
  770.0 46.9 %copy-start.8 = (bf16[1024,512]{1,0:T(8,128)(2,1)S(1)}, bf16[1024,512]{1,0:T(8,128)(2,1)}, u32[]{:S(2)}) copy-start(bf16[1024,512]{1,0:T(8,128)(2,1)} %gather_fusion.1) | copy-start | bytes 3145732
  770.0 46.9 %copy-start.50 = (f32[1024]{0:T(1024)S(1)}, f32[1024]{0:T(1024)}, u32[]{:S(2)}) copy-start(f32[1024]{0:T(1024)} %copy-done.49) | copy-start | bytes 12292
  976.9 30.8 %all-to-all-start.3 = ((bf16[8,256,512]{2,1,0:T(8,128)(2,1)}), bf16[8,256,512]{2,1,0:T(8,128)(2,1)S(1)}, u32[]{:S(2)}, u32[]{:S(2)}) async-start(bf16[8,256,512]{2,1,0:T(8,128)(2,1)} %bitcast.521), calls=%async_computation.5 | async-start | bytes 4194304 | tf_op jit(solution)/shard_map/all_to_all | solution.py:331
  989.7 52.9 %copy-start.62 = (f32[1024]{0:T(1024)S(1)}, f32[1024]{0:T(1024)}, u32[]{:S(2)}) copy-start(f32[1024]{0:T(1024)} %get-tuple-element.746) | copy-start | bytes 12292
  989.7 53.2 %copy-start.93 = (f32[16]{0:T(128)S(1)}, f32[16]{0:T(128)}, u32[]{:S(2)}) copy-start(f32[16]{0:T(128)} %param.34) | copy-start | bytes 196
  989.7 53.2 %copy-start.82 = (f32[1024]{0:T(1024)S(1)}, f32[1024]{0:T(1024)}, u32[]{:S(2)}) copy-start(f32[1024]{0:T(1024)} %get-tuple-element.664) | copy-start | bytes 12292
  1007.7 66.9 %all-to-all-start.1 = ((bf16[8,256,512]{2,1,0:T(8,128)(2,1)}), bf16[8,256,512]{2,1,0:T(8,128)(2,1)}, u32[]{:S(2)}, u32[]{:S(2)}) async-start(bf16[8,256,512]{2,1,0:T(8,128)(2,1)} %bitcast.518), calls=%async_computation.2 | async-start | bytes 4194304 | tf_op jit(solution)/shard_map/all_to_all | solution.py:324
  1074.6 296.9 %copy-start.1 = (bf16[1024,512]{1,0:T(8,128)(2,1)S(1)}, bf16[1024,512]{1,0:T(8,128)(2,1)}, u32[]{:S(2)}) copy-start(bf16[1024,512]{1,0:T(8,128)(2,1)} %param.22) | copy-start | bytes 3145732
  (128 other events, 785.6 us)
Sparse Core Ops, SparseCore 0:
  89.1 80.1 all-gather.4
  171.5 79.2 all-gather.6
  640.8 176.1 reduce-scatter.9
  819.2 145.2 reduce-scatter.7
  967.9 38.5 reduce-scatter.17
  1009.3 138.2 reduce-scatter.15
  1151.6 68.8 reduce-scatter.19
  1224.8 71.2 reduce-scatter.11
  1300.2 71.2 reduce-scatter.13
where the time goes:
time: 1390 us; the launch traced here: 1380 us
  waiting for transfers between devices  565 us (41%)
  local copies, waits for them, and re-layouts  280 us (20%)
  matrix products  242 us (17%)
  blocking collectives  131 us (9%)
  other arithmetic  114 us (8%)
  starting transfers between devices  17.9 us (1%)
  between operations  15.4 us (1%)
    reduce_scatter x1, waiting for transfers between devices, per_device(): lax.psum_scatter(out_partial, 'tensor', scatter_dimension=1, tiled=True)  132 us
    dot_general x12, matrix products, span_step(): jnp.einsum('ij,hij,jhp->ihp', scores, decay_mask, weighted, precision=hig...  80.7 us
    reduce_scatter x1, waiting for transfers between devices, per_device(): lax.psum_scatter(gate_grad, 'dp', scatter_dimension=0, tiled=True)  75.7 us
    reduce_scatter x1, waiting for transfers between devices, per_device(): lax.psum_scatter(value_grad, 'dp', scatter_dimension=0, tiled=True)  75.3 us
    psum x1, blocking collectives, per_device(): lax.psum((state_back, conv_state_back, conv_state_bias_back), 'tensor')  73.6 us
    reduce_scatter x1, waiting for transfers between devices, per_device(): lax.psum_scatter(out_grad, 'dp', scatter_dimension=0, tiled=True)  72.9 us
    reduce_scatter x1, waiting for transfers between devices, per_device(): lax.psum_scatter(contract_rows(normed_part, state_part), ('dp', 'tensor')...  65.8 us
    reduce_scatter x1, waiting for transfers between devices, per_device(): lax.psum_scatter(back_partial, 'tensor', scatter_dimension=1, tiled=True)  41.7 us
  transfers between devices with their start and end apart: 13, of which 10 were waited for; matrix products, arithmetic and copies ran while one was open for 21% of the time, Pallas kernels for 0%

commit v1 on v0

v1 whole, which is shorter than its diff:
```python
import jax
import jax.numpy as jnp
from jax import lax
from jax.experimental import pallas as pl
from jax.experimental.pallas import tpu as pltpu
from jax.sharding import PartitionSpec as P

f32 = jnp.float32
bf16 = jnp.bfloat16
Q = 256
LANES = 128
HEAD_DIM = 64
highest = lax.Precision.HIGHEST
epsilon = 1e-05


def dot_nn(a, b, precision=None):
    return lax.dot_general(a, b, (((1,), (0,)), ((), ())), precision=precision, preferred_element_type=f32)


def dot_nt(a, b, precision=None):
    return lax.dot_general(a, b, (((1,), (1,)), ((), ())), precision=precision, preferred_element_type=f32)


def halves(values):
    high = values.astype(bf16)
    return jnp.concatenate([high, (values - high.astype(f32)).astype(bf16)], axis=1)


def dot_halves(a, values):
    both = dot_nn(a, halves(values))
    return both[:, :LANES] + both[:, LANES:]


def sigmoid(values):
    return 1.0 / (1.0 + jnp.exp(-values))


def fold_rows(values):
    return jnp.sum(values.reshape(-1, 8, values.shape[-1]), axis=0)


def segment_at(position, lengths_ref):
    total = lengths_ref[0, 0]
    seg = (position >= total).astype(jnp.int32)
    for index in range(1, lengths_ref.shape[1]):
        total = total + lengths_ref[0, index]
        seg = seg + (position >= total).astype(jnp.int32)
    return seg


def tap_mask(start, shift, rows, lengths_ref):
    position = start + lax.broadcasted_iota(jnp.int32, (rows, LANES), 0)
    same = (segment_at(position, lengths_ref) == segment_at(position - shift, lengths_ref)) & (position >= shift)
    return same.astype(f32)


def triangle(start, lengths_ref, transposed):
    first = lax.broadcasted_iota(jnp.int32, (Q, Q), 0)
    second = lax.broadcasted_iota(jnp.int32, (Q, Q), 1)
    same = segment_at(start + first, lengths_ref) == segment_at(start + second, lengths_ref)
    order = (second >= first) if transposed else (first >= second)
    return same & order


def head_columns(cum, step, cum_cols, step_cols):
    lane = lax.broadcasted_iota(jnp.int32, (Q, LANES), 1)
    for head in range(cum_cols.shape[0]):
        cum_cols[head] = jnp.broadcast_to(cum[:, head : head + 1], (Q, LANES))
    for pair in range(step_cols.shape[0]):
        even = jnp.broadcast_to(step[:, 2 * pair : 2 * pair + 1], (Q, LANES))
        odd = jnp.broadcast_to(step[:, 2 * pair + 1 : 2 * pair + 2], (Q, LANES))
        step_cols[pair] = jnp.where(lane < HEAD_DIM, even, odd)


def boundary(start, lengths_ref):
    position = start + lax.broadcasted_iota(jnp.int32, (Q, LANES), 0)
    seg = segment_at(position, lengths_ref)
    last = segment_at(jnp.full((1, LANES), start + Q - 1, jnp.int32), lengths_ref)
    before = segment_at(jnp.full((1, LANES), start - 1, jnp.int32), lengths_ref)
    before = jnp.where(start > 0, before, -1)
    return (seg == last), (seg == before), (last == before)


def softplus(values):
    return jnp.maximum(values, 0.0) + jnp.log1p(jnp.exp(-jnp.abs(values)))


def causal_taps(ext_ref, taps, bias, start, lengths_ref, columns):
    total = taps[3:4] * ext_ref[pl.ds(8, Q), columns]
    for shift in range(1, 4):
        mask = tap_mask(start, shift, Q, lengths_ref)
        total = total + taps[3 - shift : 4 - shift] * (ext_ref[pl.ds(8 - shift, Q), columns] * mask)
    return total + bias


def chunk_scalars(start, step_in, rate, lengths_ref, causal):
    step = softplus(step_in)
    log_decay = -step * jnp.exp(rate)
    cum = dot_nn(causal, log_decay, highest)
    return step, log_decay, cum


def fwd_kernel(
    lengths_ref, x_ref, gain_ref, wg_ref, wv_ref, ws_ref, wt_ref, tapv_ref, biasv_ref, taps_ref, biass_ref,
    stepb_ref, rate_ref, skip_ref,
    normed_ref, inv_ref, gate_ref, vraw_ref, pre_ref, y_ref, sraw_ref, spre_ref, stepin_ref, state_ref, sq_ref,
    carry, vext, sext, cum_cols, step_cols, cum_rows, neg_bias, scores, gated_sq,
):
    chunk = pl.program_id(0)
    start = chunk * Q
    pairs = carry.shape[0]

    @pl.when(chunk == 0)
    def _():
        carry[...] = jnp.zeros_like(carry)
        vext[pl.ds(0, 8)] = jnp.zeros((8, vext.shape[1]), f32)
        sext[pl.ds(0, 8)] = jnp.zeros((8, sext.shape[1]), f32)

    @pl.when(chunk > 0)
    def _():
        vext[pl.ds(0, 8)] = vext[pl.ds(Q, 8)]
        sext[pl.ds(0, 8)] = sext[pl.ds(Q, 8)]

    wide = x_ref[...].astype(f32)
    inv = lax.rsqrt(jnp.mean(wide * wide, axis=1, keepdims=True) + epsilon)
    normed = (wide * inv * gain_ref[...]).astype(bf16)
    normed_ref[...] = normed
    inv_ref[...] = inv
    gate_ref[...] = dot_nn(normed, wg_ref[...])
    vext[pl.ds(8, Q)] = dot_nn(normed, wv_ref[...])
    sext[pl.ds(8, Q)] = dot_nn(normed, ws_ref[...])
    step_in = dot_nn(normed, wt_ref[...]) + stepb_ref[...]
    stepin_ref[...] = step_in
    vraw_ref[...] = vext[pl.ds(8, Q)]
    sraw_ref[...] = sext[pl.ds(8, Q)]

    can_see = triangle(start, lengths_ref, False)
    neg_bias[...] = jnp.where(can_see, 0.0, -1e30)
    row = lax.broadcasted_iota(jnp.int32, (Q, Q), 0)
    col = lax.broadcasted_iota(jnp.int32, (Q, Q), 1)
    step, log_decay, cum = chunk_scalars(start, step_in, rate_ref[...], lengths_ref, (row >= col).astype(f32))
    cum_rows[...] = cum.T
    head_columns(cum, step, cum_cols, step_cols)

    for half in range(2):
        columns = slice(half * LANES, (half + 1) * LANES)
        spre_ref[:, columns] = causal_taps(
            sext, taps_ref[:, columns], biass_ref[:, columns], start, lengths_ref, columns
        )
    spre = spre_ref[...]
    state_conv = spre * sigmoid(spre)
    entry = state_conv[:, :LANES]
    leave = state_conv[:, LANES:]
    scores[...] = dot_nt(leave, entry, highest)
    entry_t = entry.T.astype(bf16)
    leave_low = leave.astype(bf16)
    with_last, with_before, through = boundary(start, lengths_ref)
    to_last = with_last.astype(f32)
    from_before = with_before.astype(f32)
    passes = through.astype(f32)
    lane = lax.broadcasted_iota(jnp.int32, (Q, LANES), 1)
    gated_sq[...] = jnp.zeros_like(gated_sq)

    def one_pair(pair, nothing):
        columns = pl.ds(pl.multiple_of(pair * LANES, LANES), LANES)
        pre = causal_taps(vext, tapv_ref[:, columns], biasv_ref[:, columns], start, lengths_ref, columns)
        pre_ref[:, columns] = pre
        x = pre * sigmoid(pre)
        weighted = x * step_cols[pair]
        both = halves(weighted)
        results = []
        for half in range(2):
            head = 2 * pair + half
            c_col = cum_cols[head]
            c_row = cum_rows[pl.ds(head, 1), :]
            top = scores[:LANES, :LANES] * jnp.exp(c_col[:LANES] - c_row[:, :LANES] + neg_bias[:LANES, :LANES])
            low_left = scores[LANES:, :LANES] * jnp.exp(c_col[LANES:] - c_row[:, :LANES] + neg_bias[LANES:, :LANES])
            low_right = scores[LANES:, LANES:] * jnp.exp(c_col[LANES:] - c_row[:, LANES:] + neg_bias[LANES:, LANES:])
            upper = dot_nn(top.astype(bf16), both[:LANES])
            lower = dot_nn(jnp.concatenate([low_left, low_right], axis=1).astype(bf16), both)
            out = jnp.concatenate([upper, lower], axis=0)
            results.append(out[:, :LANES] + out[:, LANES:])
        inside = jnp.where(lane < HEAD_DIM, results[0], results[1])
        cum_pair = jnp.where(lane < HEAD_DIM, cum_cols[2 * pair], cum_cols[2 * pair + 1])
        cum_last = cum_pair[Q - 1 :]
        held = carry[pair]
        state_ref[0, pair] = held
        carried = dot_halves(leave_low, held) * (jnp.exp(cum_pair) * from_before)
        y = inside + carried + skip_ref[:, columns] * x
        y_ref[:, columns] = y
        to_end = jnp.exp(cum_last - cum_pair) * to_last
        carry[pair] = held * (jnp.exp(cum_last) * passes) + dot_halves(entry_t, to_end * weighted)
        gate = gate_ref[:, columns]
        gated = y * (gate * sigmoid(gate))
        gated_sq[...] += gated * gated
        return nothing

    lax.fori_loop(0, pairs, one_pair, 0)
    sq_ref[...] = jnp.sum(gated_sq[...], axis=1, keepdims=True)


def bwd_kernel(
    lengths_ref, dsc_ref, rms_ref, coef_ref, gain_ref, gate_ref, vraw_ref, pre_ref, y_ref, sraw_ref, spre_ref,
    stepin_ref, state_ref, next_ref, tapv_ref, taps_ref, stepb_ref, rate_ref, skip_ref,
    dgate_ref, dvalue_ref, dstate_ref, dstep_ref, dot_ref, sumv_ref, sums_ref, sumh_ref,
    d_carry, dvext, dsext, cum_cols, step_cols, cum_rows, neg_bias, scores, d_scores, d_entry, d_leave, acc_step,
    acc_cum, acc_dot,
):
    index = pl.program_id(0)
    chunks = pl.num_programs(0)
    chunk = chunks - 1 - index
    start = chunk * Q
    pairs = d_carry.shape[0]

    @pl.when(index == 0)
    def _():
        d_carry[...] = jnp.zeros_like(d_carry)
        dvext[pl.ds(Q, 8)] = jnp.zeros((8, dvext.shape[1]), f32)
        dsext[pl.ds(Q, 8)] = jnp.zeros((8, dsext.shape[1]), f32)
        sumv_ref[...] = jnp.zeros_like(sumv_ref)
        sums_ref[...] = jnp.zeros_like(sums_ref)
        sumh_ref[...] = jnp.zeros_like(sumh_ref)

    @pl.when(index > 0)
    def _():
        dvext[pl.ds(Q, 8)] = dvext[pl.ds(0, 8)]
        dsext[pl.ds(Q, 8)] = dsext[pl.ds(0, 8)]

    can_see = triangle(start, lengths_ref, True)
    neg_bias[...] = jnp.where(can_see, 0.0, -1e30)
    row = lax.broadcasted_iota(jnp.int32, (Q, Q), 0)
    col = lax.broadcasted_iota(jnp.int32, (Q, Q), 1)
    step_in = stepin_ref[...]
    step, log_decay, cum = chunk_scalars(start, step_in, rate_ref[...], lengths_ref, (row >= col).astype(f32))
    cum_rows[...] = cum.T
    head_columns(cum, step, cum_cols, step_cols)

    spre = spre_ref[...]
    spre_sig = sigmoid(spre)
    state_conv = spre * spre_sig
    entry = state_conv[:, :LANES]
    leave = state_conv[:, LANES:]
    scores[...] = dot_nt(entry, leave, highest)
    entry_low = entry.astype(bf16)
    leave_low = leave.astype(bf16)
    leave_t = leave.T.astype(bf16)
    with_last, with_before, through = boundary(start, lengths_ref)
    to_last = with_last.astype(f32)
    from_before = with_before.astype(f32)
    passes = through.astype(f32)
    lane = lax.broadcasted_iota(jnp.int32, (Q, LANES), 1)
    first_half = lane < HEAD_DIM
    row_lane = lax.broadcasted_iota(jnp.int32, (Q, LANES), 0)
    for ref in (d_scores, d_entry, d_leave, acc_step, acc_cum, acc_dot):
        ref[...] = jnp.zeros_like(ref)
    rms = rms_ref[...]
    coef = coef_ref[...]

    def one_pair(pair, nothing):
        columns = pl.ds(pl.multiple_of(pair * LANES, LANES), LANES)
        pre = pre_ref[:, columns]
        pre_sig = sigmoid(pre)
        x = pre * pre_sig
        step_pair = step_cols[pair]
        weighted = x * step_pair
        gate = gate_ref[:, columns]
        gate_sig = sigmoid(gate)
        gate_silu = gate * gate_sig
        y = y_ref[:, columns]
        gated = y * gate_silu
        d_scaled = dsc_ref[:, columns].astype(f32)
        d_gated = rms * (d_scaled * gain_ref[:, columns]) - gated * coef
        sumv_ref[pl.ds(0, 8), columns] += fold_rows(d_scaled * gated * rms)
        d_gate = (d_gated * y * (gate_sig + gate_silu * (1.0 - gate_sig))).astype(bf16)
        dgate_ref[:, columns] = d_gate
        acc_dot[...] += d_gate.astype(f32) * gate
        d_y = d_gated * gate_silu
        skip = skip_ref[:, columns]
        sumv_ref[pl.ds(8, 8), columns] += fold_rows(d_y * x)
        y_scan = y - skip * x

        d_y_low = d_y.astype(bf16)
        d_y_t = d_y.T.astype(bf16)
        d_y_both = halves(d_y)
        weighted_low = weighted.astype(bf16)
        results = []
        for half in range(2):
            head = 2 * pair + half
            own = jnp.where(first_half if half == 0 else ~first_half, weighted_low, jnp.zeros_like(weighted_low))
            d_m_top = dot_nn(own[:LANES], d_y_t)
            d_m_low = dot_nn(own[LANES:], d_y_t[:, LANES:])
            c_col = cum_cols[head]
            c_row = cum_rows[pl.ds(head, 1), :]
            l_top = jnp.exp(c_row - jnp.concatenate([c_col[:LANES]] * 2, axis=1) + neg_bias[:LANES])
            l_low = jnp.exp(c_row[:, LANES:] - c_col[LANES:] + neg_bias[LANES:, LANES:])
            d_scores[:LANES] += d_m_top * l_top
            d_scores[LANES:, LANES:] += d_m_low * l_low
            m_top = (scores[:LANES] * l_top).astype(bf16)
            m_low = (scores[LANES:, LANES:] * l_low).astype(bf16)
            upper = dot_nn(m_top, d_y_both)
            lower = dot_nn(m_low, d_y_both[LANES:])
            out = jnp.concatenate([upper, lower], axis=0)
            results.append(out[:, :LANES] + out[:, LANES:])
        d_weighted = jnp.where(first_half, results[0], results[1])
        cum_pair = jnp.where(first_half, cum_cols[2 * pair], cum_cols[2 * pair + 1])
        cum_last = cum_pair[Q - 1 :]
        to_end = jnp.exp(cum_last - cum_pair) * to_last
        from_start = jnp.exp(cum_pair) * from_before
        d_state = d_carry[pair]
        held = state_ref[0, pair]
        d_weighted = d_weighted + dot_halves(entry_low, d_state) * to_end
        d_entry[...] += dot_nt((to_end * weighted).astype(bf16), d_state.astype(bf16))
        moved = from_start * d_y
        d_leave[...] += dot_nt(moved.astype(bf16), held.astype(bf16))
        state_dot = jnp.sum(next_ref[0, pair] * d_state, axis=0, keepdims=True)
        d_carry[pair] = d_state * (jnp.exp(cum_last) * passes) + dot_halves(leave_t, moved)

        to_step = d_weighted * x
        to_cum = d_y * y_scan - to_step * step_pair + jnp.where(row_lane == Q - 1, state_dot, 0.0)
        place = lax.broadcasted_iota(jnp.int32, (2 * LANES, LANES), 1)
        source = lax.broadcasted_iota(jnp.int32, (2 * LANES, LANES), 0)
        source = (lax.rem(source, LANES) >= HEAD_DIM).astype(jnp.int32) + 2 * pair
        gather = (place == source).astype(bf16)
        acc_step[...] += dot_nn(halves(to_step), gather)
        acc_cum[...] += dot_nn(halves(to_cum), gather)

        d_x = d_weighted * step_pair + skip * d_y
        d_pre = d_x * (pre_sig + x * (1.0 - pre_sig))
        dvext[pl.ds(0, Q), columns] = d_pre
        sumv_ref[pl.ds(16, 8), columns] += fold_rows(d_pre)
        vraw = vraw_ref[:, columns]
        total = tapv_ref[3:4, columns] * d_pre
        sumv_ref[pl.ds(24, 8), columns] += fold_rows(vraw * d_pre)
        for shift in range(1, 4):
            moved_back = dvext[pl.ds(shift, Q), columns] * later_mask(start, shift)
            total = total + tapv_ref[3 - shift : 4 - shift, columns] * moved_back
            sumv_ref[pl.ds(24 + 8 * shift, 8), columns] += fold_rows(vraw * moved_back)
        d_value = total.astype(bf16)
        dvalue_ref[:, columns] = d_value
        acc_dot[...] += d_value.astype(f32) * vraw
        return nothing

    def later_mask(begin, shift):
        position = begin + lax.broadcasted_iota(jnp.int32, (Q, LANES), 0)
        same = segment_at(position, lengths_ref) == segment_at(position + shift, lengths_ref)
        return (same & (position + shift < chunks * Q)).astype(f32)

    lax.fori_loop(0, pairs, one_pair, 0)

    d_cum = acc_cum[...]
    d_log = dot_nn(can_see.astype(f32), d_cum, highest)
    rate = jnp.exp(rate_ref[...])
    d_step_in = (acc_step[...] - d_log * rate) * sigmoid(step_in)
    d_step = d_step_in.astype(bf16)
    dstep_ref[...] = d_step
    step_raw = step_in - stepb_ref[...]
    real = lane < 2 * pairs
    acc_dot[...] += jnp.where(real, d_step.astype(f32) * step_raw, 0.0)
    sumh_ref[pl.ds(0, 8)] += fold_rows(d_step_in)
    sumh_ref[pl.ds(8, 8)] += fold_rows(d_log * log_decay)

    d_scores_low = d_scores[...]
    d_b = d_entry[...] + dot_halves(d_scores_low.astype(bf16), leave)
    d_c = d_leave[...] + dot_halves(d_scores_low.T.astype(bf16), entry)
    for half, grad in enumerate((d_b, d_c)):
        columns = slice(half * LANES, (half + 1) * LANES)
        part = spre_sig[:, columns]
        d_pre = grad * (part + state_conv[:, columns] * (1.0 - part))
        dsext[pl.ds(0, Q), columns] = d_pre
        sums_ref[pl.ds(0, 8), columns] += fold_rows(d_pre)
        sraw = sraw_ref[:, columns]
        total = taps_ref[3:4, columns] * d_pre
        sums_ref[pl.ds(8, 8), columns] += fold_rows(sraw * d_pre)
        for shift in range(1, 4):
            moved_back = dsext[pl.ds(shift, Q), columns] * later_mask(start, shift)
            total = total + taps_ref[3 - shift : 4 - shift, columns] * moved_back
            sums_ref[pl.ds(8 + 8 * shift, 8), columns] += fold_rows(sraw * moved_back)
        d_state_raw = total.astype(bf16)
        dstate_ref[:, columns] = d_state_raw
        acc_dot[...] += d_state_raw.astype(f32) * sraw
    dot_ref[...] = jnp.sum(acc_dot[...], axis=1, keepdims=True)


def whole(shape):
    zeros = (0,) * len(shape)
    return pl.BlockSpec(shape, lambda i: zeros, pipeline_mode=pl.Buffered(1))


def forward_mixer(lengths, x, gain, wg, wv, ws, wt, tapv, biasv, taps, biass, stepb, rate, skip):
    rows, model = x.shape
    inner = wg.shape[1]
    chunks, pairs = rows // Q, inner // LANES

    def by_chunk(width):
        return pl.BlockSpec((Q, width), lambda i: (i, 0))

    out_shape = [
        jax.ShapeDtypeStruct((rows, model), bf16),
        jax.ShapeDtypeStruct((rows, 1), f32),
        jax.ShapeDtypeStruct((rows, inner), f32),
        jax.ShapeDtypeStruct((rows, inner), f32),
        jax.ShapeDtypeStruct((rows, inner), f32),
        jax.ShapeDtypeStruct((rows, inner), f32),
        jax.ShapeDtypeStruct((rows, 2 * LANES), f32),
        jax.ShapeDtypeStruct((rows, 2 * LANES), f32),
        jax.ShapeDtypeStruct((rows, LANES), f32),
        jax.ShapeDtypeStruct((chunks, pairs, LANES, LANES), f32),
        jax.ShapeDtypeStruct((rows, 1), f32),
    ]
    out_specs = [
        by_chunk(model), by_chunk(1), by_chunk(inner), by_chunk(inner), by_chunk(inner), by_chunk(inner),
        by_chunk(2 * LANES), by_chunk(2 * LANES), by_chunk(LANES),
        pl.BlockSpec((1, pairs, LANES, LANES), lambda i: (i, 0, 0, 0)),
        by_chunk(1),
    ]
    return pl.pallas_call(
        fwd_kernel,
        grid=(chunks,),
        out_shape=out_shape,
        in_specs=[pl.BlockSpec(memory_space=pltpu.SMEM), by_chunk(model)] + [
            whole(v.shape) for v in (gain, wg, wv, ws, wt, tapv, biasv, taps, biass, stepb, rate, skip)
        ],
        out_specs=out_specs,
        scratch_shapes=[
            pltpu.VMEM((pairs, LANES, LANES), f32),
            pltpu.VMEM((Q + 8, inner), f32),
            pltpu.VMEM((Q + 8, 2 * LANES), f32),
            pltpu.VMEM((2 * pairs, Q, LANES), f32),
            pltpu.VMEM((pairs, Q, LANES), f32),
            pltpu.VMEM((LANES, Q), f32),
            pltpu.VMEM((Q, Q), f32),
            pltpu.VMEM((Q, Q), f32),
            pltpu.VMEM((Q, LANES), f32),
        ],
        compiler_params=pltpu.CompilerParams(vmem_limit_bytes=56 << 20),
        name="mixer_forward",
    )(lengths, x, gain, wg, wv, ws, wt, tapv, biasv, taps, biass, stepb, rate, skip)


def backward_mixer(lengths, dsc, rms, coef, gain, gate, vraw, pre, y, sraw, spre, stepin, states, tapv, taps, stepb, rate, skip):
    rows, inner = gate.shape
    chunks, pairs = rows // Q, inner // LANES

    def by_chunk(width):
        return pl.BlockSpec((Q, width), lambda i: (chunks - 1 - i, 0))

    def state_block(ahead):
        return pl.BlockSpec(
            (1, pairs, LANES, LANES), lambda i: (jnp.minimum(chunks - 1 - i + ahead, chunks - 1), 0, 0, 0)
        )

    out_shape = [
        jax.ShapeDtypeStruct((rows, inner), bf16),
        jax.ShapeDtypeStruct((rows, inner), bf16),
        jax.ShapeDtypeStruct((rows, 2 * LANES), bf16),
        jax.ShapeDtypeStruct((rows, LANES), bf16),
        jax.ShapeDtypeStruct((rows, 1), f32),
        jax.ShapeDtypeStruct((56, inner), f32),
        jax.ShapeDtypeStruct((40, 2 * LANES), f32),
        jax.ShapeDtypeStruct((16, LANES), f32),
    ]
    out_specs = [
        by_chunk(inner), by_chunk(inner), by_chunk(2 * LANES), by_chunk(LANES), by_chunk(1),
        whole((56, inner)), whole((40, 2 * LANES)), whole((16, LANES)),
    ]
    return pl.pallas_call(
        bwd_kernel,
        grid=(chunks,),
        out_shape=out_shape,
        in_specs=[
            pl.BlockSpec(memory_space=pltpu.SMEM), by_chunk(inner), by_chunk(1), by_chunk(1), whole(gain.shape),
            by_chunk(inner), by_chunk(inner), by_chunk(inner), by_chunk(inner), by_chunk(2 * LANES),
            by_chunk(2 * LANES), by_chunk(LANES), state_block(0), state_block(1),
        ] + [whole(v.shape) for v in (tapv, taps, stepb, rate, skip)],
        out_specs=out_specs,
        scratch_shapes=[
            pltpu.VMEM((pairs, LANES, LANES), f32),
            pltpu.VMEM((Q + 8, inner), f32),
            pltpu.VMEM((Q + 8, 2 * LANES), f32),
            pltpu.VMEM((2 * pairs, Q, LANES), f32),
            pltpu.VMEM((pairs, Q, LANES), f32),
            pltpu.VMEM((LANES, Q), f32),
            pltpu.VMEM((Q, Q), f32),
            pltpu.VMEM((Q, Q), f32),
            pltpu.VMEM((Q, Q), f32),
            pltpu.VMEM((Q, LANES), f32),
            pltpu.VMEM((Q, LANES), f32),
            pltpu.VMEM((Q, LANES), f32),
            pltpu.VMEM((Q, LANES), f32),
            pltpu.VMEM((Q, LANES), f32),
        ],
        compiler_params=pltpu.CompilerParams(vmem_limit_bytes=56 << 20),
        name="mixer_backward",
    )(lengths, dsc, rms, coef, gain, gate, vraw, pre, y, sraw, spre, stepin, states, states, tapv, taps, stepb, rate, skip)


def contract_rows(left, right):
    return lax.dot_general(left, right, (((0,), (0,)), ((), ())), preferred_element_type=f32)


def pad_heads(values):
    return jnp.pad(values, ((0, 0), (0, LANES - values.shape[1])))


def unfold(sums, index):
    return jnp.sum(sums[8 * index : 8 * index + 8], axis=0)


def per_device(
    tokens, cotangent, norm_gain, gate_proj, value_proj, state_proj, step_proj, conv_value, conv_value_bias,
    conv_state, conv_state_bias, step_bias, decay_log, skip_gain, gate_gain, out_proj, token_order, lengths,
):
    groups = lax.axis_size("dp")
    group = lax.axis_index("dp")
    slots = lax.axis_size("tensor")
    slot = lax.axis_index("tensor")
    rows, width = tokens.shape
    model = width * slots
    inner = gate_proj.shape[1]
    heads = step_bias.shape[0]
    run = 2 * rows // groups
    runs = rows // run

    source_run = token_order.reshape(groups, runs, run)[:, :, 0] // run
    source_group = source_run // runs
    from_here = source_group == group
    send_run = jnp.sum(jnp.where(from_here, source_run % runs, 0), axis=1)
    arrive_from = lax.dynamic_index_in_dim(source_group, group, 0, keepdims=False)
    every = jnp.arange(groups, dtype=jnp.int32)
    back_run = jnp.sum(
        jnp.where(arrive_from[None, :] == every[:, None], jnp.arange(runs, dtype=jnp.int32)[None, :], 0), axis=1
    )
    local_run = group * runs + jnp.arange(runs, dtype=jnp.int32)
    return_from = jnp.sum(
        jnp.where(source_run[None] == local_run[:, None, None], every[None, :, None], 0), axis=(1, 2)
    )

    def exchange(values, choose_send, choose_arrive):
        cut = values.reshape(runs, run, width)[choose_send]
        arrived = lax.all_to_all(cut, "dp", split_axis=0, concat_axis=0, tiled=True)
        return arrived[choose_arrive].reshape(rows, width)

    packed_tokens = exchange(tokens, send_run, arrive_from)
    packed_cotangent = exchange(cotangent, send_run, arrive_from)
    full_tokens = lax.all_gather(packed_tokens, "tensor", axis=1, tiled=True)
    full_cotangent = lax.all_gather(packed_cotangent, "tensor", axis=1, tiled=True)

    gain_full = norm_gain.astype(f32)
    tapv = conv_value.astype(f32)
    taps = conv_state.astype(f32)
    stepb = pad_heads(step_bias[None])
    rate = pad_heads(decay_log[None])
    skip = jnp.repeat(skip_gain, HEAD_DIM)[None]
    (normed, inv_rms, gate, vraw, pre, y, sraw, spre, stepin, states, squares) = forward_mixer(
        lengths, full_tokens, gain_full[None], gate_proj, value_proj, state_proj, pad_heads(step_proj), tapv,
        conv_value_bias.astype(f32)[None], taps, conv_state_bias.astype(f32)[None], stepb, rate, skip,
    )
    d_scaled = dot_nn(full_cotangent, out_proj)
    gain_wide = gate_gain.astype(f32)[None]
    gated = y * jax.nn.silu(gate)
    inner_dot = jnp.sum(d_scaled * gain_wide * gated, axis=1, keepdims=True)
    squares, inner_dot = lax.psum((squares, inner_dot), "tensor")
    inner_total = inner * slots
    inner_rms = lax.rsqrt(squares / inner_total + epsilon)
    scaled = (gated * inner_rms * gain_wide).astype(bf16)
    out_partial = dot_nt(scaled, out_proj).astype(bf16)
    out_share = lax.psum_scatter(out_partial, "tensor", scatter_dimension=1, tiled=True)
    output_packed = (packed_tokens.astype(f32) + out_share.astype(f32)).astype(bf16)
    out_grad = contract_rows(full_cotangent, scaled).astype(bf16)
    coef = inner_rms**3 * inner_dot / inner_total

    (d_gate, d_value, d_state, d_step, row_dot, sumv, sums, sumh) = backward_mixer(
        lengths, d_scaled, inner_rms, coef, gain_wide, gate, vraw, pre, y, sraw, spre, stepin, states, tapv, taps,
        stepb, rate, skip,
    )
    row_dot = lax.psum(row_dot, "tensor")
    back_partial = (
        dot_nt(d_gate, gate_proj) + dot_nt(d_value, value_proj) + dot_nt(d_state, state_proj)
        + dot_nt(d_step[:, :heads], step_proj)
    ).astype(bf16)
    back_share = lax.psum_scatter(back_partial, "tensor", scatter_dimension=1, tiled=True).astype(f32)
    gate_grad = contract_rows(normed, d_gate).astype(bf16)
    value_grad = contract_rows(normed, d_value).astype(bf16)
    state_grad = contract_rows(normed, d_state)
    step_grad = contract_rows(normed, d_step[:, :heads])
    unit_share = packed_tokens.astype(f32) * inv_rms
    gain_share = lax.dynamic_slice_in_dim(gain_full, slot * width, width, 0)
    norm_gain_back = jnp.sum(back_share * unit_share, axis=0)
    d_unit = back_share * gain_share
    input_back = packed_cotangent.astype(f32) + inv_rms * (d_unit - unit_share * (row_dot / model))
    layer_output = exchange(output_packed, back_run, return_from)
    tokens_grad = exchange(input_back.astype(bf16), back_run, return_from)

    def share(grad):
        return lax.psum_scatter(grad, "dp", scatter_dimension=0, tiled=True).astype(f32)

    out_grad_share, gate_share, value_share = share(out_grad), share(gate_grad), share(value_grad)
    step_share = share(step_grad)
    state_share = lax.psum_scatter(state_grad, ("dp", "tensor"), scatter_dimension=0, tiled=True).astype(f32)
    conv_state_sum, conv_state_bias_sum = lax.psum(
        (jnp.stack([unfold(sums, 4 - tap) for tap in range(4)]), unfold(sums, 0)), "tensor"
    )
    small = lax.psum(
        (
            norm_gain_back,
            jnp.stack([unfold(sumv, 6 - tap) for tap in range(4)]),
            unfold(sumv, 2),
            conv_state_sum,
            conv_state_bias_sum,
            unfold(sumh, 0)[:heads],
            unfold(sumh, 1)[:heads],
            jnp.sum(unfold(sumv, 1).reshape(heads, HEAD_DIM), axis=1),
            unfold(sumv, 0),
        ),
        "dp",
    )
    return (
        layer_output, tokens_grad, small[0], gate_share, value_share, state_share, step_share, small[1], small[2],
        small[3], small[4], small[5], small[6], small[7], small[8], out_grad_share,
    )


def solution(mesh):
    across = P(None, "tensor")
    both = P("dp", "tensor")
    heads = P("tensor")
    return jax.shard_map(
        per_device,
        mesh=mesh,
        in_specs=(
            both, both, P(), across, across, P(), across, across, heads, P(), P(), heads, heads, heads, heads, across,
            P(), P("dp", None),
        ),
        out_specs=(
            both, both, heads, both, both, P(("dp", "tensor"), None), both, across, heads, P(), P(), heads, heads, heads,
            heads, both,
        ),
        check_vma=False,
    )
```

time: 1390 us -> 829 us (0.60)
  local copies, waits for them, and re-layouts: 280 us -> 24.1 us
  matrix products: 242 us -> 88.8 us
  waiting for transfers between devices: 565 us -> 415 us
  Pallas kernels: 0 us -> 108 us
  other arithmetic: 114 us -> 15.1 us
    dot_general x58 -> x6, matrix products: 198 us -> 49.5 us  [the longest x5 36.9 us: dot_nt(): lax.dot_general(a, b, (((1,), (1,)), ((), ())), precision=precision, pref...]
    reduce_scatter x1, waiting for transfers between devices: 132 us -> 0.02 us  [per_device(): lax.psum_scatter(out_partial, 'tensor', scatter_dimension=1, tiled=True)]
    pallas_call x0 -> x2, Pallas kernels: none -> 108 us  [the longest x1 58.3 us: backward_mixer(): pl.pallas_call(bwd_kernel, grid=(chunks,), out_shape=out_shape, in_specs=...]
    scatter x3 -> x0, local copies, waits for them, and re-layouts: 65.5 us -> none  [the longest x1 30.6 us: per_device(): return_slot = jnp.zeros((row_count,), jnp.int32).at[jnp.where(from_here,...]
    reshape x13 -> x2, local copies, waits for them, and re-layouts: 52 us -> 0.93 us  [the longest x1 0.86 us: per_device(): source_run = token_order.reshape(groups, runs, run)[:, :, 0] // run]
    gather x8, local copies, waits for them, and re-layouts: 59 us -> 17.5 us  [the longest x4 9.54 us: exchange(): return arrived[choose_arrive].reshape(rows, width)]
    reduce_scatter x1, waiting for transfers between devices: 41.7 us -> 7.22 us  [per_device(): lax.psum_scatter(back_partial, 'tensor', scatter_dimension=1, tiled=True)]
    all_gather x1, waiting for transfers between devices: 0.02 us -> 31.5 us  [per_device(): lax.all_gather(packed_cotangent, 'tensor', axis=1, tiled=True)]
  transfers between devices with their start and end apart: 13 -> 12, of which waited for: 10 -> 10; matrix products, arithmetic and copies ran while one was open for 21% -> 12% of each run, Pallas kernels for 0% -> 13%
where the time goes in v1:
time: 829 us; the launch traced here: 820 us
  waiting for transfers between devices  415 us (50%)
  blocking collectives  140 us (17%)
  Pallas kernels  108 us (13%)
  matrix products  88.8 us (11%)
  local copies, waits for them, and re-layouts  24.1 us (3%)
  other arithmetic  15.1 us (2%)
  between operations  14.5 us (2%)
  starting transfers between devices  14 us (2%)
    reduce_scatter x1, waiting for transfers between devices, per_device(): lax.psum_scatter(state_grad, ('dp', 'tensor'), scatter_dimension=0, tiled...  141 us
    reduce_scatter x4, waiting for transfers between devices, share(): lax.psum_scatter(grad, 'dp', scatter_dimension=0, tiled=True).astype(f32)  134 us
    all_to_all x3, waiting for transfers between devices, exchange(): arrived = lax.all_to_all(cut, 'dp', split_axis=0, concat_axis=0, tiled=True)  60.1 us
    pallas_call x1, Pallas kernels, backward_mixer(): pl.pallas_call(bwd_kernel, grid=(chunks,), out_shape=out_shape, in_specs=...  58.3 us
    pallas_call x1, Pallas kernels, forward_mixer(): pl.pallas_call(fwd_kernel, grid=(chunks,), out_shape=out_shape, in_specs=...  50 us
    psum x1, blocking collectives, per_device(): row_dot = lax.psum(row_dot, 'tensor')  45.5 us
    psum x1, blocking collectives, per_device(): squares, inner_dot = lax.psum((squares, inner_dot), 'tensor')  41 us
    all_gather x1, waiting for transfers between devices, per_device(): full_tokens = lax.all_gather(packed_tokens, 'tensor', axis=1, tiled=True)  40.3 us
  transfers between devices with their start and end apart: 12, of which 10 were waited for; matrix products, arithmetic and copies ran while one was open for 12% of the time, Pallas kernels for 13%

profile of v1, /device:TPU:0, one launch (start us, length us, event | category | flops | bytes accessed | tf_op | source)
XLA Modules:
  0.0 819.9 jit_solution(4602902680154648214)
XLA Ops:
  7.2 0.9 reshape.164
  8.4 2.0 gather_fusion
  10.5 5.3 all-to-all-start
  16.0 26.4 %all-to-all-done = bf16[8,256,512]{2,1,0:T(8,128)(2,1)S(1)} async-done(((bf16[8,256,512]{2,1,0:T(8,128)(2,1)}), bf16[8,256,512]{2,1,0:T(8,128)(2,1)S(1)}, u32[]{:S(2)}, u32[]{:S(2)}) %all-to-all-start) | async-done | bytes 2097184 | tf_op jit(solution)/shard_map/all_to_all | solution.py:541
  42.4 1.6 gather_fusion.1
  44.1 0.7 gather_fusion.4
  44.9 29.9 %all_to_all.20 = bf16[8,256,512]{2,1,0:T(8,128)(2,1)} all-to-all(bf16[8,256,512]{2,1,0:T(8,128)(2,1)S(1)} %gather_fusion.4), channel_id=1, replica_groups=mesh['dp'=8,'tensor'=4] {'dp'}, dimensions={0} | all-to-all | bytes 4194304 | tf_op jit(solution)/shard_map/all_to_all | solution.py:541
  74.8 3.2 gather_fusion.5
  80.9 0.7 broadcast_in_dim_reshape.3.skip_ref
  83.1 0.9 pad.11.wt_ref
  84.0 40.3 %all-gather.3.cloned.1.call-done.x_ref = bf16[1024,2048]{1,0:T(8,128)(2,1)} async-done(((bf16[1024,512]{1,0:T(8,128)(2,1)}), bf16[1024,2048]{1,0:T(8,128)(2,1)}) %all-gather.3.cloned.1.call-update) | async-done | bytes 4194320 | tf_op jit(solution)/shard_map/all_gather | solution.py:546
  124.3 50.0 %mixer_forward.1 = (bf16[1024,2048]{1,0:T(8,128)(2,1)}, f32[1024,1]{1,0:T(8,128)}, f32[1024,1024]{1,0:T(8,128)}, f32[1024,1024]{1,0:T(8,128)}, f32[1024,1024]{1,...) custom-call(s32[1,3]{1,0:T(1,128)} %lengths_ref.3, ...), custom_call_target="tpu_custom_call" | custom-call | tf_op jit(solution)/shard_map/mixer_forward/pallas_call | solution.py:417
  174.4 31.5 %all-gather.5.cloned.1.call-done = bf16[1024,2048]{1,0:T(8,128)(2,1)} async-done(((bf16[1024,512]{1,0:T(8,128)(2,1)}), bf16[1024,2048]{1,0:T(8,128)(2,1)}) %all-gather.5.cloned.1.call-update) | async-done | bytes 4194320 | tf_op jit(solution)/shard_map/all_gather | solution.py:547
  205.8 12.7 %multiply_reduce_fusion = (f32[1024]{0:T(1024)S(1)}, f32[1024,1024]{1,0:T(8,128)}) fusion(f32[1024]{0:T(1024)S(1)} %convert_element_type.69, f32[1024,1024]{1,0:T(8,128)} %get-tuple-element.35.y_ref, f32[1024,1024]{1,0:T(8,128)} %get-tuple-element.36.gate_ref, bf16[1024,2048]{1,0:T(8,128)(2,1)} %all-gather.5.cloned.1.call-done, bf16[2048,1024]{1,0:T(8,128)(2,1)} %param.33), kind=kOutput, calls=%fused_computation.9 | convolution fusion | flops 4303354880 | bytes 20979712 | tf_op jit(solution)/shard_map/dot_general | solution.py:18
  218.7 41.0 %all-reduce.5 = (f32[1024,1]{1,0:T(8,128)S(1)}, f32[1024,1]{1,0:T(8,128)S(1)}) all-reduce(f32[1024,1]{1,0:T(8,128)S(1)} %copy-done.11, f32[1024,1]{1,0:T(8,128)S(1)} %copy.53), channel_id=1, replica_groups=mesh['dp'=8,'tensor'=4] {'tensor'}, use_global_device_ids=true, to_apply=%region_1.2 | all-reduce | flops 2048 | bytes 16384 | tf_op jit(solution)/shard_map/psum | solution.py:563
  259.7 1.1 fusion.8
  260.9 11.9 %convolution_convert_fusion.3 = bf16[1024,2048]{1,0:T(8,128)(2,1)} fusion(bf16[2048,1024]{1,0:T(8,128)(2,1)} %param.33, f32[1024]{0:T(1024)S(1)} %convert_element_type.69, f32[1024]{0:T(1024)S(1)} %get-tuple-element.89, f32[1024,1024]{1,0:T(8,128)} %get-tuple-element.35.y_ref, f32[1024,1024]{1,0:T(8,128)} %get-tuple-element.36.gate_ref), kind=kOutput, calls=%fused_computation.15 | convolution fusion | flops 4305453056 | bytes 16785408 | tf_op jit(solution)/shard_map/dot_general | solution.py:22
  272.8 58.3 %mixer_backward.1 = (bf16[1024,1024]{1,0:T(8,128)(2,1)}, bf16[1024,1024]{1,0:T(8,128)(2,1)}, bf16[1024,256]{1,0:T(8,128)(2,1)}, bf16[1024,128]{1,0:T(8,128)(2,1)...) custom-call(s32[1,3]{1,0:T(1,128)} %lengths_ref.3, ...), custom_call_target="tpu_custom_call" | custom-call | tf_op jit(solution)/shard_map/mixer_backward/pallas_call | solution.py:467
  331.2 2.3 fusion.11
  333.5 0.7 copy-done.24
  334.2 6.7 fusion.25
  340.9 6.7 fusion.24
  347.6 9.2 %add_convert_fusion = bf16[1024,2048]{1,0:T(8,128)(2,1)} fusion(f32[1024,2048]{1,0:T(8,128)S(1)} %fusion.11, f32[1024,2048]{1,0:T(8,128)} %fusion.24, f32[1024,2048]{1,0:T(8,128)} %fusion.25, bf16[1024,256]{1,0:T(8,128)(2,1)S(1)} %copy-done.9, bf16[2048,256]{1,0:T(8,128)(2,1)S(1)} %copy-done.7), kind=kOutput, calls=%fused_computation.8 | convolution fusion | flops 1082130432 | bytes 30932992 | tf_op jit(solution)/shard_map/dot_general | solution.py:22
  357.6 11.9 %convolution_convert_fusion = bf16[2048,1024]{1,0:T(8,128)(2,1)} fusion(bf16[1024,2048]{1,0:T(8,128)(2,1)} %all-gather.5.cloned.1.call-done, f32[1024]{0:T(1024)S(1)} %copy-done.16, f32[1024]{0:T(1024)S(1)} %get-tuple-element.89, f32[1024,1024]{1,0:T(8,128)} %get-tuple-element.35.y_ref, f32[1024,1024]{1,0:T(8,128)} %get-tuple-element.36.gate_ref), kind=kOutput, calls=%fused_computation.12 | convolution fusion | flops 4305453056 | bytes 16785408 | tf_op jit(solution)/shard_map/dot_general | solution.py:499
  369.5 9.4 %convolution_convert_fusion.2 = bf16[2048,1024]{1,0:T(8,128)(2,1)} fusion(bf16[1024,2048]{1,0:T(8,128)(2,1)} %get-tuple-element.50, bf16[1024,1024]{1,0:T(8,128)(2,1)} %get-tuple-element.45), kind=kOutput, calls=%fused_computation.14 | convolution fusion | flops 4297064448 | bytes 10485760 | tf_op jit(solution)/shard_map/dot_general | solution.py:499
  379.2 9.4 %convolution_convert_fusion.1 = bf16[2048,1024]{1,0:T(8,128)(2,1)} fusion(bf16[1024,2048]{1,0:T(8,128)(2,1)} %get-tuple-element.50, bf16[1024,1024]{1,0:T(8,128)(2,1)} %get-tuple-element.46), kind=kOutput, calls=%fused_computation.13 | convolution fusion | flops 4297064448 | bytes 10485760 | tf_op jit(solution)/shard_map/dot_general | solution.py:499
  388.9 0.7 copy-done.8
  389.6 3.5 fusion.9
  393.2 5.0 fusion.26
  398.5 45.5 %all-reduce.4 = (f32[1024,1]{1,0:T(8,128)S(1)}, f32[4,256]{1,0:T(4,128)S(1)}, f32[256]{0:T(256)S(1)}) all-reduce(f32[1024,1]{1,0:T(8,128)} %get-tuple-element.49, f32[4,256]{1,0:T(4,128)S(1)} %pad_maximum_fusion.1, f32[256]{0:T(256)S(1)} %get-tuple-element.61), channel_id=1, replica_groups=mesh['dp'=8,'tensor'=4] {'tensor'}, use_global_device_ids=true, to_apply=%region_8.9 | all-reduce | flops 2304 | bytes 18432 | tf_op jit(solution)/shard_map/psum | solution.py:577
  444.2 7.2 reduce-scatter.10.cloned.1.call-done
  451.5 3.6 fusion.6
  455.0 3.2 gather_fusion.6
  458.2 4.4 all-to-all-start.3
  462.6 2.0 gather_fusion.2
  464.6 33.7 %all-to-all-done.3 = bf16[8,256,512]{2,1,0:T(8,128)(2,1)} async-done(((bf16[8,256,512]{2,1,0:T(8,128)(2,1)}), bf16[8,256,512]{2,1,0:T(8,128)(2,1)}, u32[]{:S(2)}, u32[]{:S(2)}) %all-to-all-start.3) | async-done | bytes 2097184 | tf_op jit(solution)/shard_map/all_to_all | solution.py:541
  498.4 3.6 all-to-all-start.1
  502.6 23.3 %reduce-scatter.20.cloned.1.call-done = bf16[256,1024]{1,0:T(8,128)(2,1)} async-done(((bf16[2048,1024]{1,0:T(8,128)(2,1)}), bf16[256,1024]{1,0:T(8,128)(2,1)}) %reduce-scatter.20.cloned.1.call-update) | async-done | bytes 524304 | tf_op jit(solution)/shard_map/reduce_scatter | solution.py:596
  525.9 2.1 convert_element_type.83
  528.0 51.9 %reduce-scatter.12.cloned.1.call-done = bf16[256,1024]{1,0:T(8,128)(2,1)} async-done(((bf16[2048,1024]{1,0:T(8,128)(2,1)}), bf16[256,1024]{1,0:T(8,128)(2,1)}) %reduce-scatter.12.cloned.1.call-update) | async-done | bytes 524304 | tf_op jit(solution)/shard_map/reduce_scatter | solution.py:596
  579.9 2.1 convert_element_type.79
  582.1 52.6 %reduce-scatter.14.cloned.1.call-done = bf16[256,1024]{1,0:T(8,128)(2,1)} async-done(((bf16[2048,1024]{1,0:T(8,128)(2,1)}), bf16[256,1024]{1,0:T(8,128)(2,1)}) %reduce-scatter.14.cloned.1.call-update) | async-done | bytes 524304 | tf_op jit(solution)/shard_map/reduce_scatter | solution.py:596
  634.6 2.1 convert_element_type.81
  636.7 24.1 %all-reduce.3 = (f32[512]{0:T(512)}, f32[4,1024]{1,0:T(4,128)}, f32[1024]{0:T(1024)}, f32[4,256]{1,0:T(4,128)}, f32[256]{0:T(256)}, /*index=5*/f32[16]{0:T(128)}, f32[16]{0:T(128)}, f32[16]{0:T(128)}, f32[1024]{0:T(1024)}) all-reduce(f32[512]{0:T(512)S(1)} %get-tuple-element.85, ...), channel_id=1, replica_groups=mesh['dp'=8,'tensor'=4] {'dp'}, use_global_device_ids=true, to_apply=%region_10.11 | all-reduce | flops 7984 | bytes 63872 | tf_op jit(solution)/shard_map/psum | solution.py:604
  660.9 3.2 gather_fusion.7
  664.0 1.6 gather_fusion.3
  665.6 6.2 reduce-scatter.18.cloned.1.call-done
  671.9 141.3 %reduce-scatter.16.cloned.1.call-done = f32[64,256]{1,0:T(8,128)} async-done(((f32[2048,256]{1,0:T(8,128)}), f32[64,256]{1,0:T(8,128)}) %reduce-scatter.16.cloned.1.call-update) | async-done | bytes 65552 | tf_op jit(solution)/shard_map/reduce_scatter | solution.py:600
  (112 shorter events, 7.8 us)
Async XLA Ops:
  7.2 1.2 copy-start
  10.5 33.6 %copy-start.6 = (bf16[1024,512]{1,0:T(8,128)(2,1)S(1)}, bf16[1024,512]{1,0:T(8,128)(2,1)}, u32[]{:S(2)}) copy-start(bf16[1024,512]{1,0:T(8,128)(2,1)} %param.19) | copy-start | bytes 3145732
  10.5 31.9 %all-to-all-start = ((bf16[8,256,512]{2,1,0:T(8,128)(2,1)}), bf16[8,256,512]{2,1,0:T(8,128)(2,1)S(1)}, u32[]{:S(2)}, u32[]{:S(2)}) async-start(bf16[8,256,512]{2,1,0:T(8,128)(2,1)} %gather_fusion), calls=%async_computation | async-start | bytes 4194304 | tf_op jit(solution)/shard_map/all_to_all | solution.py:541
  15.8 108.6 %all-gather.3.cloned.1.call-start = ((), (), s32[]{:S(2)}) async-start(), calls=%async_computation.11 | async-start | bytes 5242880 | tf_op jit(solution)/shard_map/all_gather | solution.py:546
  44.0 161.8 %all-gather.5.cloned.1.call-start = ((), (), s32[]{:S(2)}) async-start(), calls=%async_computation.13 | async-start | bytes 5242880 | tf_op jit(solution)/shard_map/all_gather | solution.py:547
  44.8 33.3 %copy-start.26 = (f32[16]{0:T(128)S(1)}, f32[16]{0:T(128)}, u32[]{:S(2)}) copy-start(f32[16]{0:T(128)} %param.29) | copy-start | bytes 196
  44.8 33.8 %copy-start.27 = (f32[16]{0:T(128)S(1)}, f32[16]{0:T(128)}, u32[]{:S(2)}) copy-start(f32[16]{0:T(128)} %param.30) | copy-start | bytes 196
  44.8 34.3 %copy-start.28 = (bf16[256]{0:T(256)(128)(2,1)S(1)}, bf16[256]{0:T(256)(128)(2,1)}, u32[]{:S(2)}) copy-start(bf16[256]{0:T(256)(128)(2,1)} %param.28) | copy-start | bytes 1540
  44.8 34.9 %copy-start.20 = (bf16[1024]{0:T(1024)(128)(2,1)S(1)}, bf16[1024]{0:T(1024)(128)(2,1)}, u32[]{:S(2)}) copy-start(bf16[1024]{0:T(1024)(128)(2,1)} %param.32) | copy-start | bytes 6148
  44.8 34.8 %copy-start.21 = (bf16[4,256]{1,0:T(4,128)(2,1)S(1)}, bf16[4,256]{1,0:T(4,128)(2,1)}, u32[]{:S(2)}) copy-start(bf16[4,256]{1,0:T(4,128)(2,1)} %param.27) | copy-start | bytes 6148
  44.8 35.4 %copy-start.22 = (bf16[1024]{0:T(1024)(128)(2,1)S(1)}, bf16[1024]{0:T(1024)(128)(2,1)}, u32[]{:S(2)}) copy-start(bf16[1024]{0:T(1024)(128)(2,1)} %param.26) | copy-start | bytes 6148
  44.8 36.0 %copy-start.23 = (f32[16]{0:T(128)S(1)}, f32[16]{0:T(128)}, u32[]{:S(2)}) copy-start(f32[16]{0:T(128)} %param.31) | copy-start | bytes 196
  44.9 36.8 %copy-start.17 = (bf16[2048]{0:T(1024)(128)(2,1)S(1)}, bf16[2048]{0:T(1024)(128)(2,1)}, u32[]{:S(2)}) copy-start(bf16[2048]{0:T(1024)(128)(2,1)} %param.20) | copy-start | bytes 12292
  44.9 37.4 %copy-start.18 = (bf16[4,1024]{1,0:T(4,128)(2,1)S(1)}, bf16[4,1024]{1,0:T(4,128)(2,1)}, u32[]{:S(2)}) copy-start(bf16[4,1024]{1,0:T(4,128)(2,1)} %param.25) | copy-start | bytes 24580
  44.9 38.0 %copy-start.12 = (bf16[2048,16]{0,1:T(8,128)(2,1)S(1)}, bf16[2048,16]{0,1:T(8,128)(2,1)}, u32[]{:S(2)}) copy-start(bf16[2048,16]{0,1:T(8,128)(2,1)} %param.24) | copy-start | bytes 196612
  78.0 366.2 %reduce-scatter.8.cloned.1.call-start = ((), (), s32[]{:S(2)}) async-start(), calls=%async_computation.12 | async-start | bytes 5242880 | tf_op jit(solution)/shard_map/reduce_scatter | solution.py:568
  79.7 181.2 %copy-start.15 = (f32[1024]{0:T(1024)}, f32[1024]{0:T(1024)S(1)}, u32[]{:S(2)}) copy-start(f32[1024]{0:T(1024)S(1)} %convert_element_type.69) | copy-start | bytes 12292
  205.8 12.9 %copy-start.11 = (f32[1024,1]{1,0:T(8,128)S(1)}, f32[1024,1]{1,0:T(8,128)}, u32[]{:S(2)}) copy-start(f32[1024,1]{1,0:T(8,128)} %get-tuple-element.37) | copy-start | bytes 12292
  272.8 178.7 %reduce-scatter.10.cloned.1.call-start = ((), (), s32[]{:S(2)}) async-start(), calls=%async_computation.14 | async-start | bytes 5242880 | tf_op jit(solution)/shard_map/reduce_scatter | solution.py:582
  331.1 2.4 copy-start.4
  331.1 3.0 copy-start.24
  334.2 6.7 copy-start.5
  334.2 6.7 copy-start.25
  340.9 6.7 copy-start.7
  340.9 6.7 copy-start.9
  356.9 0.7 copy-start.16
  356.9 169.0 %reduce-scatter.20.cloned.1.call-start = ((), (), s32[]{:S(2)}) async-start(), calls=%async_computation.19 | async-start | bytes 4718592 | tf_op jit(solution)/shard_map/reduce_scatter | solution.py:596
  369.5 210.5 %reduce-scatter.12.cloned.1.call-start = ((), (), s32[]{:S(2)}) async-start(), calls=%async_computation.15 | async-start | bytes 4718592 | tf_op jit(solution)/shard_map/reduce_scatter | solution.py:596
  378.9 255.7 %reduce-scatter.14.cloned.1.call-start = ((), (), s32[]{:S(2)}) async-start(), calls=%async_computation.16 | async-start | bytes 4718592 | tf_op jit(solution)/shard_map/reduce_scatter | solution.py:596
  388.6 0.9 copy-start.8
  388.6 283.2 %reduce-scatter.18.cloned.1.call-start = ((), (), s32[]{:S(2)}) async-start(), calls=%async_computation.18 | async-start | bytes 147456 | tf_op jit(solution)/shard_map/reduce_scatter | solution.py:596
  393.1 5.1 copy-start.10
  393.1 5.3 copy-start.14
  393.1 58.3 %copy-start.2 = (bf16[4,256,512]{2,1,0:T(8,128)(2,1)S(1)}, bf16[4,256,512]{2,1,0:T(8,128)(2,1)}, u32[]{:S(2)}) copy-start(bf16[4,256,512]{2,1,0:T(8,128)(2,1)} %gather_fusion.1) | copy-start | bytes 3145732
  393.1 58.3 %copy-start.3 = (bf16[4,256,512]{2,1,0:T(8,128)(2,1)S(1)}, bf16[4,256,512]{2,1,0:T(8,128)(2,1)}, u32[]{:S(2)}) copy-start(bf16[4,256,512]{2,1,0:T(8,128)(2,1)} %gather_fusion.5) | copy-start | bytes 3145732
  393.2 420.0 %reduce-scatter.16.cloned.1.call-start = ((), (), s32[]{:S(2)}) async-start(), calls=%async_computation.17 | async-start | bytes 2162688 | tf_op jit(solution)/shard_map/reduce_scatter | solution.py:600
  458.2 40.2 %all-to-all-start.3 = ((bf16[8,256,512]{2,1,0:T(8,128)(2,1)}), bf16[8,256,512]{2,1,0:T(8,128)(2,1)}, u32[]{:S(2)}, u32[]{:S(2)}) async-start(bf16[8,256,512]{2,1,0:T(8,128)(2,1)} %gather_fusion.6), calls=%async_computation.5 | async-start | bytes 4194304 | tf_op jit(solution)/shard_map/all_to_all | solution.py:541
  462.6 39.7 %copy-start.13 = (f32[56,1024]{1,0:T(8,128)S(1)}, f32[56,1024]{1,0:T(8,128)}, u32[]{:S(2)}) copy-start(f32[56,1024]{1,0:T(8,128)} %get-tuple-element.51) | copy-start | bytes 688132
  462.6 39.9 %copy-start.19 = (f32[16,128]{1,0:T(8,128)S(1)}, f32[16,128]{1,0:T(8,128)}, u32[]{:S(2)}) copy-start(f32[16,128]{1,0:T(8,128)} %get-tuple-element.53) | copy-start | bytes 24580
  498.4 165.7 %all-to-all-start.1 = ((bf16[8,256,512]{2,1,0:T(8,128)(2,1)}), bf16[8,256,512]{2,1,0:T(8,128)(2,1)S(1)}, u32[]{:S(2)}, u32[]{:S(2)}) async-start(bf16[8,256,512]{2,1,0:T(8,128)(2,1)} %gather_fusion.2), calls=%async_computation.2 | async-start | bytes 4194304 | tf_op jit(solution)/shard_map/all_to_all | solution.py:541
  502.5 310.6 %copy-start.1 = (bf16[1024,512]{1,0:T(8,128)(2,1)S(1)}, bf16[1024,512]{1,0:T(8,128)(2,1)}, u32[]{:S(2)}) copy-start(bf16[1024,512]{1,0:T(8,128)(2,1)} %param.18) | copy-start | bytes 3145732
Sparse Core Ops, SparseCore 0:
  44.1 80.1 all-gather.2
  126.5 79.2 all-gather.4
  272.9 77.0 reduce-scatter.7
  357.0 94.3 reduce-scatter.9
  454.7 71.1 reduce-scatter.19
  529.5 50.4 reduce-scatter.11
  583.3 51.2 reduce-scatter.13
  638.5 33.3 reduce-scatter.17
  674.7 138.4 reduce-scatter.15

commit v2 on v1

v2 whole, which is shorter than its diff:
```python
import jax
import jax.numpy as jnp
from jax import lax
from jax.experimental import pallas as pl
from jax.experimental.pallas import tpu as pltpu
from jax.sharding import PartitionSpec as P

f32 = jnp.float32
bf16 = jnp.bfloat16
Q = 256
LANES = 128
HEAD_DIM = 64
AHEAD = 2
IN_FLIGHT = 3
HEAD_VMEM = 64 << 20
highest = lax.Precision.HIGHEST
epsilon = 1e-05


def dot_nn(a, b, precision=None):
    return lax.dot_general(a, b, (((1,), (0,)), ((), ())), precision=precision, preferred_element_type=f32)


def dot_nt(a, b, precision=None):
    return lax.dot_general(a, b, (((1,), (1,)), ((), ())), precision=precision, preferred_element_type=f32)


def halves(values):
    high = values.astype(bf16)
    return jnp.concatenate([high, (values - high.astype(f32)).astype(bf16)], axis=1)


def dot_halves(a, values):
    both = dot_nn(a, halves(values))
    return both[:, :LANES] + both[:, LANES:]


def sigmoid(values):
    return 0.5 * jnp.tanh(0.5 * values) + 0.5


def fold_rows(values):
    return jnp.sum(values.reshape(-1, 8, values.shape[-1]), axis=0)


def segment_at(position, lengths_ref):
    total = lengths_ref[0, 0]
    seg = (position >= total).astype(jnp.int32)
    for index in range(1, lengths_ref.shape[1]):
        total = total + lengths_ref[0, index]
        seg = seg + (position >= total).astype(jnp.int32)
    return seg


def tap_mask(start, shift, rows, lengths_ref):
    position = start + lax.broadcasted_iota(jnp.int32, (rows, LANES), 0)
    same = (segment_at(position, lengths_ref) == segment_at(position - shift, lengths_ref)) & (position >= shift)
    return same.astype(f32)


def triangle(start, lengths_ref, transposed):
    first = lax.broadcasted_iota(jnp.int32, (Q, Q), 0)
    second = lax.broadcasted_iota(jnp.int32, (Q, Q), 1)
    same = segment_at(start + first, lengths_ref) == segment_at(start + second, lengths_ref)
    order = (second >= first) if transposed else (first >= second)
    return same & order


def head_columns(cum, step, cum_cols, step_cols):
    lane = lax.broadcasted_iota(jnp.int32, (Q, LANES), 1)
    for head in range(cum_cols.shape[0]):
        cum_cols[head] = jnp.broadcast_to(cum[:, head : head + 1], (Q, LANES))
    for pair in range(step_cols.shape[0]):
        even = jnp.broadcast_to(step[:, 2 * pair : 2 * pair + 1], (Q, LANES))
        odd = jnp.broadcast_to(step[:, 2 * pair + 1 : 2 * pair + 2], (Q, LANES))
        step_cols[pair] = jnp.where(lane < HEAD_DIM, even, odd)


def boundary(start, lengths_ref):
    position = start + lax.broadcasted_iota(jnp.int32, (Q, LANES), 0)
    seg = segment_at(position, lengths_ref)
    last = segment_at(jnp.full((1, LANES), start + Q - 1, jnp.int32), lengths_ref)
    before = segment_at(jnp.full((1, LANES), start - 1, jnp.int32), lengths_ref)
    before = jnp.where(start > 0, before, -1)
    return (seg == last), (seg == before), (last == before)


def softplus(values):
    return jnp.maximum(values, 0.0) + jnp.log1p(jnp.exp(-jnp.abs(values)))


def causal_taps(ext_ref, taps, bias, masks, columns):
    total = taps[3:4] * ext_ref[pl.ds(8, Q), columns]
    for shift in range(1, 4):
        total = total + taps[3 - shift : 4 - shift] * (ext_ref[pl.ds(8 - shift, Q), columns] * masks[shift - 1])
    return total + bias


def chunk_scalars(start, step_in, rate, lengths_ref, causal):
    step = softplus(step_in)
    log_decay = -step * jnp.exp(rate)
    cum = dot_nn(causal, log_decay, highest)
    return step, log_decay, cum


MESH = pl.DeviceIdType.MESH


def greet(groups, slots):
    group, slot = lax.axis_index("dp"), lax.axis_index("tensor")
    barrier = pltpu.get_barrier_semaphore()

    def along_dp(step, nothing):
        pl.semaphore_signal(barrier, inc=1, device_id=(lax.rem(group + step, groups), slot), device_id_type=MESH)
        return nothing

    lax.fori_loop(1, groups, along_dp, 0)
    for step in range(1, slots):
        pl.semaphore_signal(barrier, inc=1, device_id=(group, lax.rem(slot + step, slots)), device_id_type=MESH)
    pl.semaphore_wait(barrier, groups - 1 + slots - 1)


def head_kernel(
    send_run_ref, arrive_from_ref, lengths_ref, tokens, cotangent, wg_hbm, wv_hbm, ws_hbm, wt_hbm, wo_hbm,
    gain_ref, ggain_ref, tapv_ref, biasv_ref, taps_ref, biass_ref, stepb_ref, rate_ref, skip_ref,
    fulltok, fullcot, normed_out, dgate_out, dvalue_out, scaled_out, back_out, keep, out_part,
    dstate_ref, dstep_ref, inv_ref, dot_ref, sumv_ref, sums_ref, sumh_ref,
    wg, wv, ws, wt, wo, ptok, pcot, slots_buf, arr_tok, arr_cot, xbuf, nbuf, kbuf, gate_all, y_all,
    sraw_all, spre_all, stepin_all, states, d_carry, vext, dvext, sext, cum_cols, step_cols, cum_rows, neg_bias,
    scores, d_scores, d_entry, d_leave, acc_step, acc_cum, acc_dot, dsc, dgbuf, dvbuf, scbuf, bbuf, zbuf,
    sq_rows, ex_send, ex_recv, cols, masks, gathers,
    w_sem, in_sem, ts, tr, cs, cr, ags, agr, own_sem, x_sem, n_sem, keep_sem, o_sem, es, er,
):
    groups, slots = lax.axis_size("dp"), lax.axis_size("tensor")
    group, slot = lax.axis_index("dp"), lax.axis_index("tensor")
    runs, run, width = ptok.shape
    chunks = runs * run // Q
    per_chunk = Q // run
    pairs = d_carry.shape[0]
    last = slots - 1
    model = width * slots
    inner_total = wg.shape[1] * slots
    lane = lax.broadcasted_iota(jnp.int32, (Q, LANES), 1)
    first_half = lane < HEAD_DIM

    greet(groups, slots)
    weights = ((wg_hbm, wg), (wv_hbm, wv), (ws_hbm, ws), (wt_hbm, wt), (wo_hbm, wo))

    def weight_load(which):
        return pltpu.make_async_copy(weights[which][0], weights[which][1], w_sem.at[which])

    tok_in = pltpu.make_async_copy(tokens, ptok, in_sem.at[0])
    cot_in = pltpu.make_async_copy(cotangent, pcot, in_sem.at[1])
    tok_in.start()
    cot_in.start()
    for which in range(5):
        weight_load(which).start()

    def row_send(arrive, send_sem, recv_sem, step):
        other = lax.rem(group + step, groups)
        return pltpu.make_async_remote_copy(
            src_ref=slots_buf.at[other], dst_ref=arrive.at[group], send_sem=send_sem.at[other],
            recv_sem=recv_sem.at[group], device_id=(other, slot), device_id_type=MESH,
        )

    def send_rows(source, arrive, send_sem, recv_sem):
        def one(step, nothing):
            other = lax.rem(group + step, groups)
            slots_buf[other] = source[send_run_ref[other]]
            row_send(arrive, send_sem, recv_sem, step).start()
            return nothing

        lax.fori_loop(1, groups, one, 0)
        arrive[group] = source[send_run_ref[group]]

    def take_rows(packed, arrive, send_sem, recv_sem):
        def one(step, nothing):
            source = lax.rem(group + groups - step, groups)
            pltpu.make_async_remote_copy(
                src_ref=arrive.at[source], dst_ref=arrive.at[source], send_sem=send_sem.at[source],
                recv_sem=recv_sem.at[source], device_id=(group, slot), device_id_type=MESH,
            ).wait_recv()
            row_send(arrive, send_sem, recv_sem, step).wait_send()
            return nothing

        lax.fori_loop(1, groups, one, 0)
        for index in range(runs):
            packed[index] = arrive[arrive_from_ref[index]]

    def rows_of(packed, chunk):
        return packed.at[pl.ds(chunk * per_chunk, per_chunk)]

    def gather_push(kind, source, target, chunk, number, shard, to):
        return pltpu.make_async_remote_copy(
            src_ref=source, dst_ref=target.at[chunk, shard], send_sem=ags.at[kind, chunk, number],
            recv_sem=agr.at[kind, chunk, shard], device_id=(group, to), device_id_type=MESH,
        )

    gather_to = ((1, 2), (0, 2, 3), (3, 1, 0), (2, 1))

    def gather_direct(kind, packed, target, chunk, me):
        return [
            gather_push(kind, rows_of(packed, chunk), target, chunk, number, me, to)
            for number, to in enumerate(gather_to[me])
        ]

    def gather_forward(kind, target, chunk, me):
        shard, to = (3, 0) if me == 1 else (0, 3)
        return gather_push(kind, target.at[chunk, shard], target, chunk, 3, shard, to)

    def own_copy(kind, packed, target, chunk):
        return pltpu.make_async_copy(rows_of(packed, chunk), target.at[chunk, slot], own_sem.at[kind, chunk])

    def gather_start(kind, packed, target, chunk):
        own_copy(kind, packed, target, chunk).start()
        for me in range(slots):
            @pl.when(slot == me)
            def _(me=me):
                for copy in gather_direct(kind, packed, target, chunk, me):
                    copy.start()

    def gather_wait(kind, packed, target, chunk, hook=None):
        for me in range(slots):
            @pl.when(slot == me)
            def _(me=me):
                order = (3, 0, 2) if me == 1 else (0, 3, 1) if me == 2 else (1, 2, 3 - me)
                for position, shard in enumerate(order):
                    pltpu.make_async_remote_copy(
                        src_ref=target.at[chunk, shard], dst_ref=target.at[chunk, shard],
                        send_sem=ags.at[kind, chunk, 0], recv_sem=agr.at[kind, chunk, shard],
                        device_id=(group, slot), device_id_type=MESH,
                    ).wait_recv()
                    if position == 0 and me in (1, 2):
                        gather_forward(kind, target, chunk, me).start()
                    if position == 0 and hook is not None:
                        hook()
        own_copy(kind, packed, target, chunk).wait()

    def gather_drain(kind, packed, target):
        for chunk in range(chunks):
            for me in range(slots):
                @pl.when(slot == me)
                def _(me=me):
                    for copy in gather_direct(kind, packed, target, chunk, me):
                        copy.wait_send()
                    if me in (1, 2):
                        gather_forward(kind, target, chunk, me).wait_send()

    def keep_store(chunk, which):
        source = vext.at[pl.ds(8, Q)] if which == 0 else kbuf.at[1]
        return pltpu.make_async_copy(source, keep.at[chunk, which], keep_sem.at[which])

    def keep_load(chunk):
        return pltpu.make_async_copy(keep.at[chunk], kbuf, keep_sem.at[2])

    def normed_store(chunk):
        return pltpu.make_async_copy(nbuf, normed_out.at[chunk], n_sem)

    stores = ((dgbuf, dgate_out), (dvbuf, dvalue_out), (scbuf, scaled_out), (bbuf, back_out), (zbuf, out_part))

    def store(which, chunk):
        return pltpu.make_async_copy(stores[which][0], stores[which][1].at[chunk], o_sem.at[which])

    def x_load(source, chunk):
        return pltpu.make_async_copy(source.at[chunk], xbuf, x_sem)

    def ones_rows(values):
        return dot_nt(jnp.ones((8, LANES), f32), values, highest)

    def prepare(chunk, transposed):
        start = chunk * Q
        can_see = triangle(start, lengths_ref, transposed)
        neg_bias[...] = jnp.where(can_see, 0.0, -1e30)
        row = lax.broadcasted_iota(jnp.int32, (Q, Q), 0)
        col = lax.broadcasted_iota(jnp.int32, (Q, Q), 1)
        step_in = stepin_all[chunk]
        step, log_decay, cum = chunk_scalars(start, step_in, rate_ref[...], lengths_ref, (row >= col).astype(f32))
        cum_rows[...] = cum.T
        head_columns(cum, step, cum_cols, step_cols)
        return log_decay

    tok_in.wait()
    send_rows(ptok, arr_tok, ts, tr)
    states[0] = jnp.zeros_like(states[0])
    vext[pl.ds(0, 8)] = jnp.zeros((8, vext.shape[1]), f32)
    sext[pl.ds(0, 8)] = jnp.zeros((8, sext.shape[1]), f32)
    d_carry[...] = jnp.zeros_like(d_carry)
    dvext[pl.ds(Q, 8)] = jnp.zeros((8, dvext.shape[1]), f32)
    sumv_ref[...] = jnp.zeros_like(sumv_ref)
    sums_ref[...] = jnp.zeros_like(sums_ref)
    sumh_ref[...] = jnp.zeros_like(sumh_ref)
    place = lax.broadcasted_iota(jnp.int32, (2 * LANES, LANES), 1)
    source = lax.broadcasted_iota(jnp.int32, (2 * LANES, LANES), 0)
    source = (lax.rem(source, LANES) >= HEAD_DIM).astype(jnp.int32)
    for pair in range(pairs):
        gathers[pair] = (place == source + 2 * pair).astype(bf16)
    take_rows(ptok, arr_tok, ts, tr)
    gather_start(0, ptok, fulltok, 0)
    cot_in.wait()
    send_rows(pcot, arr_cot, cs, cr)
    for which in range(5):
        weight_load(which).wait()

    def forward_chunk(chunk, nothing):
        start = chunk * Q
        def second():
            @pl.when(chunk == 0)
            def _():
                gather_start(0, ptok, fulltok, 1)

        gather_wait(0, ptok, fulltok, chunk, second)
        x_load(fulltok, chunk).start()

        @pl.when(chunk + AHEAD < chunks)
        def _():
            gather_start(0, ptok, fulltok, chunk + AHEAD)

        @pl.when(chunk + AHEAD == chunks)
        def _():
            take_rows(pcot, arr_cot, cs, cr)

        @pl.when(chunk + AHEAD >= chunks)
        def _():
            gather_start(1, pcot, fullcot, 2 * chunks - 1 - AHEAD - chunk)

        @pl.when(chunk > 0)
        def _():
            normed_store(chunk - 1).wait()
            keep_store(chunk - 1, 0).wait()
            keep_store(chunk - 1, 1).wait()
            vext[pl.ds(0, 8)] = vext[pl.ds(Q, 8)]
            sext[pl.ds(0, 8)] = sext[pl.ds(Q, 8)]

        x_load(fulltok, chunk).wait()
        squares = jnp.zeros((Q, 1), f32)
        for shard in range(slots):
            wide = xbuf[shard].reshape(Q, width).astype(f32)
            squares = squares + jnp.sum(wide * wide, axis=1, keepdims=True)
        inv = lax.rsqrt(squares * (1.0 / model) + epsilon)
        inv_ref[pl.ds(start, Q)] = inv
        for shard in range(slots):
            wide = xbuf[shard].reshape(Q, width).astype(f32)
            columns = slice(shard * width, (shard + 1) * width)
            nbuf[:, columns] = (wide * inv * gain_ref[:, columns]).astype(bf16)
        normed_store(chunk).start()
        gate_all[chunk] = dot_nn(nbuf[...], wg[...])
        vext[pl.ds(8, Q)] = dot_nn(nbuf[...], wv[...])
        sext[pl.ds(8, Q)] = dot_nn(nbuf[...], ws[...])
        stepin_all[chunk] = dot_nn(nbuf[...], wt[...]) + stepb_ref[...]
        keep_store(chunk, 0).start()
        sraw_all[chunk] = sext[pl.ds(8, Q)]
        prepare(chunk, False)
        for shift in range(1, 4):
            masks[shift - 1] = tap_mask(start, shift, Q, lengths_ref)

        for half in range(2):
            columns = slice(half * LANES, (half + 1) * LANES)
            spre_all[chunk, :, columns] = causal_taps(
                sext, taps_ref[:, columns], biass_ref[:, columns], masks, columns
            )
        spre = spre_all[chunk]
        state_conv = spre * sigmoid(spre)
        entry = state_conv[:, :LANES]
        leave = state_conv[:, LANES:]
        scores[...] = dot_nt(leave, entry, highest)
        entry_t = entry.T.astype(bf16)
        leave_low = leave.astype(bf16)
        with_last, with_before, through = boundary(start, lengths_ref)
        to_last = with_last.astype(f32)
        from_before = with_before.astype(f32)
        passes = through.astype(f32)
        acc_dot[...] = jnp.zeros_like(acc_dot)

        def one_pair(pair, nothing):
            columns = pl.ds(pl.multiple_of(pair * LANES, LANES), LANES)
            pre = causal_taps(vext, tapv_ref[:, columns], biasv_ref[:, columns], masks, columns)
            kbuf[1, :, columns] = pre
            x = pre * sigmoid(pre)
            weighted = x * step_cols[pair]
            both = halves(weighted)
            results = []
            for half in range(2):
                head = 2 * pair + half
                c_col = cum_cols[head]
                c_row = cum_rows[pl.ds(head, 1), :]
                top = scores[:LANES, :LANES] * jnp.exp(c_col[:LANES] - c_row[:, :LANES] + neg_bias[:LANES, :LANES])
                low_left = scores[LANES:, :LANES] * jnp.exp(c_col[LANES:] - c_row[:, :LANES] + neg_bias[LANES:, :LANES])
                low_right = scores[LANES:, LANES:] * jnp.exp(
                    c_col[LANES:] - c_row[:, LANES:] + neg_bias[LANES:, LANES:]
                )
                upper = dot_nn(top.astype(bf16), both[:LANES])
                lower = dot_nn(jnp.concatenate([low_left, low_right], axis=1).astype(bf16), both)
                out = jnp.concatenate([upper, lower], axis=0)
                results.append(out[:, :LANES] + out[:, LANES:])
            inside = jnp.where(first_half, results[0], results[1])
            cum_pair = jnp.where(first_half, cum_cols[2 * pair], cum_cols[2 * pair + 1])
            cum_last = cum_pair[Q - 1 :]
            held = states[chunk, pair]
            carried = dot_halves(leave_low, held) * (jnp.exp(cum_pair) * from_before)
            y = inside + carried + skip_ref[:, columns] * x
            y_all[chunk, :, columns] = y
            to_end = jnp.exp(cum_last - cum_pair) * to_last
            states[chunk + 1, pair] = held * (jnp.exp(cum_last) * passes) + dot_halves(entry_t, to_end * weighted)
            gate = gate_all[chunk, :, columns]
            gated = y * (gate * sigmoid(gate))
            acc_dot[...] += gated * gated
            return nothing

        lax.fori_loop(0, pairs, one_pair, 0)
        keep_store(chunk, 1).start()
        sq_rows[chunk] = ones_rows(acc_dot[...])

        return nothing

    lax.fori_loop(0, chunks, forward_chunk, 0)
    normed_store(chunks - 1).wait()
    keep_store(chunks - 1, 0).wait()
    keep_store(chunks - 1, 1).wait()
    dsext = sext
    dsext[pl.ds(Q, 8)] = jnp.zeros((8, dsext.shape[1]), f32)

    def send_sums(chunk, step):
        return pltpu.make_async_remote_copy(
            src_ref=ex_send.at[chunk], dst_ref=ex_recv.at[chunk, slots - step], send_sem=es.at[chunk, step],
            recv_sem=er.at[chunk, slots - step], device_id=(group, lax.rem(slot + step, slots)), device_id_type=MESH,
        )

    def backward_chunk(index, nothing):
        chunk = chunks - 1 - index
        start = chunk * Q
        keep_load(chunk).start()
        gather_wait(1, pcot, fullcot, chunk)
        x_load(fullcot, chunk).start()

        @pl.when(chunk >= AHEAD)
        def _():
            gather_start(1, pcot, fullcot, chunk - AHEAD)

        x_load(fullcot, chunk).wait()
        for half in range(2):
            columns = slice(half * (dsc.shape[1] // 2), (half + 1) * (dsc.shape[1] // 2))
            value = dot_nn(xbuf[0].reshape(Q, width), wo[pl.ds(0, width), columns])
            for shard in range(1, slots):
                value = value + dot_nn(xbuf[shard].reshape(Q, width), wo[pl.ds(shard * width, width), columns])
            dsc[:, columns] = value
        acc_dot[...] = jnp.zeros_like(acc_dot)

        def product(pair, nothing):
            columns = pl.ds(pl.multiple_of(pair * LANES, LANES), LANES)
            gate = gate_all[chunk, :, columns]
            gated = y_all[chunk, :, columns] * (gate * sigmoid(gate))
            acc_dot[...] += dsc[:, columns] * ggain_ref[:, columns] * gated
            return nothing

        lax.fori_loop(0, pairs, product, 0)
        ex_send[chunk, pl.ds(0, 8)] = sq_rows[chunk]
        ex_send[chunk, pl.ds(8, 8)] = ones_rows(acc_dot[...])
        for step in range(1, slots):
            send_sums(chunk, step).start()

        @pl.when(index > 0)
        def _():
            dvext[pl.ds(Q, 8)] = dvext[pl.ds(0, 8)]
            dsext[pl.ds(Q, 8)] = dsext[pl.ds(0, 8)]
            for which in range(5):
                store(which, chunk + 1).wait()

        def later_mask(shift):
            position = start + lax.broadcasted_iota(jnp.int32, (Q, LANES), 0)
            same = segment_at(position, lengths_ref) == segment_at(position + shift, lengths_ref)
            return (same & (position + shift < chunks * Q)).astype(f32)

        log_decay = prepare(chunk, True)
        for shift in range(1, 4):
            masks[shift - 1] = later_mask(shift)
        step_in = stepin_all[chunk]
        spre = spre_all[chunk]
        spre_sig = sigmoid(spre)
        state_conv = spre * spre_sig
        entry = state_conv[:, :LANES]
        leave = state_conv[:, LANES:]
        scores[...] = dot_nt(entry, leave, highest)
        entry_low = entry.astype(bf16)
        leave_t = leave.T.astype(bf16)
        with_last, with_before, through = boundary(start, lengths_ref)
        to_last = with_last.astype(f32)
        from_before = with_before.astype(f32)
        passes = through.astype(f32)
        row_lane = lax.broadcasted_iota(jnp.int32, (Q, LANES), 0)
        for ref in (d_scores, d_entry, d_leave, acc_step, acc_cum, acc_dot):
            ref[...] = jnp.zeros_like(ref)

        sums = ex_send[chunk]
        for step in range(1, slots):
            send_sums(chunk, step).wait()
        for step in range(1, slots):
            sums = sums + ex_recv[chunk, step]
        rms_row = lax.rsqrt(sums[0:1] * (1.0 / inner_total) + epsilon)
        coef_row = rms_row * rms_row * rms_row * sums[8:9] * (1.0 / inner_total)
        cols[0] = jnp.broadcast_to(rms_row, (LANES, Q)).T
        cols[1] = jnp.broadcast_to(coef_row, (LANES, Q)).T
        keep_load(chunk).wait()

        def one_pair(pair, nothing):
            columns = pl.ds(pl.multiple_of(pair * LANES, LANES), LANES)
            rms = cols[0]
            pre = kbuf[1, :, columns]
            pre_sig = sigmoid(pre)
            x = pre * pre_sig
            step_pair = step_cols[pair]
            weighted = x * step_pair
            gate = gate_all[chunk, :, columns]
            gate_sig = sigmoid(gate)
            gate_silu = gate * gate_sig
            y = y_all[chunk, :, columns]
            gated = y * gate_silu
            d_scaled = dsc[:, columns]
            ggain = ggain_ref[:, columns]
            normalized = gated * rms
            scbuf[:, columns] = (normalized * ggain).astype(bf16)
            d_gated = rms * (d_scaled * ggain) - gated * cols[1]
            sumv_ref[pl.ds(0, 8), columns] += fold_rows(d_scaled * normalized)
            d_gate = (d_gated * y * (gate_sig + gate_silu * (1.0 - gate_sig))).astype(bf16)
            dgbuf[:, columns] = d_gate
            acc_dot[...] += d_gate.astype(f32) * gate
            d_y = d_gated * gate_silu
            skip = skip_ref[:, columns]
            sumv_ref[pl.ds(8, 8), columns] += fold_rows(d_y * x)
            y_scan = y - skip * x

            d_y_t = d_y.T.astype(bf16)
            d_y_both = halves(d_y)
            weighted_low = weighted.astype(bf16)
            results = []
            for half in range(2):
                head = 2 * pair + half
                own = jnp.where(first_half if half == 0 else ~first_half, weighted_low, jnp.zeros_like(weighted_low))
                d_m_top = dot_nn(own[:LANES], d_y_t)
                d_m_low = dot_nn(own[LANES:], d_y_t[:, LANES:])
                c_col = cum_cols[head]
                c_row = cum_rows[pl.ds(head, 1), :]
                l_top = jnp.exp(c_row - jnp.concatenate([c_col[:LANES]] * 2, axis=1) + neg_bias[:LANES])
                l_low = jnp.exp(c_row[:, LANES:] - c_col[LANES:] + neg_bias[LANES:, LANES:])
                d_scores[:LANES] += d_m_top * l_top
                d_scores[LANES:, LANES:] += d_m_low * l_low
                m_top = (scores[:LANES] * l_top).astype(bf16)
                m_low = (scores[LANES:, LANES:] * l_low).astype(bf16)
                upper = dot_nn(m_top, d_y_both)
                lower = dot_nn(m_low, d_y_both[LANES:])
                out = jnp.concatenate([upper, lower], axis=0)
                results.append(out[:, :LANES] + out[:, LANES:])
            d_weighted = jnp.where(first_half, results[0], results[1])
            cum_pair = jnp.where(first_half, cum_cols[2 * pair], cum_cols[2 * pair + 1])
            cum_last = cum_pair[Q - 1 :]
            to_end = jnp.exp(cum_last - cum_pair) * to_last
            from_start = jnp.exp(cum_pair) * from_before
            d_state = d_carry[pair]
            held = states[chunk, pair]
            d_weighted = d_weighted + dot_halves(entry_low, d_state) * to_end
            d_entry[...] += dot_nt((to_end * weighted).astype(bf16), d_state.astype(bf16))
            moved = from_start * d_y
            d_leave[...] += dot_nt(moved.astype(bf16), held.astype(bf16))
            state_dot = jnp.sum(states[chunk + 1, pair] * d_state, axis=0, keepdims=True)
            d_carry[pair] = d_state * (jnp.exp(cum_last) * passes) + dot_halves(leave_t, moved)

            to_step = d_weighted * x
            to_cum = d_y * y_scan - to_step * step_pair + jnp.where(row_lane == Q - 1, state_dot, 0.0)
            acc_step[...] += dot_nn(halves(to_step), gathers[pair])
            acc_cum[...] += dot_nn(halves(to_cum), gathers[pair])

            d_x = d_weighted * step_pair + skip * d_y
            d_pre = d_x * (pre_sig + x * (1.0 - pre_sig))
            dvext[pl.ds(0, Q), columns] = d_pre
            sumv_ref[pl.ds(16, 8), columns] += fold_rows(d_pre)
            vraw = kbuf[0, :, columns]
            total = tapv_ref[3:4, columns] * d_pre
            sumv_ref[pl.ds(24, 8), columns] += fold_rows(vraw * d_pre)
            for shift in range(1, 4):
                moved_back = dvext[pl.ds(shift, Q), columns] * masks[shift - 1]
                total = total + tapv_ref[3 - shift : 4 - shift, columns] * moved_back
                sumv_ref[pl.ds(24 + 8 * shift, 8), columns] += fold_rows(vraw * moved_back)
            d_value = total.astype(bf16)
            dvbuf[:, columns] = d_value
            acc_dot[...] += d_value.astype(f32) * vraw
            return nothing

        lax.fori_loop(0, pairs, one_pair, 0)
        for which in range(3):
            store(which, chunk).start()

        can_see = (neg_bias[...] == 0.0).astype(f32)
        d_log = dot_nn(can_see, acc_cum[...], highest)
        rate = jnp.exp(rate_ref[...])
        d_step_in = (acc_step[...] - d_log * rate) * sigmoid(step_in)
        d_step = d_step_in.astype(bf16)
        dstep_ref[pl.ds(start, Q)] = d_step
        step_raw = step_in - stepb_ref[...]
        acc_dot[...] += jnp.where(lane < 2 * pairs, d_step.astype(f32) * step_raw, 0.0)
        sumh_ref[pl.ds(0, 8)] += fold_rows(d_step_in)
        sumh_ref[pl.ds(8, 8)] += fold_rows(d_log * log_decay)

        d_scores_now = d_scores[...]
        d_b = d_entry[...] + dot_halves(d_scores_now.astype(bf16), leave)
        d_c = d_leave[...] + dot_halves(d_scores_now.T.astype(bf16), entry)
        for half, grad in enumerate((d_b, d_c)):
            columns = slice(half * LANES, (half + 1) * LANES)
            part = spre_sig[:, columns]
            d_pre = grad * (part + state_conv[:, columns] * (1.0 - part))
            dsext[pl.ds(0, Q), columns] = d_pre
            sums_ref[pl.ds(0, 8), columns] += fold_rows(d_pre)
            sraw = sraw_all[chunk, :, columns]
            total = taps_ref[3:4, columns] * d_pre
            sums_ref[pl.ds(8, 8), columns] += fold_rows(sraw * d_pre)
            for shift in range(1, 4):
                moved_back = dsext[pl.ds(shift, Q), columns] * masks[shift - 1]
                total = total + taps_ref[3 - shift : 4 - shift, columns] * moved_back
                sums_ref[pl.ds(8 + 8 * shift, 8), columns] += fold_rows(sraw * moved_back)
            d_state_raw = total.astype(bf16)
            dstate_ref[pl.ds(start, Q), columns] = d_state_raw
            acc_dot[...] += d_state_raw.astype(f32) * sraw
        dot_ref[chunk] = ones_rows(acc_dot[...])

        for shard in range(slots):
            here = pl.ds(shard * width, width)
            part = dot_nt(dgbuf[...], wg[here]) + dot_nt(dvbuf[...], wv[here])
            part = part + dot_nt(dstate_ref[pl.ds(start, Q)], ws[here]) + dot_nt(d_step, wt[here])
            bbuf[:, shard * width : (shard + 1) * width] = part.astype(bf16)
        store(3, chunk).start()
        for shard in range(slots):
            part = dot_nt(scbuf[...], wo[pl.ds(shard * width, width)])
            zbuf[:, shard * width : (shard + 1) * width] = part.astype(bf16)
        store(4, chunk).start()
        return nothing

    lax.fori_loop(0, chunks, backward_chunk, 0)
    for which in range(5):
        store(which, 0).wait()
    gather_drain(0, ptok, fulltok)
    gather_drain(1, pcot, fullcot)


def head(send_run, arrive_from, lengths, tokens, cotangent, wg, wv, ws, wt, wo, small):
    groups, slots = lax.axis_size("dp"), lax.axis_size("tensor")
    runs, run, width = tokens.shape
    rows = runs * run
    chunks, per_chunk = rows // Q, Q // run
    model, inner = wg.shape
    pairs = inner // LANES
    vmem, anywhere, smem = (pl.BlockSpec(memory_space=s) for s in (pltpu.VMEM, pl.ANY, pltpu.SMEM))
    dma = pltpu.SemaphoreType.DMA
    shape = jax.ShapeDtypeStruct
    return pl.pallas_call(
        head_kernel,
        out_shape=[
            shape((chunks, slots, per_chunk, run, width), bf16),
            shape((chunks, slots, per_chunk, run, width), bf16),
            shape((chunks, Q, model), bf16),
            shape((chunks, Q, inner), bf16),
            shape((chunks, Q, inner), bf16),
            shape((chunks, Q, inner), bf16),
            shape((chunks, Q, model), bf16),
            shape((chunks, 2, Q, inner), f32),
            shape((chunks, Q, model), bf16),
            shape((rows, 2 * LANES), bf16),
            shape((rows, LANES), bf16),
            shape((rows, 1), f32),
            shape((chunks, 8, Q), f32),
            shape((56, inner), f32),
            shape((40, 2 * LANES), f32),
            shape((16, LANES), f32),
        ],
        in_specs=[smem] * 3 + [anywhere] * 7 + [vmem] * len(small),
        out_specs=[anywhere] * 9 + [vmem] * 7,
        scratch_shapes=[
            pltpu.VMEM(wg.shape, bf16), pltpu.VMEM(wv.shape, bf16), pltpu.VMEM(ws.shape, bf16),
            pltpu.VMEM(wt.shape, bf16), pltpu.VMEM(wo.shape, bf16),
            pltpu.VMEM((runs, run, width), bf16),
            pltpu.VMEM((runs, run, width), bf16),
            pltpu.VMEM((groups, run, width), bf16),
            pltpu.VMEM((groups, run, width), bf16),
            pltpu.VMEM((groups, run, width), bf16),
            pltpu.VMEM((slots, per_chunk, run, width), bf16),
            pltpu.VMEM((Q, model), bf16),
            pltpu.VMEM((2, Q, inner), f32),
            pltpu.VMEM((chunks, Q, inner), f32),
            pltpu.VMEM((chunks, Q, inner), f32),
            pltpu.VMEM((chunks, Q, 2 * LANES), f32),
            pltpu.VMEM((chunks, Q, 2 * LANES), f32),
            pltpu.VMEM((chunks, Q, LANES), f32),
            pltpu.VMEM((chunks + 1, pairs, LANES, LANES), f32),
            pltpu.VMEM((pairs, LANES, LANES), f32),
            pltpu.VMEM((Q + 8, inner), f32),
            pltpu.VMEM((Q + 8, inner), f32),
            pltpu.VMEM((Q + 8, 2 * LANES), f32),
            pltpu.VMEM((2 * pairs, Q, LANES), f32),
            pltpu.VMEM((pairs, Q, LANES), f32),
            pltpu.VMEM((LANES, Q), f32),
            pltpu.VMEM((Q, Q), f32),
            pltpu.VMEM((Q, Q), f32),
            pltpu.VMEM((Q, Q), f32),
            pltpu.VMEM((Q, LANES), f32),
            pltpu.VMEM((Q, LANES), f32),
            pltpu.VMEM((Q, LANES), f32),
            pltpu.VMEM((Q, LANES), f32),
            pltpu.VMEM((Q, LANES), f32),
            pltpu.VMEM((Q, inner), f32),
            pltpu.VMEM((Q, inner), bf16),
            pltpu.VMEM((Q, inner), bf16),
            pltpu.VMEM((Q, inner), bf16),
            pltpu.VMEM((Q, model), bf16),
            pltpu.VMEM((Q, model), bf16),
            pltpu.VMEM((chunks, 8, Q), f32),
            pltpu.VMEM((chunks, 16, Q), f32),
            pltpu.VMEM((chunks, slots, 16, Q), f32),
            pltpu.VMEM((2, Q, LANES), f32),
            pltpu.VMEM((3, Q, LANES), f32),
            pltpu.VMEM((pairs, 2 * LANES, LANES), bf16),
            dma((5,)), dma((2,)), dma((groups,)), dma((groups,)), dma((groups,)), dma((groups,)),
            dma((2, chunks, 4)), dma((2, chunks, slots)), dma((2, chunks)), dma, dma, dma((3,)), dma((5,)),
            dma((chunks, slots)), dma((chunks, slots)),
        ],
        compiler_params=pltpu.CompilerParams(collective_id=2, has_side_effects=True, vmem_limit_bytes=HEAD_VMEM),
        name="head",
    )(send_run, arrive_from, lengths, tokens, cotangent, wg, wv, ws, wt, wo, *small)


def tail_kernel(
    back_run_ref, return_from_ref, out_part, back_part, normed, tokens, cotangent, scaled, d_gate, d_value,
    row_dot_ref, inv_ref, gain_ref, small_ref, small_z_ref,
    layer_ref, tgrad_ref, small_out, ngain_out, share0, share1, share2,
    z_recv, z_comb, z_own, z_mix, ptok, pcot, rd_recv, rd_col, row_buf, slots_buf, arrive, left, right, full,
    core_recv, chip_recv, total, sz_recv, small_all, small_recv, ngain_all, ngain_recv,
    load_sem, mix_sem, left_sem, right_sem, zs, zr, zc, rds, rdr, szs, szr, sms, smr, ngs, ngr, rs, rr, cs, cr, hs, hr,
):
    groups, slots = lax.axis_size("dp"), lax.axis_size("tensor")
    group, slot = lax.axis_index("dp"), lax.axis_index("tensor")
    jobs = z_recv.shape[0]
    pieces = jobs // 2
    runs, run, width = layer_ref.shape
    rows = runs * run
    piece_run = run // pieces
    chips = groups // 2
    core = lax.rem(group, 2)
    chip = group // 2
    grow = share0.shape[0]
    per_block = 256 // grow
    blocks = full.shape[1] // per_block
    inner = share0.shape[1]
    last = slots - 1

    greet(groups, slots)

    def z_small(source, target, send_sem, recv_sem, step):
        return pltpu.make_async_remote_copy(
            src_ref=source, dst_ref=target.at[slots - step], send_sem=send_sem.at[step],
            recv_sem=recv_sem.at[slots - step], device_id=(group, lax.rem(slot + step, slots)), device_id_type=MESH,
        )

    def send_dot(step):
        return z_small(row_dot_ref, rd_recv, rds, rdr, step)

    def send_state(step):
        return z_small(small_z_ref, sz_recv, szs, szr, step)

    for step in range(1, slots):
        send_state(step).start()
        send_dot(step).start()

    def piece_of(job, shard):
        source = out_part if job < pieces else back_part
        return source.at[:, pl.ds((job % pieces) * piece_run, piece_run), pl.ds(shard * width, width)]

    def landing(job, me, to):
        return z_recv.at[job, me if me < to else me - 1], zr.at[job, me if me < to else me - 1]

    def z_push(job, number, shard, to, source, target, sem):
        return pltpu.make_async_remote_copy(
            src_ref=source, dst_ref=target, send_sem=zs.at[job, number], recv_sem=sem, device_id=(group, to),
            device_id_type=MESH,
        )

    def direct(job, me):
        def push(number, to):
            return z_push(job, number, to, to, piece_of(job, to), *landing(job, me, to))

        def to_mix(number, shard, to):
            return z_push(job, number, shard, to, piece_of(job, shard), z_comb.at[job], zc.at[job])

        if me == 0:
            return [to_mix(0, 3, 1), push(1, 2), push(2, 1)]
        if me == last:
            return [to_mix(0, 0, 2), push(1, 1), push(2, 2)]
        return [push(0, 0), push(1, 2)] if me == 1 else [push(0, 3), push(1, 1)]

    def mixed(job, me):
        to = 3 if me == 1 else 0
        return z_push(job, 2, to, to, z_mix.at[job], *landing(job, me, to))

    def own_load(kind):
        source = back_part if kind else out_part
        return pltpu.make_async_copy(source.at[:, :, pl.ds(slot * width, width)], z_own.at[kind], load_sem.at[kind])

    def mix_load(job, me):
        return pltpu.make_async_copy(piece_of(job, 3 if me == 1 else 0), z_mix.at[job], mix_sem.at[job])

    def shard_load(which):
        source, target = ((tokens, ptok), (cotangent, pcot))[which]
        return pltpu.make_async_copy(source.at[:, slot], target, load_sem.at[2 + which])

    def push(job):
        for me in range(slots):
            @pl.when(slot == me)
            def _(me=me):
                for copy in direct(job, me):
                    copy.start()

    def combine(job):
        for me in (1, 2):
            @pl.when(slot == me)
            def _(me=me):
                mix_load(job, me).wait()
                z_push(job, 2, 0, 0, z_comb.at[job], z_comb.at[job], zc.at[job]).wait_recv()
                both = z_mix[job].astype(f32) + z_comb[job].astype(f32)
                z_mix[job] = both.astype(bf16)
                mixed(job, me).start()

    rights = (scaled, d_gate, d_value)
    shares = (share0, share1, share2)

    def right_load(which):
        return pltpu.make_async_copy(rights[which], right.at[which % 2], right_sem.at[which])

    def left_load(which, block, place):
        if which == 0:
            per_shard = width // 256
            columns = pl.ds(pl.multiple_of(lax.rem(block, per_shard) * 256, 256), 256)
            source = cotangent.at[:, block // per_shard, :, :, columns]
        else:
            source = normed.at[:, :, :, pl.ds(pl.multiple_of(block * 256, 256), 256)]
        return pltpu.make_async_copy(source, left.at[place], left_sem.at[place])

    def grad_blocks(which, begin, end):
        def one(block, nothing):
            place = lax.rem(block, 2)

            @pl.when(block + 1 < blocks)
            def _():
                left_load(which, block + 1, 1 - place).start()

            left_load(which, block, place).wait()
            value = lax.dot_general(
                left[place].reshape(rows, 256), right[which % 2], (((0,), (0,)), ((), ())), preferred_element_type=f32
            )
            full[which % 2, pl.ds(block * per_block, per_block)] = value.reshape(per_block, grow, -1).astype(bf16)
            return nothing

        lax.fori_loop(begin, end, one, 0)

    partner = group + 1 - 2 * core

    def core_send(which):
        theirs = full.at[which % 2].reshape(chips, 2, grow, inner).at[:, 1 - core]
        return pltpu.make_async_remote_copy(
            src_ref=theirs, dst_ref=core_recv.at[which], send_sem=cs.at[which], recv_sem=cr.at[which],
            device_id=(partner, slot), device_id_type=MESH,
        )

    def chip_send(which, step):
        other = lax.rem(chip + step, chips)
        return pltpu.make_async_remote_copy(
            src_ref=full.at[which % 2, 2 * other + core], dst_ref=chip_recv.at[which, chips - step],
            send_sem=hs.at[which, step], recv_sem=hr.at[which, chips - step], device_id=(2 * other + core, slot),
            device_id_type=MESH,
        )

    def chip_pushes(which):
        core_send(which).wait()

        def one(step, nothing):
            other = lax.rem(chip + step, chips)
            mine = 2 * other + core
            both = full[which % 2, mine].astype(f32) + core_recv[which, other].astype(f32)
            full[which % 2, mine] = both.astype(bf16)
            chip_send(which, step).start()
            return nothing

        lax.fori_loop(1, chips, one, 0)
        shares[which][...] = full[which % 2, group].astype(f32) + core_recv[which, chip].astype(f32)

    def chip_drain(which):
        def drain(step, nothing):
            chip_send(which, step).wait_send()
            return nothing

        lax.fori_loop(1, chips, drain, 0)

    def chip_total(which):
        def one(step, nothing):
            pltpu.make_async_remote_copy(
                src_ref=chip_recv.at[which, step], dst_ref=chip_recv.at[which, step], send_sem=hs.at[which, step],
                recv_sem=hr.at[which, step], device_id=(group, slot), device_id_type=MESH,
            ).wait_recv()
            shares[which][...] += chip_recv[which, step].astype(f32)
            return nothing

        lax.fori_loop(1, chips, one, 0)

    def dp_small(source, target, send_sem, recv_sem, step):
        return pltpu.make_async_remote_copy(
            src_ref=source, dst_ref=target.at[groups - step], send_sem=send_sem.at[step],
            recv_sem=recv_sem.at[groups - step], device_id=(lax.rem(group + step, groups), slot), device_id_type=MESH,
        )

    def dp_small_start(source, target, send_sem, recv_sem):
        def one(step, nothing):
            dp_small(source, target, send_sem, recv_sem, step).start()
            return nothing

        lax.fori_loop(1, groups, one, 0)

    def dp_small_finish(source, target, send_sem, recv_sem, result):
        result[...] = source[...]

        def one(step, nothing):
            pltpu.make_async_remote_copy(
                src_ref=target.at[step], dst_ref=target.at[step], send_sem=send_sem.at[step],
                recv_sem=recv_sem.at[step], device_id=(group, slot), device_id_type=MESH,
            ).wait_recv()
            result[...] += target[step]
            return nothing

        lax.fori_loop(1, groups, one, 0)

        def drain(step, nothing):
            dp_small(source, target, send_sem, recv_sem, step).wait_send()
            return nothing

        lax.fori_loop(1, groups, drain, 0)

    def row_send(job, step):
        other = lax.rem(group + step, groups)
        return pltpu.make_async_remote_copy(
            src_ref=slots_buf.at[job, other], dst_ref=arrive.at[job, group], send_sem=rs.at[job, other],
            recv_sem=rr.at[job, group], device_id=(other, slot), device_id_type=MESH,
        )

    def finish(job):
        kind, piece = job // pieces, job % pieces
        here = pl.ds(piece * piece_run, piece_run)
        tall = runs * piece_run
        for me in range(slots):
            @pl.when(slot == me)
            def _(me=me):
                acc = z_own[kind, :, here, :].astype(f32)
                for source in ((1, 2) if me in (0, 3) else tuple(s for s in range(slots) if s != me)):
                    place, sem = landing(job, source, me)
                    z_push(job, 0, 0, 0, place, place, sem).wait_recv()
                    acc = acc + place[...].astype(f32)
                total[...] = acc
        summed = total[...].reshape(tall, width)
        kept = ptok[:, :, here, :].reshape(tall, width).astype(f32)
        if kind == 0:
            result = kept + summed
        else:
            inv = inv_ref[:, here, :].reshape(tall, 1)
            unit = kept * inv
            ngain_all[...] += fold_rows(summed * unit)
            dot_cols = rd_col[:, here, :].reshape(tall, LANES)
            dot_cols = jnp.concatenate([dot_cols] * (width // LANES), axis=1)
            cot = pcot[:, :, here, :].reshape(tall, width).astype(f32)
            result = cot + inv * (summed * gain_ref[...] - unit * dot_cols)
        row_buf[...] = result.astype(bf16).reshape(runs, piece_run, width)

        def fill(step, nothing):
            other = lax.rem(group + step, groups)
            slots_buf[job, other] = row_buf[back_run_ref[other]]
            row_send(job, step).start()
            return nothing

        lax.fori_loop(1, groups, fill, 0)
        arrive[job, group] = row_buf[back_run_ref[group]]

    def rows_wait(kind):
        for job in range(kind * pieces, (kind + 1) * pieces):
            def one(step, nothing, job=job):
                source = lax.rem(group + groups - step, groups)
                pltpu.make_async_remote_copy(
                    src_ref=arrive.at[job, source], dst_ref=arrive.at[job, source], send_sem=rs.at[job, source],
                    recv_sem=rr.at[job, source], device_id=(group, slot), device_id_type=MESH,
                ).wait_recv()
                row_send(job, step).wait_send()
                return nothing

            lax.fori_loop(1, groups, one, 0)

    def rows_take(kind, target):
        for piece in range(pieces):
            for index in range(runs):
                target[index, pl.ds(piece * piece_run, piece_run)] = arrive[kind * pieces + piece, return_from_ref[index]]

    z_groups = []
    for job in range(jobs):
        group_steps = [(combine, job)]
        if job + IN_FLIGHT < jobs:
            group_steps.append((push, job + IN_FLIGHT))
        if job > 0:
            group_steps.append((finish, job - 1))
        z_groups.append(group_steps)
    z_groups.append([(finish, jobs - 1)])

    def z_work():
        if z_groups:
            for step, job in z_groups.pop(0):
                step(job)

    for job in range(min(IN_FLIGHT, jobs)):
        push(job)
    own_load(0).start()
    own_load(1).start()
    shard_load(0).start()
    shard_load(1).start()
    for me in (1, 2):
        @pl.when(slot == me)
        def _(me=me):
            for job in range(jobs):
                mix_load(job, me).start()
    right_load(0).start()
    left_load(0, 0, 0).start()
    right_load(1).start()
    ngain_all[...] = jnp.zeros_like(ngain_all)

    half = blocks // 2
    right_load(0).wait()
    grad_blocks(0, 0, half)
    small_z = small_z_ref[...]
    for step in range(1, slots):
        send_state(step).wait()
    for step in range(1, slots):
        small_z = small_z + sz_recv[step]
    small_all[:, pl.ds(0, inner)] = small_ref[...]
    small_all[:, pl.ds(inner, 2 * LANES)] = small_z
    dp_small_start(small_all, small_recv, sms, smr)
    grad_blocks(0, half, blocks)
    core_send(0).start()
    right_load(2).start()
    for kind in range(2):
        own_load(kind).wait()
        shard_load(kind).wait()
    left_load(1, 0, 0).start()
    z_work()
    right_load(1).wait()
    grad_blocks(1, 0, half)
    chip_pushes(0)
    grad_blocks(1, half, blocks)
    core_send(1).start()
    left_load(2, 0, 0).start()
    rd_total = row_dot_ref[...]
    for step in range(1, slots):
        send_dot(step).wait()
    for step in range(1, slots):
        rd_total = rd_total + rd_recv[step]
    rd_total = rd_total * (1.0 / (width * slots))
    for block in range(rows // 256):
        piece_row = jnp.broadcast_to(rd_total[0:1, block * 256 : (block + 1) * 256], (LANES, 256))
        count = 256 // run
        rd_col[pl.ds(block * count, count)] = piece_row.T.reshape(count, run, LANES)
    z_work()
    right_load(2).wait()
    chip_drain(0)
    grad_blocks(2, 0, half)
    chip_pushes(1)
    z_work()
    grad_blocks(2, half, blocks)
    core_send(2).start()
    z_work()
    chip_pushes(2)
    while z_groups:
        z_work()
    dp_small_start(ngain_all, ngain_recv, ngs, ngr)

    rows_wait(0)
    rows_wait(1)
    rows_take(0, layer_ref)
    rows_take(1, tgrad_ref)
    dp_small_finish(small_all, small_recv, sms, smr, small_out)
    for which in range(3):
        chip_total(which)
    chip_drain(1)
    chip_drain(2)
    dp_small_finish(ngain_all, ngain_recv, ngs, ngr, ngain_out)
    for me in range(slots):
        @pl.when(slot == me)
        def _(me=me):
            for job in range(jobs):
                for copy in direct(job, me):
                    copy.wait_send()
                if me in (1, 2):
                    mixed(job, me).wait_send()


def tail(back_run, return_from, out_part, back_part, normed, tokens, cotangent, scaled, d_gate, d_value, row_dot, inv,
         gain, small, small_z):
    groups, slots = lax.axis_size("dp"), lax.axis_size("tensor")
    runs, run, model = out_part.shape
    width = model // slots
    rows = runs * run
    inner = scaled.shape[1]
    pieces = min(4, run // 16)
    jobs = 2 * pieces
    piece_run = run // pieces
    grow = model // groups
    chips = groups // 2
    vmem, anywhere, smem = (pl.BlockSpec(memory_space=s) for s in (pltpu.VMEM, pl.ANY, pltpu.SMEM))
    dma = pltpu.SemaphoreType.DMA
    shape = jax.ShapeDtypeStruct
    by_chunk = tokens.shape[:1] + tokens.shape[2:]
    part = (runs, piece_run, width)
    return pl.pallas_call(
        tail_kernel,
        out_shape=[
            shape((runs, run, width), bf16), shape((runs, run, width), bf16), shape((8, inner + 2 * LANES), f32),
            shape((8, width), f32),
        ] + [shape((grow, inner), f32)] * 3,
        in_specs=[smem] * 2 + [anywhere] * 8 + [vmem] * 5,
        out_specs=[vmem] * 7,
        scratch_shapes=[
            pltpu.VMEM((jobs, slots - 1) + part, bf16),
            pltpu.VMEM((jobs,) + part, bf16),
            pltpu.VMEM((2, runs, run, width), bf16),
            pltpu.VMEM((jobs,) + part, bf16),
            pltpu.VMEM(by_chunk, bf16),
            pltpu.VMEM(by_chunk, bf16),
            pltpu.VMEM((slots, 8, rows), f32),
            pltpu.VMEM((runs, run, LANES), f32),
            pltpu.VMEM(part, bf16),
            pltpu.VMEM((jobs, groups, piece_run, width), bf16),
            pltpu.VMEM((jobs, groups, piece_run, width), bf16),
            pltpu.VMEM((2,) + by_chunk[:-1] + (256,), bf16),
            pltpu.VMEM((2, rows, inner), bf16),
            pltpu.VMEM((2, groups, grow, inner), bf16),
            pltpu.VMEM((3, chips, grow, inner), bf16),
            pltpu.VMEM((3, chips, grow, inner), bf16),
            pltpu.VMEM(part, f32),
            pltpu.VMEM((slots, 8, 2 * LANES), f32),
            pltpu.VMEM((8, inner + 2 * LANES), f32),
            pltpu.VMEM((groups, 8, inner + 2 * LANES), f32),
            pltpu.VMEM((8, width), f32),
            pltpu.VMEM((groups, 8, width), f32),
            dma((4,)), dma((jobs,)), dma((2,)), dma((3,)),
            dma((jobs, 3)), dma((jobs, slots - 1)), dma((jobs,)),
            dma((slots,)), dma((slots,)), dma((slots,)), dma((slots,)),
            dma((groups,)), dma((groups,)), dma((groups,)), dma((groups,)),
            dma((jobs, groups)), dma((jobs, groups)),
            dma((3,)), dma((3,)), dma((3, chips)), dma((3, chips)),
        ],
        compiler_params=pltpu.CompilerParams(collective_id=3, has_side_effects=True, vmem_limit_bytes=64 << 20),
        name="tail",
    )(back_run, return_from, out_part, back_part, normed, tokens, cotangent, scaled, d_gate, d_value, row_dot, inv, gain,
      small, small_z)


def contract_rows(left, right):
    return lax.dot_general(left, right, (((0,), (0,)), ((), ())), preferred_element_type=f32)


def pad_heads(values):
    return jnp.pad(values, ((0, 0), (0, LANES - values.shape[1])))


def unfold(sums, index):
    return jnp.sum(sums[8 * index : 8 * index + 8], axis=0)


def per_device(
    tokens, cotangent, norm_gain, gate_proj, value_proj, state_proj, step_proj, conv_value, conv_value_bias,
    conv_state, conv_state_bias, step_bias, decay_log, skip_gain, gate_gain, out_proj, token_order, lengths,
):
    groups = lax.axis_size("dp")
    group = lax.axis_index("dp")
    slots = lax.axis_size("tensor")
    slot = lax.axis_index("tensor")
    rows, width = tokens.shape
    model = width * slots
    inner = gate_proj.shape[1]
    heads = step_bias.shape[0]
    run = 2 * rows // groups
    runs = rows // run

    source_run = token_order.reshape(groups, runs, run)[:, :, 0] // run
    source_group = source_run // runs
    from_here = source_group == group
    send_run = jnp.sum(jnp.where(from_here, source_run % runs, 0), axis=1)
    arrive_from = lax.dynamic_index_in_dim(source_group, group, 0, keepdims=False)
    every = jnp.arange(groups, dtype=jnp.int32)
    back_run = jnp.sum(
        jnp.where(arrive_from[None, :] == every[:, None], jnp.arange(runs, dtype=jnp.int32)[None, :], 0), axis=1
    )
    local_run = group * runs + jnp.arange(runs, dtype=jnp.int32)
    return_from = jnp.sum(
        jnp.where(source_run[None] == local_run[:, None, None], every[None, :, None], 0), axis=(1, 2)
    )

    def cut(values):
        return values.reshape(runs, run, values.shape[1])

    gain_full = norm_gain.astype(f32)
    small = (
        gain_full[None], gate_gain.astype(f32)[None], conv_value.astype(f32), conv_value_bias.astype(f32)[None],
        conv_state.astype(f32), conv_state_bias.astype(f32)[None], pad_heads(step_bias[None]),
        pad_heads(decay_log[None]), jnp.repeat(skip_gain, HEAD_DIM)[None],
    )
    (full_tokens, full_cotangent, normed, d_gate, d_value, scaled, back_partial, _, out_partial, d_state, d_step,
     inv_rms, row_dot, sumv, sums, sumh) = head(
        send_run, arrive_from, lengths, cut(tokens), cut(cotangent), gate_proj, value_proj, state_proj,
        pad_heads(step_proj), out_proj, small,
    )
    row_dot = row_dot.transpose(1, 0, 2).reshape(8, rows)
    normed_cut = normed.reshape(full_tokens.shape[0], full_tokens.shape[2], run, model)
    normed, d_gate, d_value, scaled, back_partial, out_partial = (
        v.reshape(rows, v.shape[2]) for v in (normed, d_gate, d_value, scaled, back_partial, out_partial)
    )
    state_grad = contract_rows(normed, d_state)
    step_grad = contract_rows(normed, d_step[:, :heads])
    gain_share = lax.dynamic_slice_in_dim(gain_full, slot * width, width, 0)
    by_head = jnp.pad(sumh.reshape(2, 8, LANES).sum(1).reshape(1, 2 * LANES), ((0, 0), (0, inner - 2 * LANES)))
    small = jnp.concatenate([sumv.reshape(7, 8, inner).sum(1), by_head])
    small_z = jnp.pad(sums.reshape(5, 8, 2 * LANES).sum(1), ((0, 3), (0, 0)))
    layer_output, tokens_grad, small, norm_gain_rows, out_grad_share, gate_share, value_share = tail(
        back_run, return_from, cut(out_partial), cut(back_partial), normed_cut, full_tokens, full_cotangent, scaled,
        d_gate, d_value, row_dot, cut(inv_rms), gain_share[None], small, small_z,
    )
    state_sums = small[:, inner:]

    def share(grad):
        return lax.psum_scatter(grad, "dp", scatter_dimension=0, tiled=True)

    step_share = share(step_grad)
    state_share = lax.psum_scatter(state_grad, ("dp", "tensor"), scatter_dimension=0, tiled=True)
    return (
        layer_output.reshape(rows, width),
        tokens_grad.reshape(rows, width),
        jnp.sum(norm_gain_rows, axis=0),
        gate_share,
        value_share,
        state_share,
        step_share,
        small[6:2:-1, :inner],
        small[2, :inner],
        state_sums[4:0:-1],
        state_sums[0],
        small[7, :heads],
        small[7, LANES : LANES + heads],
        jnp.sum(small[1, :inner].reshape(heads, HEAD_DIM), axis=1),
        small[0, :inner],
        out_grad_share,
    )


def solution(mesh):
    across = P(None, "tensor")
    both = P("dp", "tensor")
    heads = P("tensor")
    return jax.shard_map(
        per_device,
        mesh=mesh,
        in_specs=(
            both, both, P(), across, across, P(), across, across, heads, P(), P(), heads, heads, heads, heads, across,
            P(), P("dp", None),
        ),
        out_specs=(
            both, both, heads, both, both, P(("dp", "tensor"), None), both, across, heads, P(), P(), heads, heads, heads,
            heads, both,
        ),
        check_vma=False,
    )
```

time: 829 us -> 525 us (0.63)
  waiting for transfers between devices: 415 us -> 0.04 us
  Pallas kernels: 108 us -> 463 us
  blocking collectives: 140 us -> 0 us
  matrix products: 88.8 us -> 8.53 us
  starting transfers between devices: 14 us -> 0.08 us
    pallas_call x2, Pallas kernels: 108 us -> 463 us  [the longest x1 260 us: head(): pl.pallas_call(head_kernel, out_shape=[shape((chunks, slots, per_chunk, r...]
    reduce_scatter x1, waiting for transfers between devices: 141 us -> 0.01 us  [per_device(): lax.psum_scatter(state_grad, ('dp', 'tensor'), scatter_dimension=0, tiled...]
    reduce_scatter x6 -> x1, waiting for transfers between devices: 141 us -> 0.01 us  [share(): return lax.psum_scatter(grad, 'dp', scatter_dimension=0, tiled=True)]
    psum x3 -> x0, blocking collectives: 111 us -> none  [the longest x1 45.5 us: per_device(): row_dot = lax.psum(row_dot, 'tensor')]
    all_gather x2 -> x0, waiting for transfers between devices: 71.8 us -> none  [the longest x1 40.3 us: per_device(): full_tokens = lax.all_gather(packed_tokens, 'tensor', axis=1, tiled=True)]
    all_to_all x3 -> x0, waiting for transfers between devices: 60.1 us -> none  [exchange(): arrived = lax.all_to_all(cut, 'dp', split_axis=0, concat_axis=0, tiled=True)]
    dot_general x6 -> x0, matrix products: 49.5 us -> none  [the longest x5 36.9 us: dot_nt(): lax.dot_general(a, b, (((1,), (1,)), ((), ())), precision=precision, pref...]
    dot_general x5 -> x2, matrix products: 39.2 us -> 8.53 us  [contract_rows(): lax.dot_general(left, right, (((0,), (0,)), ((), ())), preferred_element_...]
  transfers between devices with their start and end apart: 12 -> 2, of which waited for: 10 -> 0; matrix products, arithmetic and copies ran while one was open for 12% -> 4% of each run, Pallas kernels for 13% -> 39%
where the time goes in v2:
time: 525 us; the launch traced here: 523 us
  Pallas kernels  463 us (88%)
  local copies, waits for them, and re-layouts  24.8 us (5%)
  between operations  14.2 us (3%)
  other arithmetic  12.7 us (2%)
  matrix products  8.53 us (2%)
    pallas_call x1, Pallas kernels, head(): pl.pallas_call(head_kernel, out_shape=[shape((chunks, slots, per_chunk, r...  260 us
    pallas_call x1, Pallas kernels, tail(): pl.pallas_call(tail_kernel, out_shape=[shape((runs, run, width), bf16), s...  203 us
  transfers between devices with their start and end apart: 2, of which 0 were waited for; matrix products, arithmetic and copies ran while one was open for 4% of the time, Pallas kernels for 39%

profile of v2, /device:TPU:0, one launch (start us, length us, event | category | flops | bytes accessed | tf_op | source)
XLA Modules:
  0.0 523.3 jit_solution(11599793015717732974)
XLA Ops:
  7.2 0.0 reduce-scatter.5.cloned.1.call-start
  7.2 0.8 reshape.112
  8.0 0.1 copy.39
  8.1 1.1 fusion.4
  9.2 1.1 copy.40
  10.3 1.3 convert_element_type.21
  11.6 1.3 broadcast_in_dim.74
  12.9 1.3 convert_element_type.22.tapv_ref
  14.2 1.3 broadcast_in_dim.75
  15.5 1.3 convert_element_type.23.taps_ref
  16.8 1.2 broadcast_in_dim.76
  18.0 1.2 pad.20.stepb_ref
  19.2 1.2 pad.21.rate_ref
  20.3 0.7 broadcast_in_dim.72
  21.0 0.7 broadcast_in_dim_reshape.3.skip_ref
  21.7 0.7 dynamic-slice_reduce_fusion.arrive_from_ref
  22.4 0.9 pad.19.wt_hbm
  23.3 259.6 %head.1 = (bf16[4,4,1,256,512]{4,3,2,1,0:T(8,128)(2,1)}, bf16[4,4,1,256,512]{4,3,2,1,0:T(8,128)(2,1)}, bf16[4,256,2048]{2,1,0:T(8,128)(2,1)}, bf16[4,256,1024]{2...) custom-call(s32[8]{0:T(128)} %get-tuple-element.60.send_run_ref, ...), custom_call_target="tpu_custom_call" | custom-call | tf_op jit(solution)/shard_map/head/pallas_call | solution.py:652
  282.9 3.6 fusion
  286.5 0.0 reduce-scatter.5.cloned.1.call-update
  286.5 0.0 reduce-scatter.3.cloned.1.call-start
  286.6 0.0 copy-start.5
  286.6 0.0 copy-start.6
  286.7 0.0 copy-start.8
  286.7 4.9 fusion.9
  291.6 0.0 reduce-scatter.3.cloned.1.call-update
  291.6 0.7 dynamic_slice.8
  292.3 0.6 pad.23.small_z_ref
  292.9 0.7 select_reduce_fusion.return_from_ref
  293.7 0.1 bitcast_reduce_fusion
  293.7 0.6 select_maximum_fusion.small_ref
  294.4 0.6 select_reduce_fusion.1.back_run_ref
  295.0 203.3 %tail.1 = (bf16[4,256,512]{2,1,0:T(8,128)(2,1)}, bf16[4,256,512]{2,1,0:T(8,128)(2,1)}, f32[8,1280]{1,0:T(8,128)}, f32[8,512]{1,0:T(8,128)}, f32[256,1024]{1,0:T(...) custom-call(s32[8]{0:T(128)} %select_reduce_fusion.1.back_run_ref, s32[4]{0:T(128)} %select_reduce_fusion.return_from_ref, ...), custom_call_target="tpu_custom_call" | custom-call | tf_op jit(solution)/shard_map/tail/pallas_call | solution.py:1118
  498.3 0.9 slice.35
  499.2 0.7 slice.37
  499.9 1.3 slice.38
  501.2 1.3 reduce_sum.78
  502.5 2.4 rev.6
  504.9 0.6 rev.7
  505.5 1.5 fusion.8
  507.0 0.1 reshape_squeeze.3
  507.1 0.6 reduce_sum.79
  507.7 1.2 slice_bitcast_fusion
  508.9 2.4 copy.46
  511.3 2.3 copy.47
  513.5 1.0 copy.48
  514.5 1.0 copy.49
  515.5 1.0 copy.50
  (23 shorter events, 0.1 us)
Async XLA Ops:
  7.2 501.7 %reduce-scatter.5.cloned.1.call-start = ((), (), s32[]{:S(2)}) async-start(), calls=%async_computation.3 | async-start | bytes 147456 | tf_op jit(solution)/shard_map/reduce_scatter | solution.py:1235
  282.9 3.7 copy-start.9
  286.5 222.4 %reduce-scatter.3.cloned.1.call-start = ((), (), s32[]{:S(2)}) async-start(), calls=%async_computation.2 | async-start | bytes 2162688 | tf_op jit(solution)/shard_map/reduce_scatter | solution.py:1238
  286.6 5.0 copy-start.5
  286.6 5.7 %copy-start.4 = (f32[40,256]{1,0:T(8,128)S(1)}, f32[40,256]{1,0:T(8,128)}, u32[]{:S(2)}) copy-start(f32[40,256]{1,0:T(8,128)} %get-tuple-element.50) | copy-start | bytes 122884
  286.6 6.3 %copy-start.7 = (f32[16,128]{1,0:T(8,128)S(1)}, f32[16,128]{1,0:T(8,128)}, u32[]{:S(2)}) copy-start(f32[16,128]{1,0:T(8,128)} %get-tuple-element.49) | copy-start | bytes 24580
  286.6 6.3 %copy-start.6 = (s32[8,4]{0,1:T(4,128)S(1)}, s32[8,4]{0,1:T(4,128)}, u32[]{:S(2)}) copy-start(s32[8,4]{0,1:T(4,128)} %get-tuple-element.62) | copy-start | bytes 388
  286.6 7.0 %copy-start.3 = (f32[56,1024]{1,0:T(8,128)S(1)}, f32[56,1024]{1,0:T(8,128)}, u32[]{:S(2)}) copy-start(f32[56,1024]{1,0:T(8,128)} %get-tuple-element.48) | copy-start | bytes 688132
  286.7 7.7 %copy-start.8 = (s32[4]{0:T(128)S(1)}, s32[4]{0:T(128)}, u32[]{:S(2)}) copy-start(s32[4]{0:T(128)} %dynamic-slice_reduce_fusion.arrive_from_ref) | copy-start | bytes 52
  498.3 15.2 %copy-start.2 = (f32[256,1024]{1,0:T(8,128)S(1)}, f32[256,1024]{1,0:T(8,128)}, u32[]{:S(2)}) copy-start(f32[256,1024]{1,0:T(8,128)} %get-tuple-element.87) | copy-start | bytes 3145732
  498.3 16.2 %copy-start.1 = (f32[256,1024]{1,0:T(8,128)S(1)}, f32[256,1024]{1,0:T(8,128)}, u32[]{:S(2)}) copy-start(f32[256,1024]{1,0:T(8,128)} %get-tuple-element.88) | copy-start | bytes 3145732
  508.9 6.6 %copy-start = (f32[256,1024]{1,0:T(8,128)S(1)}, f32[256,1024]{1,0:T(8,128)}, u32[]{:S(2)}) copy-start(f32[256,1024]{1,0:T(8,128)} %get-tuple-element.99) | copy-start | bytes 3145732
Sparse Core Ops, SparseCore 0:
  286.7 43.0 reduce-scatter.4
  332.7 151.7 reduce-scatter.2

commit v3 on v2

--- a/solution.py
+++ b/solution.py
@@ -11,7 +11,8 @@
 LANES = 128
 HEAD_DIM = 64
 AHEAD = 2
-IN_FLIGHT = 3
+WINDOW = 2
+EARLY = 5
 HEAD_VMEM = 64 << 20
 highest = lax.Precision.HIGHEST
 epsilon = 1e-05
@@ -124,7 +125,7 @@
     send_run_ref, arrive_from_ref, lengths_ref, tokens, cotangent, wg_hbm, wv_hbm, ws_hbm, wt_hbm, wo_hbm,
     gain_ref, ggain_ref, tapv_ref, biasv_ref, taps_ref, biass_ref, stepb_ref, rate_ref, skip_ref,
     fulltok, fullcot, normed_out, dgate_out, dvalue_out, scaled_out, back_out, keep, out_part,
-    dstate_ref, dstep_ref, inv_ref, dot_ref, sumv_ref, sums_ref, sumh_ref,
+    dsmall_ref, inv_ref, dot_ref, sumv_ref, sums_ref, sumh_ref,
     wg, wv, ws, wt, wo, ptok, pcot, slots_buf, arr_tok, arr_cot, xbuf, nbuf, kbuf, gate_all, y_all,
     sraw_all, spre_all, stepin_all, states, d_carry, vext, dvext, sext, cum_cols, step_cols, cum_rows, neg_bias,
     scores, d_scores, d_entry, d_leave, acc_step, acc_cum, acc_dot, dsc, dgbuf, dvbuf, scbuf, bbuf, zbuf,
@@ -593,7 +594,7 @@
         rate = jnp.exp(rate_ref[...])
         d_step_in = (acc_step[...] - d_log * rate) * sigmoid(step_in)
         d_step = d_step_in.astype(bf16)
-        dstep_ref[pl.ds(start, Q)] = d_step
+        dsmall_ref[pl.ds(start, Q), 2 * LANES :] = d_step
         step_raw = step_in - stepb_ref[...]
         acc_dot[...] += jnp.where(lane < 2 * pairs, d_step.astype(f32) * step_raw, 0.0)
         sumh_ref[pl.ds(0, 8)] += fold_rows(d_step_in)
@@ -616,14 +617,14 @@
                 total = total + taps_ref[3 - shift : 4 - shift, columns] * moved_back
                 sums_ref[pl.ds(8 + 8 * shift, 8), columns] += fold_rows(sraw * moved_back)
             d_state_raw = total.astype(bf16)
-            dstate_ref[pl.ds(start, Q), columns] = d_state_raw
+            dsmall_ref[pl.ds(start, Q), columns] = d_state_raw
             acc_dot[...] += d_state_raw.astype(f32) * sraw
         dot_ref[chunk] = ones_rows(acc_dot[...])
 
         for shard in range(slots):
             here = pl.ds(shard * width, width)
             part = dot_nt(dgbuf[...], wg[here]) + dot_nt(dvbuf[...], wv[here])
-            part = part + dot_nt(dstate_ref[pl.ds(start, Q)], ws[here]) + dot_nt(d_step, wt[here])
+            part = part + dot_nt(dsmall_ref[pl.ds(start, Q), : 2 * LANES], ws[here]) + dot_nt(d_step, wt[here])
             bbuf[:, shard * width : (shard + 1) * width] = part.astype(bf16)
         store(3, chunk).start()
         for shard in range(slots):
@@ -661,8 +662,7 @@
             shape((chunks, Q, model), bf16),
             shape((chunks, 2, Q, inner), f32),
             shape((chunks, Q, model), bf16),
-            shape((rows, 2 * LANES), bf16),
-            shape((rows, LANES), bf16),
+            shape((rows, 3 * LANES), bf16),
             shape((rows, 1), f32),
             shape((chunks, 8, Q), f32),
             shape((56, inner), f32),
@@ -670,7 +670,7 @@
             shape((16, LANES), f32),
         ],
         in_specs=[smem] * 3 + [anywhere] * 7 + [vmem] * len(small),
-        out_specs=[anywhere] * 9 + [vmem] * 7,
+        out_specs=[anywhere] * 9 + [vmem] * 6,
         scratch_shapes=[
             pltpu.VMEM(wg.shape, bf16), pltpu.VMEM(wv.shape, bf16), pltpu.VMEM(ws.shape, bf16),
             pltpu.VMEM(wt.shape, bf16), pltpu.VMEM(wo.shape, bf16),
@@ -726,11 +726,12 @@
 
 def tail_kernel(
     back_run_ref, return_from_ref, out_part, back_part, normed, tokens, cotangent, scaled, d_gate, d_value,
-    row_dot_ref, inv_ref, gain_ref, small_ref, small_z_ref,
-    layer_ref, tgrad_ref, small_out, ngain_out, share0, share1, share2,
+    row_dot_ref, inv_ref, gain_ref, small_ref, small_z_ref, dsmall_ref,
+    layer_ref, tgrad_ref, small_out, ngain_out, share0, share1, share2, state_out, step_out,
     z_recv, z_comb, z_own, z_mix, ptok, pcot, rd_recv, rd_col, row_buf, slots_buf, arrive, left, right, full,
     core_recv, chip_recv, total, sz_recv, small_all, small_recv, ngain_all, ngain_recv,
-    load_sem, mix_sem, left_sem, right_sem, zs, zr, zc, rds, rdr, szs, szr, sms, smr, ngs, ngr, rs, rr, cs, cr, hs, hr,
+    thin, thin_core, thin_chip, thin_own, thin_z,
+    load_sem, mix_sem, left_sem, right_sem, zs, zr, zc, rds, rdr, szs, szr, sms, smr, ngs, ngr, rs, rr, cs, cr, hs, hr, tcs, ths, thr, tzs, tzr,
 ):
     groups, slots = lax.axis_size("dp"), lax.axis_size("tensor")
     group, slot = lax.axis_index("dp"), lax.axis_index("tensor")
@@ -779,7 +780,7 @@
             device_id_type=MESH,
         )
 
-    def direct(job, me):
+    def direct(job, me, early):
         def push(number, to):
             return z_push(job, number, to, to, piece_of(job, to), *landing(job, me, to))
 
@@ -787,9 +788,11 @@
             return z_push(job, number, shard, to, piece_of(job, shard), z_comb.at[job], zc.at[job])
 
         if me == 0:
-            return [to_mix(0, 3, 1), push(1, 2), push(2, 1)]
+            return [to_mix(0, 3, 1)] if early else [push(1, 2), push(2, 1)]
         if me == last:
-            return [to_mix(0, 0, 2), push(1, 1), push(2, 2)]
+            return [to_mix(0, 0, 2)] if early else [push(1, 1), push(2, 2)]
+        if early:
+            return []
         return [push(0, 0), push(1, 2)] if me == 1 else [push(0, 3), push(1, 1)]
 
     def mixed(job, me):
@@ -807,11 +810,11 @@
         source, target = ((tokens, ptok), (cotangent, pcot))[which]
         return pltpu.make_async_copy(source.at[:, slot], target, load_sem.at[2 + which])
 
-    def push(job):
-        for me in range(slots):
+    def push(job, early):
+        for me in (0, last) if early else range(slots):
             @pl.when(slot == me)
             def _(me=me):
-                for copy in direct(job, me):
+                for copy in direct(job, me, early):
                     copy.start()
 
     def combine(job):
@@ -852,6 +855,11 @@
                 left[place].reshape(rows, 256), right[which % 2], (((0,), (0,)), ((), ())), preferred_element_type=f32
             )
             full[which % 2, pl.ds(block * per_block, per_block)] = value.reshape(per_block, grow, -1).astype(bf16)
+            if which == 1:
+                value = lax.dot_general(
+                    left[place].reshape(rows, 256), dsmall_ref[...], (((0,), (0,)), ((), ())), preferred_element_type=f32
+                )
+                thin[pl.ds(block * per_block, per_block)] = value.reshape(per_block, grow, -1)
             return nothing
 
         lax.fori_loop(begin, end, one, 0)
@@ -905,6 +913,69 @@
 
         lax.fori_loop(1, chips, one, 0)
 
+    def thin_core_send():
+        theirs = thin.reshape(chips, 2, grow, thin.shape[2]).at[:, 1 - core]
+        return pltpu.make_async_remote_copy(
+            src_ref=theirs, dst_ref=thin_core, send_sem=tcs.at[0], recv_sem=tcs.at[1], device_id=(partner, slot),
+            device_id_type=MESH,
+        )
+
+    def thin_chip_send(step):
+        other = lax.rem(chip + step, chips)
+        return pltpu.make_async_remote_copy(
+            src_ref=thin.at[2 * other + core], dst_ref=thin_chip.at[chips - step], send_sem=ths.at[step],
+            recv_sem=thr.at[chips - step], device_id=(2 * other + core, slot), device_id_type=MESH,
+        )
+
+    def thin_pushes():
+        thin_core_send().wait()
+
+        def one(step, nothing):
+            other = lax.rem(chip + step, chips)
+            thin[2 * other + core] = thin[2 * other + core] + thin_core[other]
+            thin_chip_send(step).start()
+            return nothing
+
+        lax.fori_loop(1, chips, one, 0)
+        thin_own[...] = thin[group] + thin_core[chip]
+
+    def thin_z_send(step):
+        other = lax.rem(slot + step, slots)
+        part = state_out.shape[0]
+        return pltpu.make_async_remote_copy(
+            src_ref=thin_own.at[pl.ds(other * part, part), pl.ds(0, 2 * LANES)], dst_ref=thin_z.at[slots - step],
+            send_sem=tzs.at[step], recv_sem=tzr.at[slots - step], device_id=(group, other), device_id_type=MESH,
+        )
+
+    def thin_total():
+        def one(step, nothing):
+            pltpu.make_async_remote_copy(
+                src_ref=thin_chip.at[step], dst_ref=thin_chip.at[step], send_sem=ths.at[step], recv_sem=thr.at[step],
+                device_id=(group, slot), device_id_type=MESH,
+            ).wait_recv()
+            thin_own[...] += thin_chip[step]
+            return nothing
+
+        lax.fori_loop(1, chips, one, 0)
+        for step in range(1, slots):
+            thin_z_send(step).start()
+        step_out[...] = thin_own[:, 2 * LANES :]
+
+    def thin_finish():
+        part = state_out.shape[0]
+        acc = thin_own[pl.ds(slot * part, part), : 2 * LANES]
+        for step in range(1, slots):
+            thin_z_send(step).wait()
+        for step in range(1, slots):
+            acc = acc + thin_z[step]
+        state_out[...] = acc
+
+        def drain(step, nothing):
+            thin_chip_send(step).wait_send()
+            return nothing
+
+        lax.fori_loop(1, chips, drain, 0)
+
     def dp_small(source, target, send_sem, recv_sem, step):
         return pltpu.make_async_remote_copy(
             src_ref=source, dst_ref=target.at[groups - step], send_sem=send_sem.at[step],
@@ -940,9 +1011,16 @@
     def row_send(job, step):
         other = lax.rem(group + step, groups)
         return pltpu.make_async_remote_copy(
-            src_ref=slots_buf.at[job, other], dst_ref=arrive.at[job, group], send_sem=rs.at[job, other],
+            src_ref=slots_buf.at[job % pieces, other], dst_ref=arrive.at[job, group], send_sem=rs.at[job, other],
             recv_sem=rr.at[job, group], device_id=(other, slot), device_id_type=MESH,
         )
+
+    def rows_drain(job):
+        def one(step, nothing):
+            row_send(job, step).wait_send()
+            return nothing
+
+        lax.fori_loop(1, groups, one, 0)
 
     def finish(job):
         kind, piece = job // pieces, job % pieces
@@ -973,10 +1051,12 @@
 
         def fill(step, nothing):
             other = lax.rem(group + step, groups)
-            slots_buf[job, other] = row_buf[back_run_ref[other]]
+            slots_buf[job % pieces, other] = row_buf[back_run_ref[other]]
             row_send(job, step).start()
             return nothing
 
+        if kind == 1:
+            rows_drain(job - pieces)
         lax.fori_loop(1, groups, fill, 0)
         arrive[job, group] = row_buf[back_run_ref[group]]
 
@@ -988,7 +1068,6 @@
                     src_ref=arrive.at[job, source], dst_ref=arrive.at[job, source], send_sem=rs.at[job, source],
                     recv_sem=rr.at[job, source], device_id=(group, slot), device_id_type=MESH,
                 ).wait_recv()
-                row_send(job, step).wait_send()
                 return nothing
 
             lax.fori_loop(1, groups, one, 0)
@@ -998,23 +1077,19 @@
             for index in range(runs):
                 target[index, pl.ds(piece * piece_run, piece_run)] = arrive[kind * pieces + piece, return_from_ref[index]]
 
-    z_groups = []
-    for job in range(jobs):
-        group_steps = [(combine, job)]
-        if job + IN_FLIGHT < jobs:
-            group_steps.append((push, job + IN_FLIGHT))
-        if job > 0:
-            group_steps.append((finish, job - 1))
-        z_groups.append(group_steps)
-    z_groups.append([(finish, jobs - 1)])
-
-    def z_work():
-        if z_groups:
-            for step, job in z_groups.pop(0):
-                step(job)
-
-    for job in range(min(IN_FLIGHT, jobs)):
-        push(job)
+    def let_in(job):
+        if job < jobs:
+            push(job, False)
+            combine(job)
+
+    def step_of(job):
+        if job + EARLY < jobs:
+            push(job + EARLY, True)
+        let_in(job + WINDOW)
+        finish(job)
+
+    for job in range(min(EARLY, jobs)):
+        push(job, True)
     own_load(0).start()
     own_load(1).start()
     shard_load(0).start()
@@ -1047,12 +1122,13 @@
         own_load(kind).wait()
         shard_load(kind).wait()
     left_load(1, 0, 0).start()
-    z_work()
+    push(0, False)
     right_load(1).wait()
     grad_blocks(1, 0, half)
     chip_pushes(0)
     grad_blocks(1, half, blocks)
     core_send(1).start()
+    thin_core_send().start()
     left_load(2, 0, 0).start()
     rd_total = row_dot_ref[...]
     for step in range(1, slots):
@@ -1064,27 +1140,35 @@
         piece_row = jnp.broadcast_to(rd_total[0:1, block * 256 : (block + 1) * 256], (LANES, 256))
         count = 256 // run
         rd_col[pl.ds(block * count, count)] = piece_row.T.reshape(count, run, LANES)
-    z_work()
+    combine(0)
     right_load(2).wait()
     chip_drain(0)
+    let_in(1)
     grad_blocks(2, 0, half)
     chip_pushes(1)
-    z_work()
+    thin_pushes()
     grad_blocks(2, half, blocks)
     core_send(2).start()
-    z_work()
-    chip_pushes(2)
-    while z_groups:
-        z_work()
+    for job in range(2, WINDOW):
+        let_in(job)
+    for job in range(jobs):
+        if job == 1:
+            chip_pushes(2)
+        step_of(job)
+        if job == jobs // 2:
+            thin_total()
     dp_small_start(ngain_all, ngain_recv, ngs, ngr)
 
     rows_wait(0)
     rows_wait(1)
+    for job in range(pieces, jobs):
+        rows_drain(job)
     rows_take(0, layer_ref)
     rows_take(1, tgrad_ref)
     dp_small_finish(small_all, small_recv, sms, smr, small_out)
     for which in range(3):
         chip_total(which)
+    thin_finish()
     chip_drain(1)
     chip_drain(2)
     dp_small_finish(ngain_all, ngain_recv, ngs, ngr, ngain_out)
@@ -1092,14 +1176,14 @@
         @pl.when(slot == me)
         def _(me=me):
             for job in range(jobs):
-                for copy in direct(job, me):
+                for copy in direct(job, me, True) + direct(job, me, False):
                     copy.wait_send()
                 if me in (1, 2):
                     mixed(job, me).wait_send()
 
 
 def tail(back_run, return_from, out_part, back_part, normed, tokens, cotangent, scaled, d_gate, d_value, row_dot, inv,
-         gain, small, small_z):
+         gain, small, small_z, d_small):
     groups, slots = lax.axis_size("dp"), lax.axis_size("tensor")
     runs, run, model = out_part.shape
     width = model // slots
@@ -1120,9 +1204,9 @@
         out_shape=[
             shape((runs, run, width), bf16), shape((runs, run, width), bf16), shape((8, inner + 2 * LANES), f32),
             shape((8, width), f32),
-        ] + [shape((grow, inner), f32)] * 3,
-        in_specs=[smem] * 2 + [anywhere] * 8 + [vmem] * 5,
-        out_specs=[vmem] * 7,
+        ] + [shape((grow, inner), f32)] * 3 + [shape((grow // slots, 2 * LANES), f32), shape((grow, LANES), f32)],
+        in_specs=[smem] * 2 + [anywhere] * 8 + [vmem] * 6,
+        out_specs=[vmem] * 9,
         scratch_shapes=[
             pltpu.VMEM((jobs, slots - 1) + part, bf16),
             pltpu.VMEM((jobs,) + part, bf16),
@@ -1133,7 +1217,7 @@
             pltpu.VMEM((slots, 8, rows), f32),
             pltpu.VMEM((runs, run, LANES), f32),
             pltpu.VMEM(part, bf16),
-            pltpu.VMEM((jobs, groups, piece_run, width), bf16),
+            pltpu.VMEM((pieces, groups, piece_run, width), bf16),
             pltpu.VMEM((jobs, groups, piece_run, width), bf16),
             pltpu.VMEM((2,) + by_chunk[:-1] + (256,), bf16),
             pltpu.VMEM((2, rows, inner), bf16),
@@ -1146,29 +1230,27 @@
             pltpu.VMEM((groups, 8, inner + 2 * LANES), f32),
             pltpu.VMEM((8, width), f32),
             pltpu.VMEM((groups, 8, width), f32),
+            pltpu.VMEM((groups, grow, 3 * LANES), f32),
+            pltpu.VMEM((chips, grow, 3 * LANES), f32),
+            pltpu.VMEM((chips, grow, 3 * LANES), f32),
+            pltpu.VMEM((grow, 3 * LANES), f32),
+            pltpu.VMEM((slots, grow // slots, 2 * LANES), f32),
             dma((4,)), dma((jobs,)), dma((2,)), dma((3,)),
             dma((jobs, 3)), dma((jobs, slots - 1)), dma((jobs,)),
             dma((slots,)), dma((slots,)), dma((slots,)), dma((slots,)),
             dma((groups,)), dma((groups,)), dma((groups,)), dma((groups,)),
             dma((jobs, groups)), dma((jobs, groups)),
             dma((3,)), dma((3,)), dma((3, chips)), dma((3, chips)),
+            dma((2,)), dma((chips,)), dma((chips,)), dma((slots,)), dma((slots,)),
         ],
         compiler_params=pltpu.CompilerParams(collective_id=3, has_side_effects=True, vmem_limit_bytes=64 << 20),
         name="tail",
     )(back_run, return_from, out_part, back_part, normed, tokens, cotangent, scaled, d_gate, d_value, row_dot, inv, gain,
-      small, small_z)
-
-
-def contract_rows(left, right):
-    return lax.dot_general(left, right, (((0,), (0,)), ((), ())), preferred_element_type=f32)
+      small, small_z, d_small)
 
 
 def pad_heads(values):
     return jnp.pad(values, ((0, 0), (0, LANES - values.shape[1])))
-
-
-def unfold(sums, index):
-    return jnp.sum(sums[8 * index : 8 * index + 8], axis=0)
 
 
 def per_device(
@@ -1209,33 +1291,25 @@
         conv_state.astype(f32), conv_state_bias.astype(f32)[None], pad_heads(step_bias[None]),
         pad_heads(decay_log[None]), jnp.repeat(skip_gain, HEAD_DIM)[None],
     )
-    (full_tokens, full_cotangent, normed, d_gate, d_value, scaled, back_partial, _, out_partial, d_state, d_step,
+    (full_tokens, full_cotangent, normed, d_gate, d_value, scaled, back_partial, _, out_partial, d_small,
      inv_rms, row_dot, sumv, sums, sumh) = head(
         send_run, arrive_from, lengths, cut(tokens), cut(cotangent), gate_proj, value_proj, state_proj,
         pad_heads(step_proj), out_proj, small,
     )
     row_dot = row_dot.transpose(1, 0, 2).reshape(8, rows)
     normed_cut = normed.reshape(full_tokens.shape[0], full_tokens.shape[2], run, model)
-    normed, d_gate, d_value, scaled, back_partial, out_partial = (
-        v.reshape(rows, v.shape[2]) for v in (normed, d_gate, d_value, scaled, back_partial, out_partial)
+    d_gate, d_value, scaled, back_partial, out_partial = (
+        v.reshape(rows, v.shape[2]) for v in (d_gate, d_value, scaled, back_partial, out_partial)
     )
-    state_grad = contract_rows(normed, d_state)
-    step_grad = contract_rows(normed, d_step[:, :heads])
     gain_share = lax.dynamic_slice_in_dim(gain_full, slot * width, width, 0)
     by_head = jnp.pad(sumh.reshape(2, 8, LANES).sum(1).reshape(1, 2 * LANES), ((0, 0), (0, inner - 2 * LANES)))
     small = jnp.concatenate([sumv.reshape(7, 8, inner).sum(1), by_head])
     small_z = jnp.pad(sums.reshape(5, 8, 2 * LANES).sum(1), ((0, 3), (0, 0)))
-    layer_output, tokens_grad, small, norm_gain_rows, out_grad_share, gate_share, value_share = tail(
+    layer_output, tokens_grad, small, norm_gain_rows, out_grad_share, gate_share, value_share, state_share, step_share = tail(
         back_run, return_from, cut(out_partial), cut(back_partial), normed_cut, full_tokens, full_cotangent, scaled,
-        d_gate, d_value, row_dot, cut(inv_rms), gain_share[None], small, small_z,
+        d_gate, d_value, row_dot, cut(inv_rms), gain_share[None], small, small_z, d_small,
     )
     state_sums = small[:, inner:]
-
-    def share(grad):
-        return lax.psum_scatter(grad, "dp", scatter_dimension=0, tiled=True)
-
-    step_share = share(step_grad)
-    state_share = lax.psum_scatter(state_grad, ("dp", "tensor"), scatter_dimension=0, tiled=True)
     return (
         layer_output.reshape(rows, width),
         tokens_grad.reshape(rows, width),
@@ -1243,7 +1317,7 @@
         gate_share,
         value_share,
         state_share,
-        step_share,
+        step_share[:, :heads],
         small[6:2:-1, :inner],
         small[2, :inner],
         state_sums[4:0:-1],

time: 525 us -> 489 us (0.931)
  Pallas kernels: 463 us -> 444 us
  between operations: 14.2 us -> 0.73 us
  matrix products: 8.53 us -> 0 us
    pallas_call x1, Pallas kernels: 203 us -> 184 us  [tail(): pl.pallas_call(tail_kernel, out_shape=[shape((runs, run, width), bf16), s...]
    dot_general x2 -> x0, matrix products: 8.53 us -> none  [contract_rows(): lax.dot_general(left, right, (((0,), (0,)), ((), ())), preferred_element_...]
    unnamed x26 -> x18, local copies, waits for them, and re-layouts: 8.68 us -> 11.4 us
  transfers between devices with their start and end apart: 2 -> 0, of which waited for: 0 -> 0; matrix products, arithmetic and copies ran while one was open for 4% -> 0% of each run, Pallas kernels for 39% -> 0%
where the time goes in v3:
time: 489 us; the launch traced here: 487 us
  Pallas kernels  444 us (91%)
  local copies, waits for them, and re-layouts  27.5 us (6%)
  other arithmetic  14.7 us (3%)
    pallas_call x1, Pallas kernels, head(): pl.pallas_call(head_kernel, out_shape=[shape((chunks, slots, per_chunk, r...  260 us
    pallas_call x1, Pallas kernels, tail(): pl.pallas_call(tail_kernel, out_shape=[shape((runs, run, width), bf16), s...  184 us
    unnamed x18, local copies, waits for them, and re-layouts  11.4 us

profile of v3, /device:TPU:0, one launch (start us, length us, event | category | flops | bytes accessed | tf_op | source)
XLA Modules:
  0.0 486.8 jit_solution(11875311580328259449)
XLA Ops:
  0.7 0.8 reshape.109
  1.4 0.1 copy.41
  1.5 0.5 fusion.2
  2.1 0.2 dynamic-slice_reduce_fusion.arrive_from_ref
  2.3 0.5 copy-done.4
  2.8 0.6 select_reduce_fusion.1.back_run_ref
  3.4 0.7 select_reduce_fusion.return_from_ref
  4.1 1.1 copy.42
  5.3 0.9 pad.19.wt_hbm
  6.2 1.3 convert_element_type.21
  7.4 1.3 broadcast_in_dim.74
  8.7 1.3 convert_element_type.22.tapv_ref
  10.0 1.3 broadcast_in_dim.75
  11.3 1.3 convert_element_type.23.taps_ref
  12.6 1.2 broadcast_in_dim.76
  13.8 1.2 pad.20.stepb_ref
  15.0 1.2 pad.21.rate_ref
  16.1 0.7 broadcast_in_dim.72
  16.9 0.7 broadcast_in_dim_reshape.3.skip_ref
  17.5 259.6 %head.1 = (bf16[4,4,1,256,512]{4,3,2,1,0:T(8,128)(2,1)}, bf16[4,4,1,256,512]{4,3,2,1,0:T(8,128)(2,1)}, bf16[4,256,2048]{2,1,0:T(8,128)(2,1)}, bf16[4,256,1024]{2...) custom-call(s32[8]{0:T(128)} %get-tuple-element.110.send_run_ref, ...), custom_call_target="tpu_custom_call" | custom-call | tf_op jit(solution)/shard_map/head/pallas_call | solution.py:653
  277.1 1.3 dynamic_slice.8
  278.5 0.7 bitcast_reduce_fusion.2
  279.2 1.0 bitcast_reduce_fusion
  280.2 0.6 select_maximum_fusion.small_ref
  280.8 0.8 bitcast_reduce_fusion.1
  281.6 0.6 pad.23.small_z_ref
  282.2 184.2 %tail.1 = (bf16[4,256,512]{2,1,0:T(8,128)(2,1)}, bf16[4,256,512]{2,1,0:T(8,128)(2,1)}, f32[8,1280]{1,0:T(8,128)}, f32[8,512]{1,0:T(8,128)}, f32[256,1024]{1,0:T(...) custom-call(s32[8]{0:T(128)} %select_reduce_fusion.1.back_run_ref, ...), custom_call_target="tpu_custom_call" | custom-call | tf_op jit(solution)/shard_map/tail/pallas_call | solution.py:1202
  466.4 0.0 copy-start.2
  466.4 0.0 copy-start.1
  466.4 1.5 reduce_sum.78
  467.9 1.6 copy.43
  469.5 0.8 slice.35
  470.2 2.4 rev.6
  472.6 1.5 fusion.6
  474.1 0.7 slice.37
  474.8 0.6 rev.7
  475.4 1.3 slice.38
  476.7 1.2 slice_bitcast_fusion
  477.9 0.1 reshape_squeeze.3
  478.0 0.6 reduce_sum.79
  478.6 2.4 copy.50
  481.0 2.3 copy.51
  483.2 0.0 copy-done.2
  483.2 1.0 copy.52
  484.2 1.0 copy.53
  485.2 0.0 copy-done.3
  485.2 0.6 copy.54
  485.8 1.0 copy.55
  (7 shorter events, 0.0 us)
Async XLA Ops:
  2.3 0.5 copy-start.4
  466.4 16.8 %copy-start.2 = (f32[256,1024]{1,0:T(8,128)S(1)}, f32[256,1024]{1,0:T(8,128)}, u32[]{:S(2)}) copy-start(f32[256,1024]{1,0:T(8,128)} %get-tuple-element.137) | copy-start | bytes 3145732
  466.4 17.8 %copy-start.1 = (f32[256,1024]{1,0:T(8,128)S(1)}, f32[256,1024]{1,0:T(8,128)}, u32[]{:S(2)}) copy-start(f32[256,1024]{1,0:T(8,128)} %get-tuple-element.138) | copy-start | bytes 3145732
  478.6 6.6 %copy-start.3 = (f32[64,256]{1,0:T(8,128)S(1)}, f32[64,256]{1,0:T(8,128)}, u32[]{:S(2)}) copy-start(f32[64,256]{1,0:T(8,128)} %get-tuple-element.139) | copy-start | bytes 196612
  478.6 7.2 %copy-start = (f32[256,1024]{1,0:T(8,128)S(1)}, f32[256,1024]{1,0:T(8,128)}, u32[]{:S(2)}) copy-start(f32[256,1024]{1,0:T(8,128)} %get-tuple-element.149) | copy-start | bytes 3145732

commit v4 on v3

--- a/solution.py
+++ b/solution.py
@@ -10,7 +10,6 @@
 Q = 256
 LANES = 128
 HEAD_DIM = 64
-AHEAD = 2
 WINDOW = 2
 EARLY = 5
 HEAD_VMEM = 64 << 20
@@ -128,7 +127,7 @@
     dsmall_ref, inv_ref, dot_ref, sumv_ref, sums_ref, sumh_ref,
     wg, wv, ws, wt, wo, ptok, pcot, slots_buf, arr_tok, arr_cot, xbuf, nbuf, kbuf, gate_all, y_all,
     sraw_all, spre_all, stepin_all, states, d_carry, vext, dvext, sext, cum_cols, step_cols, cum_rows, neg_bias,
-    scores, d_scores, d_entry, d_leave, acc_step, acc_cum, acc_dot, dsc, dgbuf, dvbuf, scbuf, bbuf, zbuf,
+    scores, d_scores, d_entry, d_leave, acc_step, acc_cum, acc_dot, acc_prod, dsc, dgbuf, dvbuf, scbuf, bbuf, zbuf,
     sq_rows, ex_send, ex_recv, cols, masks, gathers,
     w_sem, in_sem, ts, tr, cs, cr, ags, agr, own_sem, x_sem, n_sem, keep_sem, o_sem, es, er,
 ):
@@ -197,12 +196,14 @@
             recv_sem=agr.at[kind, chunk, shard], device_id=(group, to), device_id_type=MESH,
         )
 
-    gather_to = ((1, 2), (0, 2, 3), (3, 1, 0), (2, 1))
-
-    def gather_direct(kind, packed, target, chunk, me):
+    far_to = ((2,), (), (), (1,))
+    near_to = ((1,), (0, 2, 3), (3, 1, 0), (2,))
+
+    def gather_direct(kind, packed, target, chunk, me, far):
+        first = 0 if far else len(far_to[me])
         return [
-            gather_push(kind, rows_of(packed, chunk), target, chunk, number, me, to)
-            for number, to in enumerate(gather_to[me])
+            gather_push(kind, rows_of(packed, chunk), target, chunk, first + number, me, to)
+            for number, to in enumerate(far_to[me] if far else near_to[me])
         ]
 
     def gather_forward(kind, target, chunk, me):
@@ -212,29 +213,42 @@
     def own_copy(kind, packed, target, chunk):
         return pltpu.make_async_copy(rows_of(packed, chunk), target.at[chunk, slot], own_sem.at[kind, chunk])
 
-    def gather_start(kind, packed, target, chunk):
+    def gather_far(kind, packed, target, chunk):
+        for me in (0, 3):
+            @pl.when(slot == me)
+            def _(me=me):
+                for copy in gather_direct(kind, packed, target, chunk, me, True):
+                    copy.start()
+
+    def gather_near(kind, packed, target, chunk):
         own_copy(kind, packed, target, chunk).start()
         for me in range(slots):
             @pl.when(slot == me)
             def _(me=me):
-                for copy in gather_direct(kind, packed, target, chunk, me):
+                for copy in gather_direct(kind, packed, target, chunk, me, False):
                     copy.start()
 
-    def gather_wait(kind, packed, target, chunk, hook=None):
+    def gather_arrived(kind, target, chunk, shard):
+        pltpu.make_async_remote_copy(
+            src_ref=target.at[chunk, shard], dst_ref=target.at[chunk, shard], send_sem=ags.at[kind, chunk, 0],
+            recv_sem=agr.at[kind, chunk, shard], device_id=(group, slot), device_id_type=MESH,
+        ).wait_recv()
+
+    def gather_pass(kind, target, chunk):
+        for me in (1, 2):
+            @pl.when(slot == me)
+            def _(me=me):
+                gather_arrived(kind, target, chunk, 3 if me == 1 else 0)
+                gather_forward(kind, target, chunk, me).start()
+
+    def gather_wait(kind, packed, target, chunk):
         for me in range(slots):
             @pl.when(slot == me)
             def _(me=me):
-                order = (3, 0, 2) if me == 1 else (0, 3, 1) if me == 2 else (1, 2, 3 - me)
-                for position, shard in enumerate(order):
-                    pltpu.make_async_remote_copy(
-                        src_ref=target.at[chunk, shard], dst_ref=target.at[chunk, shard],
-                        send_sem=ags.at[kind, chunk, 0], recv_sem=agr.at[kind, chunk, shard],
-                        device_id=(group, slot), device_id_type=MESH,
-                    ).wait_recv()
-                    if position == 0 and me in (1, 2):
-                        gather_forward(kind, target, chunk, me).start()
-                    if position == 0 and hook is not None:
-                        hook()
+                for shard in (1, 2) if me in (0, 3) else (0, 2) if me == 1 else (3, 1):
+                    gather_arrived(kind, target, chunk, shard)
+                if me in (0, 3):
+                    gather_arrived(kind, target, chunk, 3 - me)
         own_copy(kind, packed, target, chunk).wait()
 
     def gather_drain(kind, packed, target):
@@ -242,7 +256,9 @@
             for me in range(slots):
                 @pl.when(slot == me)
                 def _(me=me):
-                    for copy in gather_direct(kind, packed, target, chunk, me):
+                    for copy in gather_direct(kind, packed, target, chunk, me, True):
+                        copy.wait_send()
+                    for copy in gather_direct(kind, packed, target, chunk, me, False):
                         copy.wait_send()
                     if me in (1, 2):
                         gather_forward(kind, target, chunk, me).wait_send()
@@ -296,7 +312,9 @@
     for pair in range(pairs):
         gathers[pair] = (place == source + 2 * pair).astype(bf16)
     take_rows(ptok, arr_tok, ts, tr)
-    gather_start(0, ptok, fulltok, 0)
+    gather_far(0, ptok, fulltok, 0)
+    gather_near(0, ptok, fulltok, 0)
+    gather_far(0, ptok, fulltok, 1)
     cot_in.wait()
     send_rows(pcot, arr_cot, cs, cr)
     for which in range(5):
@@ -304,25 +322,34 @@
 
     def forward_chunk(chunk, nothing):
         start = chunk * Q
-        def second():
-            @pl.when(chunk == 0)
-            def _():
-                gather_start(0, ptok, fulltok, 1)
-
-        gather_wait(0, ptok, fulltok, chunk, second)
+        @pl.when(chunk == 0)
+        def _():
+            gather_pass(0, fulltok, 0)
+            gather_near(0, ptok, fulltok, 1)
+            gather_far(0, ptok, fulltok, 2)
+
+        gather_wait(0, ptok, fulltok, chunk)
         x_load(fulltok, chunk).start()
 
-        @pl.when(chunk + AHEAD < chunks)
+        @pl.when(chunk + 2 < chunks)
         def _():
-            gather_start(0, ptok, fulltok, chunk + AHEAD)
-
-        @pl.when(chunk + AHEAD == chunks)
+            gather_near(0, ptok, fulltok, chunk + 2)
+
+        @pl.when(chunk + 3 < chunks)
+        def _():
+            gather_far(0, ptok, fulltok, chunk + 3)
+
+        @pl.when(chunk + 3 == chunks)
         def _():
             take_rows(pcot, arr_cot, cs, cr)
 
-        @pl.when(chunk + AHEAD >= chunks)
+        @pl.when(chunk + 3 >= chunks)
         def _():
-            gather_start(1, pcot, fullcot, 2 * chunks - 1 - AHEAD - chunk)
+            gather_far(1, pcot, fullcot, 2 * chunks - 4 - chunk)
+
+        @pl.when(chunk + 2 >= chunks)
+        def _():
+            gather_near(1, pcot, fullcot, 2 * chunks - 3 - chunk)
 
         @pl.when(chunk > 0)
         def _():
@@ -366,6 +393,14 @@
         scores[...] = dot_nt(leave, entry, highest)
         entry_t = entry.T.astype(bf16)
         leave_low = leave.astype(bf16)
+        @pl.when(chunk + 1 < chunks)
+        def _():
+            gather_pass(0, fulltok, chunk + 1)
+
+        @pl.when(chunk + 1 == chunks)
+        def _():
+            gather_pass(1, fullcot, chunk)
+
         with_last, with_before, through = boundary(start, lengths_ref)
         to_last = with_last.astype(f32)
         from_before = with_before.astype(f32)
@@ -426,16 +461,17 @@
             recv_sem=er.at[chunk, slots - step], device_id=(group, lax.rem(slot + step, slots)), device_id_type=MESH,
         )
 
-    def backward_chunk(index, nothing):
-        chunk = chunks - 1 - index
-        start = chunk * Q
-        keep_load(chunk).start()
+    def products(chunk):
         gather_wait(1, pcot, fullcot, chunk)
         x_load(fullcot, chunk).start()
 
-        @pl.when(chunk >= AHEAD)
+        @pl.when(chunk >= 2)
         def _():
-            gather_start(1, pcot, fullcot, chunk - AHEAD)
+            gather_near(1, pcot, fullcot, chunk - 2)
+
+        @pl.when(chunk >= 3)
+        def _():
+            gather_far(1, pcot, fullcot, chunk - 3)
 
         x_load(fullcot, chunk).wait()
         for half in range(2):
@@ -444,21 +480,25 @@
             for shard in range(1, slots):
                 value = value + dot_nn(xbuf[shard].reshape(Q, width), wo[pl.ds(shard * width, width), columns])
             dsc[:, columns] = value
-        acc_dot[...] = jnp.zeros_like(acc_dot)
+        acc_prod[...] = jnp.zeros_like(acc_prod)
 
         def product(pair, nothing):
             columns = pl.ds(pl.multiple_of(pair * LANES, LANES), LANES)
             gate = gate_all[chunk, :, columns]
             gated = y_all[chunk, :, columns] * (gate * sigmoid(gate))
-            acc_dot[...] += dsc[:, columns] * ggain_ref[:, columns] * gated
+            acc_prod[...] += dsc[:, columns] * ggain_ref[:, columns] * gated
             return nothing
 
         lax.fori_loop(0, pairs, product, 0)
         ex_send[chunk, pl.ds(0, 8)] = sq_rows[chunk]
-        ex_send[chunk, pl.ds(8, 8)] = ones_rows(acc_dot[...])
+        ex_send[chunk, pl.ds(8, 8)] = ones_rows(acc_prod[...])
         for step in range(1, slots):
             send_sums(chunk, step).start()
 
+    def backward_chunk(index, nothing):
+        chunk = chunks - 1 - index
+        start = chunk * Q
+        keep_load(chunk).start()
         @pl.when(index > 0)
         def _():
             dvext[pl.ds(Q, 8)] = dvext[pl.ds(0, 8)]
@@ -483,6 +523,10 @@
         scores[...] = dot_nt(entry, leave, highest)
         entry_low = entry.astype(bf16)
         leave_t = leave.T.astype(bf16)
+        @pl.when(chunk > 0)
+        def _():
+            gather_pass(1, fullcot, chunk - 1)
+
         with_last, with_before, through = boundary(start, lengths_ref)
         to_last = with_last.astype(f32)
         from_before = with_before.astype(f32)
@@ -589,6 +633,11 @@
         for which in range(3):
             store(which, chunk).start()
 
+        @pl.when(chunk > 0)
+        def _():
+            products(chunk - 1)
+
+
         can_see = (neg_bias[...] == 0.0).astype(f32)
         d_log = dot_nn(can_see, acc_cum[...], highest)
         rate = jnp.exp(rate_ref[...])
@@ -633,6 +682,7 @@
         store(4, chunk).start()
         return nothing
 
+    products(chunks - 1)
     lax.fori_loop(0, chunks, backward_chunk, 0)
     for which in range(5):
         store(which, 0).wait()
@@ -698,6 +748,7 @@
             pltpu.VMEM((Q, Q), f32),
             pltpu.VMEM((Q, Q), f32),
             pltpu.VMEM((Q, Q), f32),
+            pltpu.VMEM((Q, LANES), f32),
             pltpu.VMEM((Q, LANES), f32),
             pltpu.VMEM((Q, LANES), f32),
             pltpu.VMEM((Q, LANES), f32),

time: 489 us -> 466 us (0.953)
  Pallas kernels: 444 us -> 421 us
    pallas_call x1, Pallas kernels: 260 us -> 239 us  [head(): pl.pallas_call(head_kernel, out_shape=[shape((chunks, slots, per_chunk, r...]
where the time goes in v4:
time: 466 us; the launch traced here: 464 us
  Pallas kernels  421 us (90%)
  local copies, waits for them, and re-layouts  27.5 us (6%)
  other arithmetic  14.7 us (3%)
    pallas_call x1, Pallas kernels, head(): pl.pallas_call(head_kernel, out_shape=[shape((chunks, slots, per_chunk, r...  239 us
    pallas_call x1, Pallas kernels, tail(): pl.pallas_call(tail_kernel, out_shape=[shape((runs, run, width), bf16), s...  182 us
    unnamed x18, local copies, waits for them, and re-layouts  11.4 us

profile of v4, /device:TPU:0, one launch (start us, length us, event | category | flops | bytes accessed | tf_op | source)
XLA Modules:
  0.0 464.3 jit_solution(16423324748771723615)
XLA Ops:
  0.7 0.8 reshape.109
  1.4 0.1 copy.41
  1.5 0.5 fusion.2
  2.1 0.2 dynamic-slice_reduce_fusion.arrive_from_ref
  2.3 0.5 copy-done.4
  2.8 0.6 select_reduce_fusion.1.back_run_ref
  3.4 0.7 select_reduce_fusion.return_from_ref
  4.1 1.1 copy.42
  5.3 0.9 pad.19.wt_hbm
  6.2 1.3 convert_element_type.21
  7.4 1.3 broadcast_in_dim.74
  8.7 1.3 convert_element_type.22.tapv_ref
  10.0 1.3 broadcast_in_dim.75
  11.3 1.3 convert_element_type.23.taps_ref
  12.6 1.2 broadcast_in_dim.76
  13.8 1.2 pad.20.stepb_ref
  15.0 1.2 pad.21.rate_ref
  16.1 0.7 broadcast_in_dim.72
  16.9 0.7 broadcast_in_dim_reshape.3.skip_ref
  17.5 239.3 %head.1 = (bf16[4,4,1,256,512]{4,3,2,1,0:T(8,128)(2,1)}, bf16[4,4,1,256,512]{4,3,2,1,0:T(8,128)(2,1)}, bf16[4,256,2048]{2,1,0:T(8,128)(2,1)}, bf16[4,256,1024]{2...) custom-call(s32[8]{0:T(128)} %get-tuple-element.110.send_run_ref, ...), custom_call_target="tpu_custom_call" | custom-call | tf_op jit(solution)/shard_map/head/pallas_call | solution.py:703
  256.8 1.3 dynamic_slice.8
  258.2 0.7 bitcast_reduce_fusion.2
  258.9 1.0 bitcast_reduce_fusion
  259.9 0.6 select_maximum_fusion.small_ref
  260.5 0.8 bitcast_reduce_fusion.1
  261.3 0.6 pad.23.small_z_ref
  261.9 182.1 %tail.1 = (bf16[4,256,512]{2,1,0:T(8,128)(2,1)}, bf16[4,256,512]{2,1,0:T(8,128)(2,1)}, f32[8,1280]{1,0:T(8,128)}, f32[8,512]{1,0:T(8,128)}, f32[256,1024]{1,0:T(...) custom-call(s32[8]{0:T(128)} %select_reduce_fusion.1.back_run_ref, ...), custom_call_target="tpu_custom_call" | custom-call | tf_op jit(solution)/shard_map/tail/pallas_call | solution.py:1253
  444.0 0.0 copy-start.2
  444.0 0.0 copy-start.1
  444.0 1.5 reduce_sum.78
  445.5 1.6 copy.43
  447.0 0.8 slice.35
  447.8 2.4 rev.6
  450.2 1.5 fusion.6
  451.7 0.7 slice.37
  452.4 0.6 rev.7
  453.0 1.3 slice.38
  454.3 1.2 slice_bitcast_fusion
  455.5 0.1 reshape_squeeze.3
  455.5 0.6 reduce_sum.79
  456.2 2.4 copy.50
  458.5 2.3 copy.51
  460.8 0.0 copy-done.2
  460.8 1.0 copy.52
  461.7 0.0 copy-done.1
  461.8 1.0 copy.53
  462.7 0.6 copy.54
  463.4 1.0 copy.55
  (7 shorter events, 0.0 us)
Async XLA Ops:
  2.3 0.5 copy-start.4
  444.0 16.8 %copy-start.2 = (f32[256,1024]{1,0:T(8,128)S(1)}, f32[256,1024]{1,0:T(8,128)}, u32[]{:S(2)}) copy-start(f32[256,1024]{1,0:T(8,128)} %get-tuple-element.137) | copy-start | bytes 3145732
  444.0 17.8 %copy-start.1 = (f32[256,1024]{1,0:T(8,128)S(1)}, f32[256,1024]{1,0:T(8,128)}, u32[]{:S(2)}) copy-start(f32[256,1024]{1,0:T(8,128)} %get-tuple-element.138) | copy-start | bytes 3145732
  456.2 6.6 %copy-start.3 = (f32[64,256]{1,0:T(8,128)S(1)}, f32[64,256]{1,0:T(8,128)}, u32[]{:S(2)}) copy-start(f32[64,256]{1,0:T(8,128)} %get-tuple-element.139) | copy-start | bytes 196612
  456.2 7.2 %copy-start = (f32[256,1024]{1,0:T(8,128)S(1)}, f32[256,1024]{1,0:T(8,128)}, u32[]{:S(2)}) copy-start(f32[256,1024]{1,0:T(8,128)} %get-tuple-element.149) | copy-start | bytes 3145732

commit v5 on v4

--- a/solution.py
+++ b/solution.py
@@ -122,7 +122,7 @@
 
 def head_kernel(
     send_run_ref, arrive_from_ref, lengths_ref, tokens, cotangent, wg_hbm, wv_hbm, ws_hbm, wt_hbm, wo_hbm,
-    gain_ref, ggain_ref, tapv_ref, biasv_ref, taps_ref, biass_ref, stepb_ref, rate_ref, skip_ref,
+    tapv_ref, taps_ref, heads_ref, small_ref,
     fulltok, fullcot, normed_out, dgate_out, dvalue_out, scaled_out, back_out, keep, out_part,
     dsmall_ref, inv_ref, dot_ref, sumv_ref, sums_ref, sumh_ref,
     wg, wv, ws, wt, wo, ptok, pcot, slots_buf, arr_tok, arr_cot, xbuf, nbuf, kbuf, gate_all, y_all,
@@ -137,6 +137,8 @@
     chunks = runs * run // Q
     per_chunk = Q // run
     pairs = d_carry.shape[0]
+    gain_ref, ggain_ref, biasv_ref, biass_ref, skip_ref = (small_ref.at[row] for row in range(5))
+    stepb_ref, rate_ref = heads_ref.at[0], heads_ref.at[1]
     last = slots - 1
     model = width * slots
     inner_total = wg.shape[1] * slots
@@ -619,11 +621,11 @@
             sumv_ref[pl.ds(16, 8), columns] += fold_rows(d_pre)
             vraw = kbuf[0, :, columns]
             total = tapv_ref[3:4, columns] * d_pre
-            sumv_ref[pl.ds(24, 8), columns] += fold_rows(vraw * d_pre)
+            sumv_ref[pl.ds(48, 8), columns] += fold_rows(vraw * d_pre)
             for shift in range(1, 4):
                 moved_back = dvext[pl.ds(shift, Q), columns] * masks[shift - 1]
                 total = total + tapv_ref[3 - shift : 4 - shift, columns] * moved_back
-                sumv_ref[pl.ds(24 + 8 * shift, 8), columns] += fold_rows(vraw * moved_back)
+                sumv_ref[pl.ds(48 - 8 * shift, 8), columns] += fold_rows(vraw * moved_back)
             d_value = total.astype(bf16)
             dvbuf[:, columns] = d_value
             acc_dot[...] += d_value.astype(f32) * vraw
@@ -660,11 +662,11 @@
             sums_ref[pl.ds(0, 8), columns] += fold_rows(d_pre)
             sraw = sraw_all[chunk, :, columns]
             total = taps_ref[3:4, columns] * d_pre
-            sums_ref[pl.ds(8, 8), columns] += fold_rows(sraw * d_pre)
+            sums_ref[pl.ds(32, 8), columns] += fold_rows(sraw * d_pre)
             for shift in range(1, 4):
                 moved_back = dsext[pl.ds(shift, Q), columns] * masks[shift - 1]
                 total = total + taps_ref[3 - shift : 4 - shift, columns] * moved_back
-                sums_ref[pl.ds(8 + 8 * shift, 8), columns] += fold_rows(sraw * moved_back)
+                sums_ref[pl.ds(32 - 8 * shift, 8), columns] += fold_rows(sraw * moved_back)
             d_state_raw = total.astype(bf16)
             dsmall_ref[pl.ds(start, Q), columns] = d_state_raw
             acc_dot[...] += d_state_raw.astype(f32) * sraw
@@ -779,7 +781,7 @@
     back_run_ref, return_from_ref, out_part, back_part, normed, tokens, cotangent, scaled, d_gate, d_value,
     row_dot_ref, inv_ref, gain_ref, small_ref, small_z_ref, dsmall_ref,
     layer_ref, tgrad_ref, small_out, ngain_out, share0, share1, share2, state_out, step_out,
-    z_recv, z_comb, z_own, z_mix, ptok, pcot, rd_recv, rd_col, row_buf, slots_buf, arrive, left, right, full,
+    z_recv, z_comb, z_own, z_mix, ptok, pcot, rd_recv, rd_col, row_buf, slots_buf, arrive_out, arrive_grad, left, right, full,
     core_recv, chip_recv, total, sz_recv, small_all, small_recv, ngain_all, ngain_recv,
     thin, thin_core, thin_chip, thin_own, thin_z,
     load_sem, mix_sem, left_sem, right_sem, zs, zr, zc, rds, rdr, szs, szr, sms, smr, ngs, ngr, rs, rr, cs, cr, hs, hr, tcs, ths, thr, tzs, tzr,
@@ -1059,10 +1061,12 @@
 
         lax.fori_loop(1, groups, drain, 0)
 
+    arrives = (arrive_out, arrive_grad)
+
     def row_send(job, step):
         other = lax.rem(group + step, groups)
         return pltpu.make_async_remote_copy(
-            src_ref=slots_buf.at[job % pieces, other], dst_ref=arrive.at[job, group], send_sem=rs.at[job, other],
+            src_ref=slots_buf.at[job % pieces, other], dst_ref=arrives[job // pieces].at[job % pieces, group], send_sem=rs.at[job, other],
             recv_sem=rr.at[job, group], device_id=(other, slot), device_id_type=MESH,
         )
 
@@ -1109,14 +1113,15 @@
         if kind == 1:
             rows_drain(job - pieces)
         lax.fori_loop(1, groups, fill, 0)
-        arrive[job, group] = row_buf[back_run_ref[group]]
+        arrives[kind][piece, group] = row_buf[back_run_ref[group]]
 
     def rows_wait(kind):
         for job in range(kind * pieces, (kind + 1) * pieces):
             def one(step, nothing, job=job):
                 source = lax.rem(group + groups - step, groups)
                 pltpu.make_async_remote_copy(
-                    src_ref=arrive.at[job, source], dst_ref=arrive.at[job, source], send_sem=rs.at[job, source],
+                    src_ref=arrives[kind].at[job % pieces, source], dst_ref=arrives[kind].at[job % pieces, source],
+                    send_sem=rs.at[job, source],
                     recv_sem=rr.at[job, source], device_id=(group, slot), device_id_type=MESH,
                 ).wait_recv()
                 return nothing
@@ -1126,7 +1131,7 @@
     def rows_take(kind, target):
         for piece in range(pieces):
             for index in range(runs):
-                target[index, pl.ds(piece * piece_run, piece_run)] = arrive[kind * pieces + piece, return_from_ref[index]]
+                target[index, pl.ds(piece * piece_run, piece_run)] = arrives[kind][piece, return_from_ref[index]]
 
     def let_in(job):
         if job < jobs:
@@ -1202,23 +1207,30 @@
     core_send(2).start()
     for job in range(2, WINDOW):
         let_in(job)
+    def out_rows():
+        rows_wait(0)
+        rows_take(0, layer_ref)
+
+    meanwhile = [
+        thin_total,
+        lambda: [chip_total(which) for which in range(3)],
+        lambda: dp_small_finish(small_all, small_recv, sms, smr, small_out),
+    ]
     for job in range(jobs):
         if job == 1:
             chip_pushes(2)
+        if job == jobs - 1:
+            out_rows()
         step_of(job)
-        if job == jobs // 2:
-            thin_total()
+        if job >= jobs // 2 and meanwhile:
+            meanwhile.pop(0)()
     dp_small_start(ngain_all, ngain_recv, ngs, ngr)
-
-    rows_wait(0)
+    for action in meanwhile:
+        action()
     rows_wait(1)
     for job in range(pieces, jobs):
         rows_drain(job)
-    rows_take(0, layer_ref)
     rows_take(1, tgrad_ref)
-    dp_small_finish(small_all, small_recv, sms, smr, small_out)
-    for which in range(3):
-        chip_total(which)
     thin_finish()
     chip_drain(1)
     chip_drain(2)
@@ -1269,7 +1281,8 @@
             pltpu.VMEM((runs, run, LANES), f32),
             pltpu.VMEM(part, bf16),
             pltpu.VMEM((pieces, groups, piece_run, width), bf16),
-            pltpu.VMEM((jobs, groups, piece_run, width), bf16),
+            pltpu.VMEM((pieces, groups, piece_run, width), bf16),
+            pltpu.VMEM((pieces, groups, piece_run, width), bf16),
             pltpu.VMEM((2,) + by_chunk[:-1] + (256,), bf16),
             pltpu.VMEM((2, rows, inner), bf16),
             pltpu.VMEM((2, groups, grow, inner), bf16),
@@ -1337,10 +1350,15 @@
         return values.reshape(runs, run, values.shape[1])
 
     gain_full = norm_gain.astype(f32)
+    def row(values):
+        return jnp.pad(values.astype(f32), (0, model - values.shape[0]))
+
+    rows_of = (norm_gain, gate_gain, conv_value_bias, conv_state_bias, jnp.repeat(skip_gain, HEAD_DIM))
     small = (
-        gain_full[None], gate_gain.astype(f32)[None], conv_value.astype(f32), conv_value_bias.astype(f32)[None],
-        conv_state.astype(f32), conv_state_bias.astype(f32)[None], pad_heads(step_bias[None]),
-        pad_heads(decay_log[None]), jnp.repeat(skip_gain, HEAD_DIM)[None],
+        conv_value.astype(f32),
+        conv_state.astype(f32),
+        pad_heads(jnp.stack([step_bias, decay_log])).reshape(2, 1, LANES),
+        jnp.stack([row(v) for v in rows_of]).reshape(len(rows_of), 1, model),
     )
     (full_tokens, full_cotangent, normed, d_gate, d_value, scaled, back_partial, _, out_partial, d_small,
      inv_rms, row_dot, sumv, sums, sumh) = head(
@@ -1369,9 +1387,9 @@
         value_share,
         state_share,
         step_share[:, :heads],
-        small[6:2:-1, :inner],
+        small[3:7, :inner],
         small[2, :inner],
-        state_sums[4:0:-1],
+        state_sums[1:5],
         state_sums[0],
         small[7, :heads],
         small[7, LANES : LANES + heads],

time: 466 us -> 461 us (0.989)
  no operation moved by 1% of the time
where the time goes in v5:
time: 461 us; the launch traced here: 459 us
  Pallas kernels  422 us (92%)
  local copies, waits for them, and re-layouts  23.5 us (5%)
  other arithmetic  13.6 us (3%)
    pallas_call x1, Pallas kernels, head(): pl.pallas_call(head_kernel, out_shape=[shape((chunks, slots, per_chunk, r...  240 us
    pallas_call x1, Pallas kernels, tail(): pl.pallas_call(tail_kernel, out_shape=[shape((runs, run, width), bf16), s...  182 us
    unnamed x18, local copies, waits for them, and re-layouts  11.4 us

profile of v5, /device:TPU:0, one launch (start us, length us, event | category | flops | bytes accessed | tf_op | source)
XLA Modules:
  0.0 459.4 jit_solution(12194489722017491508)
XLA Ops:
  0.7 0.8 reshape.118
  1.4 0.1 copy.41
  1.5 0.5 fusion.2
  2.1 0.2 dynamic-slice_reduce_fusion.arrive_from_ref
  2.3 0.5 copy-done.4
  2.8 0.6 select_reduce_fusion.1.back_run_ref
  3.4 0.7 select_reduce_fusion.return_from_ref
  4.1 1.1 copy.42
  5.3 0.9 pad.33.wt_hbm
  6.2 1.3 convert_element_type.27.tapv_ref
  7.5 1.3 convert_element_type.28.taps_ref
  8.7 1.2 select_maximum_fusion.1
  10.0 0.7 convert_element_type.29
  10.7 0.7 pad_convert_fusion.2
  11.3 0.7 pad_convert_fusion.1
  12.0 0.7 pad_convert_fusion
  12.7 0.7 broadcast_in_dim.39
  13.4 0.1 reshape.122
  13.5 0.1 stack.47
  13.6 0.6 reshape.123.small_ref
  14.2 239.7 %head.1 = (bf16[4,4,1,256,512]{4,3,2,1,0:T(8,128)(2,1)}, bf16[4,4,1,256,512]{4,3,2,1,0:T(8,128)(2,1)}, bf16[4,256,2048]{2,1,0:T(8,128)(2,1)}, bf16[4,256,1024]{2...) custom-call(s32[8]{0:T(128)} %get-tuple-element.110.send_run_ref, ...), custom_call_target="tpu_custom_call" | custom-call | tf_op jit(solution)/shard_map/head/pallas_call | solution.py:705
  253.9 1.3 dynamic_slice.8
  255.2 0.7 bitcast_reduce_fusion.2
  255.9 1.0 bitcast_reduce_fusion
  256.9 0.6 select_maximum_fusion.small_ref
  257.6 0.8 bitcast_reduce_fusion.1
  258.4 0.6 pad.40.small_z_ref
  259.0 181.9 %tail.1 = (bf16[4,256,512]{2,1,0:T(8,128)(2,1)}, bf16[4,256,512]{2,1,0:T(8,128)(2,1)}, f32[8,1280]{1,0:T(8,128)}, f32[8,512]{1,0:T(8,128)}, f32[256,1024]{1,0:T(...) custom-call(s32[8]{0:T(128)} %select_reduce_fusion.1.back_run_ref, ...), custom_call_target="tpu_custom_call" | custom-call | tf_op jit(solution)/shard_map/tail/pallas_call | solution.py:1265
  440.9 0.0 copy-start.2
  440.9 0.0 copy-start.1
  440.9 1.5 reduce_sum.78
  442.4 1.6 copy.43
  443.9 1.4 slice.35
  445.3 1.5 fusion.6
  446.8 1.3 slice.37
  448.1 1.3 slice.38
  449.3 1.2 slice_bitcast_fusion
  450.5 0.1 reshape_squeeze.3
  450.6 0.6 reduce_sum.79
  451.2 2.4 copy.50
  453.6 2.3 copy.51
  455.9 0.0 copy-done.2
  455.9 1.0 copy.52
  456.8 0.0 copy-done.1
  456.8 1.0 copy.53
  457.8 0.6 copy.54
  458.4 0.0 copy-done
  458.4 1.0 copy.55
  (7 shorter events, 0.0 us)
Async XLA Ops:
  2.3 0.5 copy-start.4
  440.9 15.0 %copy-start.2 = (f32[256,1024]{1,0:T(8,128)S(1)}, f32[256,1024]{1,0:T(8,128)}, u32[]{:S(2)}) copy-start(f32[256,1024]{1,0:T(8,128)} %get-tuple-element.137) | copy-start | bytes 3145732
  440.9 15.9 %copy-start.1 = (f32[256,1024]{1,0:T(8,128)S(1)}, f32[256,1024]{1,0:T(8,128)}, u32[]{:S(2)}) copy-start(f32[256,1024]{1,0:T(8,128)} %get-tuple-element.138) | copy-start | bytes 3145732
  451.2 6.6 %copy-start.3 = (f32[64,256]{1,0:T(8,128)S(1)}, f32[64,256]{1,0:T(8,128)}, u32[]{:S(2)}) copy-start(f32[64,256]{1,0:T(8,128)} %get-tuple-element.139) | copy-start | bytes 196612
  451.2 7.2 %copy-start = (f32[256,1024]{1,0:T(8,128)S(1)}, f32[256,1024]{1,0:T(8,128)}, u32[]{:S(2)}) copy-start(f32[256,1024]{1,0:T(8,128)} %get-tuple-element.149) | copy-start | bytes 3145732

commit v6 on v5

--- a/solution.py
+++ b/solution.py
@@ -10,8 +10,8 @@
 Q = 256
 LANES = 128
 HEAD_DIM = 64
-WINDOW = 2
-EARLY = 5
+WINDOW = 3
+EARLY = 6
 HEAD_VMEM = 64 << 20
 highest = lax.Precision.HIGHEST
 epsilon = 1e-05
@@ -1146,6 +1146,8 @@
 
     for job in range(min(EARLY, jobs)):
         push(job, True)
+    for job in range(2):
+        push(job, False)
     own_load(0).start()
     own_load(1).start()
     shard_load(0).start()
@@ -1178,7 +1180,7 @@
         own_load(kind).wait()
         shard_load(kind).wait()
     left_load(1, 0, 0).start()
-    push(0, False)
+    combine(0)
     right_load(1).wait()
     grad_blocks(1, 0, half)
     chip_pushes(0)
@@ -1196,16 +1198,16 @@
         piece_row = jnp.broadcast_to(rd_total[0:1, block * 256 : (block + 1) * 256], (LANES, 256))
         count = 256 // run
         rd_col[pl.ds(block * count, count)] = piece_row.T.reshape(count, run, LANES)
-    combine(0)
+    combine(1)
+    let_in(2)
     right_load(2).wait()
     chip_drain(0)
-    let_in(1)
     grad_blocks(2, 0, half)
     chip_pushes(1)
     thin_pushes()
     grad_blocks(2, half, blocks)
     core_send(2).start()
-    for job in range(2, WINDOW):
+    for job in range(3, WINDOW):
         let_in(job)
     def out_rows():
         rows_wait(0)

time: 461 us -> 444 us (0.963)
  Pallas kernels: 422 us -> 404 us
    pallas_call x1, Pallas kernels: 182 us -> 165 us  [tail(): pl.pallas_call(tail_kernel, out_shape=[shape((runs, run, width), bf16), s...]
where the time goes in v6:
time: 444 us; the launch traced here: 442 us
  Pallas kernels  404 us (91%)
  local copies, waits for them, and re-layouts  23.5 us (5%)
  other arithmetic  13.6 us (3%)
    pallas_call x1, Pallas kernels, head(): pl.pallas_call(head_kernel, out_shape=[shape((chunks, slots, per_chunk, r...  240 us
    pallas_call x1, Pallas kernels, tail(): pl.pallas_call(tail_kernel, out_shape=[shape((runs, run, width), bf16), s...  165 us
    unnamed x18, local copies, waits for them, and re-layouts  11.4 us

profile of v6, /device:TPU:0, one launch (start us, length us, event | category | flops | bytes accessed | tf_op | source)
XLA Modules:
  0.0 442.2 jit_solution(10934518124565644125)
XLA Ops:
  0.7 0.8 reshape.118
  1.4 0.1 copy.41
  1.5 0.5 fusion.2
  2.1 0.2 dynamic-slice_reduce_fusion.arrive_from_ref
  2.3 0.5 copy-done.4
  2.8 0.6 select_reduce_fusion.1.back_run_ref
  3.4 0.7 select_reduce_fusion.return_from_ref
  4.1 1.1 copy.42
  5.3 0.9 pad.33.wt_hbm
  6.2 1.3 convert_element_type.27.tapv_ref
  7.5 1.3 convert_element_type.28.taps_ref
  8.7 1.2 select_maximum_fusion.1
  10.0 0.7 convert_element_type.29
  10.7 0.7 pad_convert_fusion.2
  11.3 0.7 pad_convert_fusion.1
  12.0 0.7 pad_convert_fusion
  12.7 0.7 broadcast_in_dim.39
  13.4 0.1 reshape.122
  13.5 0.1 stack.47
  13.6 0.6 reshape.123.small_ref
  14.2 239.7 %head.1 = (bf16[4,4,1,256,512]{4,3,2,1,0:T(8,128)(2,1)}, bf16[4,4,1,256,512]{4,3,2,1,0:T(8,128)(2,1)}, bf16[4,256,2048]{2,1,0:T(8,128)(2,1)}, bf16[4,256,1024]{2...) custom-call(s32[8]{0:T(128)} %get-tuple-element.110.send_run_ref, ...), custom_call_target="tpu_custom_call" | custom-call | tf_op jit(solution)/shard_map/head/pallas_call | solution.py:705
  253.9 1.3 dynamic_slice.8
  255.2 0.7 bitcast_reduce_fusion.2
  255.9 1.0 bitcast_reduce_fusion
  256.9 0.6 select_maximum_fusion.small_ref
  257.6 0.8 bitcast_reduce_fusion.1
  258.4 0.6 pad.40.small_z_ref
  259.0 164.7 %tail.1 = (bf16[4,256,512]{2,1,0:T(8,128)(2,1)}, bf16[4,256,512]{2,1,0:T(8,128)(2,1)}, f32[8,1280]{1,0:T(8,128)}, f32[8,512]{1,0:T(8,128)}, f32[256,1024]{1,0:T(...) custom-call(s32[8]{0:T(128)} %select_reduce_fusion.1.back_run_ref, ...), custom_call_target="tpu_custom_call" | custom-call | tf_op jit(solution)/shard_map/tail/pallas_call | solution.py:1267
  423.7 0.0 copy-start.2
  423.7 0.0 copy-start.1
  423.7 1.5 reduce_sum.78
  425.2 1.6 copy.43
  426.7 1.4 slice.35
  428.1 1.5 fusion.6
  429.6 1.3 slice.37
  430.9 1.3 slice.38
  432.1 1.2 slice_bitcast_fusion
  433.3 0.1 reshape_squeeze.3
  433.4 0.6 reduce_sum.79
  434.0 2.4 copy.50
  436.4 2.3 copy.51
  438.7 0.0 copy-done.2
  438.7 1.0 copy.52
  439.6 0.0 copy-done.1
  439.6 1.0 copy.53
  440.6 0.0 copy-done.3
  440.6 0.6 copy.54
  441.2 1.0 copy.55
  (7 shorter events, 0.0 us)
Async XLA Ops:
  2.3 0.5 copy-start.4
  423.7 15.0 %copy-start.2 = (f32[256,1024]{1,0:T(8,128)S(1)}, f32[256,1024]{1,0:T(8,128)}, u32[]{:S(2)}) copy-start(f32[256,1024]{1,0:T(8,128)} %get-tuple-element.137) | copy-start | bytes 3145732
  423.7 15.9 %copy-start.1 = (f32[256,1024]{1,0:T(8,128)S(1)}, f32[256,1024]{1,0:T(8,128)}, u32[]{:S(2)}) copy-start(f32[256,1024]{1,0:T(8,128)} %get-tuple-element.138) | copy-start | bytes 3145732
  434.0 6.6 %copy-start.3 = (f32[64,256]{1,0:T(8,128)S(1)}, f32[64,256]{1,0:T(8,128)}, u32[]{:S(2)}) copy-start(f32[64,256]{1,0:T(8,128)} %get-tuple-element.139) | copy-start | bytes 196612
  434.0 7.2 %copy-start = (f32[256,1024]{1,0:T(8,128)S(1)}, f32[256,1024]{1,0:T(8,128)}, u32[]{:S(2)}) copy-start(f32[256,1024]{1,0:T(8,128)} %get-tuple-element.149) | copy-start | bytes 3145732
